TPU v7x, 512 devices: a whole 4x8x8 slice. The times are simulated.
512 devices in a mesh: ens: 8 (over x, y_hi), dom: 64 (over z, y_lo, core).
Axes of the slice: x: 4, y: 8 (y_hi: 2, y_lo: 4; y = y_hi * 4 + y_lo), z: 8, core: 2. Of those that a mesh axis runs over, the one named last changes fastest.
Arguments:
- features: bfloat16 [8, 256, 128, 256], P('ens', None, 'dom'), may hold values from -6 to 6
- w_first: bfloat16 [256, 2304], replicated, may hold values from -0.125 to 0.125
- later_kernel_matrix: bfloat16 [100, 2304], replicated, may hold values from -0.125 to 0.125
- observed_state: float32 [100, 128, 256], P(None, 'dom'), may hold values from -6 to 6
- land: int32 [128, 256], P('dom'), may hold values 0 or 1
Outputs:
- ensemble_outlook: float32 [8, 100, 128, 256], P('ens', None, 'dom')
- grad_first: bfloat16 [256, 2304], replicated
- grad_second: bfloat16 [100, 2304], replicated
- loss: float32 [], replicated
All inputs are finite; a program needn't handle non-finite values. No bound on the sum of `land` on one device may be relied on, other than what follows from the above.
Results may differ from a plain program's by a relative error of at most 0.008.
Values may be sent and summed in bfloat16 or wider, within the bound.
No kernel may reach another device: no remote copies, remote signals or barrier semaphores. Data moves between devices by JAX's collectives and lax.ppermute only.
A program may use at most 64 MiB of HBM per device.

v0:
```python
import jax
import jax.numpy as jnp
from jax import lax
from jax.sharding import PartitionSpec as P

SOFTNESS = 0.25
LAND_WEIGHT = 2.0
LOSS_SCALE = 65536.0


def padded_2(array, sides, width):
    for axis, dim in sides:
        size, length = (lax.axis_size(axis), array.shape[dim])
        up = [(i, (i + 1) % size) for i in range(size - 1)]
        down = [(j, i) for i, j in up]
        last = lax.slice_in_dim(array, length - width, length, axis=dim)
        leading = lax.slice_in_dim(array, 0, width, axis=dim)
        before = lax.ppermute(last, axis, up)
        after = lax.ppermute(leading, axis, down)
        array = jnp.concatenate([before, array, after], axis=dim)
    return array


def activate(values):
    return jax.nn.gelu(values, approximate=True)


def columns(padded, row_count):
    pieces = []
    for row_off in range(3):
        stripe = padded[:, row_off : row_off + row_count, :]
        for lon_off in range(3):
            pieces.append(jnp.roll(stripe, 1 - lon_off, axis=2))
    stacked = jnp.concatenate(pieces, axis=0)
    return stacked.reshape(stacked.shape[0], row_count * padded.shape[2])


def back_columns(padded, row_count):
    pieces = []
    for row_off in range(3):
        stripe = padded[:, 2 - row_off : 2 - row_off + row_count, :]
        for lon_off in range(3):
            pieces.append(jnp.roll(stripe, lon_off - 1, axis=2))
    stacked = jnp.concatenate(pieces, axis=0)
    return stacked.reshape(stacked.shape[0], row_count * padded.shape[2])


def soft_abs(diff):
    return jnp.sqrt(diff * diff + SOFTNESS * SOFTNESS)


def misfits_per_member(chosen, emitted_quantities, observed_state, area_factor, mesh_points):
    members = emitted_quantities.shape[0]
    skill = (chosen - observed_state[None]) / soft_abs(chosen - observed_state[None]) / members
    spread = jnp.zeros_like(chosen)
    for other in range(members):
        diff = chosen - emitted_quantities[other][None]
        spread = spread + diff / soft_abs(diff)
    return (
        LOSS_SCALE
        / mesh_points
        * area_factor[None, None]
        * (skill - spread / (members * (members - 1)))
    )


def probabilistic_skill_total(emitted_quantities, observed_state, area_factor):
    members = emitted_quantities.shape[0]
    skill = jnp.sum(soft_abs(emitted_quantities - observed_state[None]), axis=0) / members
    pairs = jnp.zeros_like(skill)
    for first in range(members):
        for second in range(first + 1, members):
            pairs = pairs + soft_abs(emitted_quantities[first] - emitted_quantities[second])
    return jnp.sum(area_factor[None] * (skill - pairs / (members * (members - 1))))


def body(features, w_first, later_kernel_matrix, observed_state, land):
    local = features[0]
    channels, row_count, lon_count = local.shape
    variables = observed_state.shape[0]
    members = lax.axis_size("ens")
    lat_total = row_count * lax.axis_size("dom")
    padded = padded_2(local, (("dom", 1),), 1)
    cols_first = columns(padded, row_count)
    before = jnp.dot(w_first, cols_first, preferred_element_type=jnp.float32)
    hidden = activate(before).astype(jnp.bfloat16).reshape(channels, row_count, lon_count)
    hidden_pad = padded_2(hidden, (("dom", 1),), 1)
    second_columns = columns(hidden_pad, row_count)
    ensemble_outlook = jnp.dot(
        later_kernel_matrix, second_columns, preferred_element_type=jnp.float32
    ).reshape(variables, row_count, lon_count)
    area_factor = 1.0 + LAND_WEIGHT * land.astype(jnp.float32)
    mesh_points = float(variables * lat_total * lon_count)
    emitted_quantities = lax.all_gather(ensemble_outlook[None], "ens", axis=0, tiled=True)
    member_misfits = misfits_per_member(
        ensemble_outlook[None], emitted_quantities, observed_state, area_factor, mesh_points
    )[0].astype(jnp.bfloat16)
    partial_loss = (
        probabilistic_skill_total(emitted_quantities, observed_state, area_factor) / members
    )
    err_pad = padded_2(member_misfits, (("dom", 1),), 1)
    w_back = (
        later_kernel_matrix.reshape(variables, 9, channels)
        .transpose(2, 1, 0)
        .reshape(channels, 9 * variables)
    )
    back = jnp.dot(w_back, back_columns(err_pad, row_count), preferred_element_type=jnp.float32)
    unused_out, pull = jax.vjp(activate, before)
    pre_grad = pull(back)[0].astype(jnp.bfloat16)
    dims = (((1,), (1,)), ((), ()))
    err_flat = member_misfits.reshape(variables, row_count * lon_count)
    grad_two = lax.dot_general(err_flat, second_columns, dims, preferred_element_type=jnp.float32)
    grad_one = lax.dot_general(pre_grad, cols_first, dims, preferred_element_type=jnp.float32)
    aggregate_first, total_two, total_loss = lax.psum(
        (grad_one, grad_two, partial_loss), ("ens", "dom")
    )
    return (
        ensemble_outlook[None],
        aggregate_first.astype(jnp.bfloat16),
        total_two.astype(jnp.bfloat16),
        total_loss / mesh_points,
    )


def solution(mesh):
    placed = (P("ens", None, "dom", None), P(), P(), P(None, "dom", None), P("dom", None))
    return jax.shard_map(
        body,
        mesh=mesh,
        in_specs=placed,
        out_specs=(P("ens", None, "dom", None), P(), P(), P()),
        check_vma=False,
    )
```

profile of v0, /device:TPU:1, one launch (start us, length us, event | category | flops | bytes accessed | tf_op | source)
XLA Modules:
  0.0 295.7 jit_solution(11990545265115029706)
XLA Ops:
  7.2 1.6 fusion.70
  8.8 4.6 %collective-permute-start = (bf16[256,1,256]{2,1,0:T(2,128)(2,1)S(1)}, bf16[256,1,256]{2,1,0:T(2,128)(2,1)S(1)}, u32[]{:S(2)}, u32[]{:S(2)}) collective-permute-start(bf16[256,1,256]{2,1,0:T(2,128)(2,1)S(1)} %get-tuple-element.56), channel_id=1, source_target_pairs={{0,1},{1,2},{2,3},{3,4},{4,5},{5,6},{6,7},{7,8},{8,9},{9,10},{10,1... | collective-permute-start | bytes 393224 | tf_op jit(solution)/shard_map/ppermute | solution.py:18
  13.5 5.5 %collective-permute-start.1 = (bf16[256,1,256]{2,1,0:T(2,128)(2,1)S(1)}, bf16[256,1,256]{2,1,0:T(2,128)(2,1)S(1)}, u32[]{:S(2)}, u32[]{:S(2)}) collective-permute-start(bf16[256,1,256]{2,1,0:T(2,128)(2,1)S(1)} %get-tuple-element.55), channel_id=1, source_target_pairs={{1,0},{2,1},{3,2},{4,3},{5,4},{6,5},{7,6},{8,7},{9,8},{10,9},{11,1... | collective-permute-start | bytes 393224 | tf_op jit(solution)/shard_map/ppermute | solution.py:19
  19.0 1.0 copy.71
  20.0 3.8 %collective-permute-done.1 = bf16[256,1,256]{2,1,0:T(2,128)(2,1)S(1)} collective-permute-done((bf16[256,1,256]{2,1,0:T(2,128)(2,1)S(1)}, bf16[256,1,256]{2,1,0:T(2,128)(2,1)S(1)}, u32[]{:S(2)}, u32[]{:S(2)}) %collective-permute-start.1) | collective-permute-done | bytes 131104 | tf_op jit(solution)/shard_map/ppermute | solution.py:19
  23.8 5.6 %fusion.17 = (bf16[256,2,255]{2,1,0:T(2,128)(2,1)S(1)}, bf16[256,2,255]{2,1,0:T(2,128)(2,1)S(1)}, bf16[256,2,255]{2,1,0:T(2,128)(2,1)S(1)}, bf16[256,2,255]{2,1,...) fusion(bf16[256,2,256]{2,1,0:T(2,128)(2,1)} %bitcast.167, ...), kind=kLoop, calls=%fused_computation.56 | loop fusion | flops 2088960 | bytes 2615296 | tf_op jit(solution)/shard_map/concatenate | solution.py:20
  29.4 1.1 fusion.39
  30.5 1.1 pad_maximum_fusion.4
  31.7 3.0 %fusion.25 = (bf16[256,2,256]{2,1,0:T(2,128)(2,1)S(1)}, bf16[256,2,256]{2,1,0:T(2,128)(2,1)S(1)}, bf16[256,2,256]{2,1,0:T(2,128)(2,1)S(1)}, bf16[256,2,256]{2,1,0:T(2,128)(2,1)S(1)}) fusion(bf16[256,1,256]{2,1,0:T(2,128)(2,1)S(1)} %collective-permute-done.1, bf16[256,2,256]{2,1,0:T(2,128)(2,1)S(1)} %bitcast.169, ...), kind=kLoop, calls=%fused_computation.67 | loop fusion | flops 2621440 | bytes 2095104 | tf_op jit(solution)/shard_map/jit(_roll_static)/concatenate | solution.py:33
  34.8 1.0 pad_maximum_fusion.6
  36.2 1.7 multiply_convert_fusion
  38.0 1.9 collective-permute-start.2
  40.0 2.6 collective-permute-start.3
  42.6 5.0 %collective-permute-done.3 = bf16[256,1,256]{2,0,1:T(8,128)(2,1)S(1)} collective-permute-done((bf16[256,1,256]{2,0,1:T(8,128)(2,1)S(1)}, bf16[256,1,256]{2,0,1:T(8,128)(2,1)S(1)}, u32[]{:S(2)}, u32[]{:S(2)}) %collective-permute-start.3) | collective-permute-done | bytes 131104 | tf_op jit(solution)/shard_map/ppermute | solution.py:19
  47.7 0.3 fusion.11
  48.2 0.8 constant_dynamic-update-slice_fusion.25
  49.7 1.4 copy-done.3
  51.7 0.8 copy.54
  52.5 1.8 copy.51
  54.4 0.8 copy.50
  55.4 1.0 constant_dynamic-update-slice_fusion.16
  56.4 1.0 constant_dynamic-update-slice_fusion.15
  57.4 1.0 constant_dynamic-update-slice_fusion.14
  58.5 0.8 convolution_bitcast_fusion.3
  59.3 0.8 broadcast_in_dim_reshape.7
  60.2 0.3 copy.63
  60.5 0.3 copy.64
  60.8 0.8 reshape.200
  61.8 77.8 %all-gather.2.cloned.1.call-done = f32[8,100,2,256]{3,2,1,0:T(2,128)} async-done(((f32[1,100,2,256]{3,2,1,0:T(2,128)}), f32[8,100,2,256]{3,2,1,0:T(2,128)}) %all-gather.2.cloned.1.call-update) | async-done | bytes 1638416 | tf_op jit(solution)/shard_map/all_gather | solution.py:94
  139.6 2.9 fusion.54
  142.7 5.4 %collective-permute-start.4 = (bf16[100,1,256]{2,1,0:T(2,128)(2,1)S(1)}, bf16[100,1,256]{2,1,0:T(2,128)(2,1)S(1)}, u32[]{:S(2)}, u32[]{:S(2)}) collective-permute-start(bf16[100,1,256]{2,1,0:T(2,128)(2,1)S(1)} %get-tuple-element.70), channel_id=1, source_target_pairs={{1,0},{2,1},{3,2},{4,3},{5,4},{6,5},{7,6},{8,7},{9,8},{10,9},{11,1... | collective-permute-start | bytes 153608 | tf_op jit(solution)/shard_map/ppermute | solution.py:19
  148.1 2.3 collective-permute-start.5
  150.5 3.3 %sqrt_reduce_fusion = f32[100,2,256]{2,1,0:T(2,128)S(1)} fusion(f32[8,100,2,256]{3,2,1,0:T(2,128)S(1)} %copy-done.2, f32[100,2,256]{2,1,0:T(2,128)S(1)} %copy-done.7), kind=kLoop, calls=%fused_computation.1 | loop fusion | flops 1587200 | bytes 2048000 | tf_op jit(solution)/shard_map/reduce_sum | solution.py:69
  153.8 9.2 %fusion.38 = f32[]{:T(128)} fusion(f32[100,2,256]{2,1,0:T(2,128)S(1)} %sqrt_reduce_fusion, f32[8,100,2,256]{3,2,1,0:T(2,128)S(1)} %copy-done.2, f32[2,256]{1,0:T(2,128)S(1)} %get-tuple-element.71), kind=kLoop, calls=%fused_computation.121 | loop fusion | flops 5939199 | bytes 1845252 | tf_op jit(solution)/shard_map/reduce_sum | solution.py:74
  163.0 0.8 convolution_bitcast_fusion
  164.5 1.0 fusion.44
  165.5 0.6 fusion.55
  166.3 0.3 fusion.49
  166.6 0.6 fusion.53
  167.2 0.2 maximum_dynamic-update-slice_fusion.2
  167.6 0.3 maximum_dynamic-update-slice_fusion.1
  167.8 0.2 maximum_dynamic-update-slice_fusion
  168.0 0.2 fusion.46
  168.3 0.5 fusion.51
  168.8 0.7 pad.84
  169.5 0.2 copy.76
  169.7 5.1 %fusion.7 = f32[256,2304]{1,0:T(8,128)} fusion(bf16[2304,512]{1,0:T(8,128)(2,1)} %copy-done.8, f32[256,512]{0,1:T(8,128)} %get-tuple-element.74, bf16[900,512]{1,0:T(8,128)(2,1)S(1)} %bitcast.198, bf16[256,900]{0,1:T(8,128)(2,1)} %reshape.200), kind=kOutput, calls=%fused_computation.38 | convolution fusion | flops 842530816 | bytes 6625280 | tf_op jit(solution)/shard_map/dot_general | solution.py:113
  174.9 112.1 %all-reduce.2 = (bf16[256,2304]{1,0:T(8,128)(2,1)}, bf16[100,2304]{1,0:T(8,128)(2,1)}, f32[]{:T(128)}) all-reduce(f32[256,2304]{1,0:T(8,128)} %fusion.7, f32[100,2304]{1,0:T(8,128)S(1)} %convolution_bitcast_fusion, f32[]{:T(128)S(6)} %div.74), channel_id=1, replica_groups=mesh['ens'=8,'dom'=64] {'ens','dom'}, use_global_device_ids=true, to_apply=%region_0.1 | all-reduce | flops 820225 | bytes 4921352 | tf_op jit(solution)/shard_map/psum | solution.py:114
  (69 shorter events, 3.0 us)
Async XLA Ops:
  7.2 29.0 %copy-start = (bf16[256,2304]{1,0:T(8,128)(2,1)S(1)}, bf16[256,2304]{1,0:T(8,128)(2,1)}, u32[]{:S(2)}) copy-start(bf16[256,2304]{1,0:T(8,128)(2,1)} %param.6) | copy-start | bytes 3538948
  7.2 22.2 %copy-start.1 = (bf16[1,256,2,256]{3,2,1,0:T(2,128)(2,1)S(1)}, bf16[1,256,2,256]{3,2,1,0:T(2,128)(2,1)}, u32[]{:S(2)}) copy-start(bf16[1,256,2,256]{3,2,1,0:T(2,128)(2,1)} %param.5) | copy-start | bytes 786436
  7.2 132.4 %all-gather.2.cloned.1.call-start = ((), (), s32[]{:S(2)}) async-start(), calls=%async_computation | async-start | bytes 1843200 | tf_op jit(solution)/shard_map/all_gather | solution.py:94
  8.8 11.1 %collective-permute-start = (bf16[256,1,256]{2,1,0:T(2,128)(2,1)S(1)}, bf16[256,1,256]{2,1,0:T(2,128)(2,1)S(1)}, u32[]{:S(2)}, u32[]{:S(2)}) collective-permute-start(bf16[256,1,256]{2,1,0:T(2,128)(2,1)S(1)} %get-tuple-element.56), channel_id=1, source_target_pairs={{0,1},{1,2},{2,3},{3,4},{4,5},{5,6},{6,7},{7,8},{8,9},{9,10},{10,1... | collective-permute-start | bytes 393224 | tf_op jit(solution)/shard_map/ppermute | solution.py:18
  13.5 10.3 %collective-permute-start.1 = (bf16[256,1,256]{2,1,0:T(2,128)(2,1)S(1)}, bf16[256,1,256]{2,1,0:T(2,128)(2,1)S(1)}, u32[]{:S(2)}, u32[]{:S(2)}) collective-permute-start(bf16[256,1,256]{2,1,0:T(2,128)(2,1)S(1)} %get-tuple-element.55), channel_id=1, source_target_pairs={{1,0},{2,1},{3,2},{4,3},{5,4},{6,5},{7,6},{8,7},{9,8},{10,9},{11,1... | collective-permute-start | bytes 393224 | tf_op jit(solution)/shard_map/ppermute | solution.py:19
  36.2 1.7 copy-start.8
  38.0 4.5 %collective-permute-start.2 = (bf16[256,1,256]{2,0,1:T(8,128)(2,1)S(1)}, bf16[256,1,256]{2,0,1:T(8,128)(2,1)S(1)}, u32[]{:S(2)}, u32[]{:S(2)}) collective-permute-start(bf16[256,1,256]{2,0,1:T(8,128)(2,1)S(1)} %get-tuple-element.44), channel_id=1, source_target_pairs={{0,1},{1,2},{2,3},{3,4},{4,5},{5,6},{6,7},{7,8},{8,9},{9,10},{10,1... | collective-permute-start | bytes 393224 | tf_op jit(solution)/shard_map/ppermute | solution.py:18
  40.0 7.6 %collective-permute-start.3 = (bf16[256,1,256]{2,0,1:T(8,128)(2,1)S(1)}, bf16[256,1,256]{2,0,1:T(8,128)(2,1)S(1)}, u32[]{:S(2)}, u32[]{:S(2)}) collective-permute-start(bf16[256,1,256]{2,0,1:T(8,128)(2,1)S(1)} %get-tuple-element.43), channel_id=1, source_target_pairs={{1,0},{2,1},{3,2},{4,3},{5,4},{6,5},{7,6},{8,7},{9,8},{10,9},{11,1... | collective-permute-start | bytes 393224 | tf_op jit(solution)/shard_map/ppermute | solution.py:19
  49.7 1.4 copy-start.3
  55.3 3.1 %copy-start.5 = (bf16[100,2304]{1,0:T(8,128)(2,1)S(1)}, bf16[100,2304]{1,0:T(8,128)(2,1)}, u32[]{:S(2)}) copy-start(bf16[100,2304]{1,0:T(8,128)(2,1)} %param.7) | copy-start | bytes 1382404
  59.3 2.3 copy-start.9
  59.3 80.3 %copy-start.7 = (f32[100,2,256]{2,1,0:T(2,128)S(1)}, f32[100,2,256]{2,1,0:T(2,128)}, u32[]{:S(2)}) copy-start(f32[100,2,256]{2,1,0:T(2,128)} %param.8) | copy-start | bytes 614404
  60.2 79.4 %copy-start.6 = (f32[1,100,2,256]{3,2,1,0:T(2,128)S(1)}, f32[1,100,2,256]{3,2,1,0:T(2,128)}, u32[]{:S(2)}) copy-start(f32[1,100,2,256]{3,2,1,0:T(2,128)} %broadcast_in_dim_reshape.7) | copy-start | bytes 614404
  139.6 10.9 %copy-start.2 = (f32[8,100,2,256]{3,2,1,0:T(2,128)S(1)}, f32[8,100,2,256]{3,2,1,0:T(2,128)}, u32[]{:S(2)}) copy-start(f32[8,100,2,256]{3,2,1,0:T(2,128)} %all-gather.2.cloned.1.call-done) | copy-start | bytes 4915204
  142.7 21.8 %collective-permute-start.4 = (bf16[100,1,256]{2,1,0:T(2,128)(2,1)S(1)}, bf16[100,1,256]{2,1,0:T(2,128)(2,1)S(1)}, u32[]{:S(2)}, u32[]{:S(2)}) collective-permute-start(bf16[100,1,256]{2,1,0:T(2,128)(2,1)S(1)} %get-tuple-element.70), channel_id=1, source_target_pairs={{1,0},{2,1},{3,2},{4,3},{5,4},{6,5},{7,6},{8,7},{9,8},{10,9},{11,1... | collective-permute-start | bytes 153608 | tf_op jit(solution)/shard_map/ppermute | solution.py:19
  148.1 14.9 %copy-start.4 = (bf16[2304,2,256]{2,0,1:T(8,128)(2,1)S(1)}, bf16[2304,2,256]{2,0,1:T(8,128)(2,1)}, u32[]{:S(2)}) copy-start(bf16[2304,2,256]{2,0,1:T(8,128)(2,1)} %copy-done.3) | copy-start | bytes 7077892
  148.1 16.4 %collective-permute-start.5 = (bf16[100,1,256]{2,1,0:T(2,128)(2,1)S(1)}, bf16[100,1,256]{2,1,0:T(2,128)(2,1)S(1)}, u32[]{:S(2)}, u32[]{:S(2)}) collective-permute-start(bf16[100,1,256]{2,1,0:T(2,128)(2,1)S(1)} %get-tuple-element.69), channel_id=1, source_target_pairs={{0,1},{1,2},{2,3},{3,4},{4,5},{5,6},{6,7},{7,8},{8,9},{9,10},{10,1... | collective-permute-start | bytes 153608 | tf_op jit(solution)/shard_map/ppermute | solution.py:18
Sparse Core Ops, SparseCore 0:
  60.3 79.2 all-gather.1
where the time goes:
time: 296 us
  blocking collectives  112 us (38%)
  waiting for transfers between devices  86.6 us (29%)
  other arithmetic  33.5 us (11%)
  starting transfers between devices  22.4 us (8%)
  between operations  17.1 us (6%)
  local copies, waits for them, and re-layouts  15.5 us (5%)
  matrix products  8.48 us (3%)
    psum x1, blocking collectives, body(): lax.psum((grad_one, grad_two, partial_loss), ('ens', 'dom'))  112 us
    all_gather x1, waiting for transfers between devices, body(): lax.all_gather(ensemble_outlook[None], 'ens', axis=0, tiled=True)  77.8 us
    ppermute x3, starting transfers between devices, padded_2(): after = lax.ppermute(leading, axis, down)  13.5 us
    reduce_sum x1, other arithmetic, probabilistic_skill_total(): jnp.sum(area_factor[None] * (skill - pairs / (members * (members - 1))))  9.21 us
    ppermute x3, starting transfers between devices, padded_2(): before = lax.ppermute(last, axis, up)  8.81 us
    ppermute x3, waiting for transfers between devices, padded_2(): after = lax.ppermute(leading, axis, down)  8.79 us
    concatenate x6, other arithmetic, padded_2(): array = jnp.concatenate([before, array, after], axis=dim)  8.75 us
    unnamed x50, local copies, waits for them, and re-layouts  7.29 us
  transfers between devices with their start and end apart: 7, of which 3 were waited for; matrix products, arithmetic and copies ran while one was open for 5% of the time, Pallas kernels for 0%

commit v1 on v0

v1 whole, which is shorter than its diff:
```python
import jax
import jax.numpy as jnp
from jax import lax
from jax.sharding import Mesh
from jax.sharding import PartitionSpec as P

SOFTNESS = 0.25
LAND_WEIGHT = 2.0
LOSS_SCALE = 65536.0

ENS = ("x", "yh")
DOM = ("z", "yl", "c")
PARTS = {"x": 4, "yh": 2, "z": 8, "yl": 4, "c": 2}
F32 = jnp.float32
BF16 = jnp.bfloat16


def activate(values):
    return jax.nn.gelu(values, approximate=True)


def columns(padded, row_count):
    pieces = []
    for row_off in range(3):
        stripe = padded[:, row_off : row_off + row_count, :]
        for lon_off in range(3):
            pieces.append(jnp.roll(stripe, 1 - lon_off, axis=2))
    stacked = jnp.concatenate(pieces, axis=0)
    return stacked.reshape(stacked.shape[0], row_count * padded.shape[2])


def back_columns(padded, row_count):
    pieces = []
    for row_off in range(3):
        stripe = padded[:, 2 - row_off : 2 - row_off + row_count, :]
        for lon_off in range(3):
            pieces.append(jnp.roll(stripe, lon_off - 1, axis=2))
    stacked = jnp.concatenate(pieces, axis=0)
    return stacked.reshape(stacked.shape[0], row_count * padded.shape[2])


def soft_abs(diff):
    return jnp.sqrt(diff * diff + SOFTNESS * SOFTNESS)


def with_neighbours(array, width):
    size = lax.axis_size(DOM)
    up = [(i, i + 1) for i in range(size - 1)]
    down = [(j, i) for i, j in up]
    before = lax.ppermute(array[:, array.shape[1] - width :], DOM, up)
    after = lax.ppermute(array[:, :width], DOM, down)
    return jnp.concatenate([before, array, after], axis=1)


def exchange(array, axes):
    return lax.all_to_all(array, axes, 0, 0, tiled=True)


def body(features, w_first, later_kernel_matrix, observed_state, land):
    local = features[0]
    channels, row_count, lon_count = local.shape
    cells = row_count * lon_count
    variables = observed_state.shape[0]
    members = lax.axis_size(ENS)
    dom_size = lax.axis_size(DOM)
    dom = lax.axis_index(DOM)
    mesh_points = float(variables * row_count * dom_size * lon_count)

    padded = with_neighbours(local, 2)
    wide = row_count + 2
    pre_wide = jnp.dot(w_first, columns(padded, wide), preferred_element_type=F32)
    pre_wide = pre_wide.reshape(channels, wide, lon_count)
    row = jnp.arange(wide)
    inside = ((row > 0) | (dom > 0)) & ((row < wide - 1) | (dom < dom_size - 1))
    hidden_pad = jnp.where(inside[None, :, None], activate(pre_wide), 0.0).astype(BF16)
    before = pre_wide[:, 1 : 1 + row_count].reshape(channels, cells)
    second_columns = columns(hidden_pad, row_count)
    outlook = jnp.dot(later_kernel_matrix, second_columns, preferred_element_type=F32)

    share = -(-variables // members)
    spare = share * members - variables
    area = (1.0 + LAND_WEIGHT * land.astype(F32)).reshape(1, cells)
    mine = lax.axis_index(ENS) * share
    obs = jnp.pad(observed_state.reshape(variables, cells), ((0, spare), (0, 0)))
    obs = lax.dynamic_slice_in_dim(obs, mine, share, axis=0)
    every = exchange(
        jnp.pad(outlook, ((0, spare), (0, 0))).reshape(members, share, cells), ENS
    )
    real = (mine + jnp.arange(share) < variables)[:, None]
    slopes = [None] * members
    crps = jnp.zeros((share, cells), F32)
    pairs = jnp.zeros((share, cells), F32)
    for p in range(members):
        d = every[p] - obs
        square = d * d + SOFTNESS * SOFTNESS
        inverse = lax.rsqrt(square)
        crps = crps + square * inverse
        slopes[p] = d * inverse / members
    spread = [jnp.zeros((share, cells), F32)] * members
    for p in range(members):
        for q in range(p + 1, members):
            d = every[p] - every[q]
            square = d * d + SOFTNESS * SOFTNESS
            inverse = lax.rsqrt(square)
            pairs = pairs + square * inverse
            s = d * inverse
            spread[p] = spread[p] + s
            spread[q] = spread[q] - s
    count = members * (members - 1)
    score = area * (crps / members - pairs / count)
    partial_loss = jnp.sum(jnp.where(real, score, 0.0)) / mesh_points
    errors = jnp.stack(
        [LOSS_SCALE / mesh_points * area * (slopes[p] - spread[p] / count) for p in range(members)]
    ).astype(BF16)
    errors = exchange(errors, ENS).reshape(share * members, cells)[:variables]

    err_pad = with_neighbours(errors.reshape(variables, row_count, lon_count), 1)
    w_back = (
        later_kernel_matrix.reshape(variables, 9, channels)
        .transpose(2, 1, 0)
        .reshape(channels, 9 * variables)
    )
    back = jnp.dot(w_back, back_columns(err_pad, row_count), preferred_element_type=F32)
    unused_out, pull = jax.vjp(activate, before)
    pre_grad = pull(back)[0].astype(BF16)
    dims = (((1,), (1,)), ((), ()))
    cols_first = columns(padded[:, 1 : 1 + wide], row_count)
    grad_two = lax.dot_general(errors, second_columns, dims, preferred_element_type=F32)
    grad_one = lax.dot_general(pre_grad, cols_first, dims, preferred_element_type=F32)

    total_rows = 384
    width = grad_one.shape[1]
    loss_row = jnp.pad(partial_loss.reshape(1, 1), ((0, 0), (0, width - 1)))
    filler = jnp.zeros((total_rows - channels - variables - 1, width), F32)
    grads = jnp.concatenate([grad_one, grad_two, loss_row, filler], axis=0).astype(BF16)
    xc, y = ("x", "c"), ("yh", "yl")
    part = exchange(grads.reshape(8, 48, width), xc)
    part = jnp.sum(part.astype(F32), axis=0).astype(BF16)
    part = exchange(part.reshape(8, 6, width), y)
    part = jnp.sum(part.astype(F32), axis=0).astype(BF16)
    part = exchange(jnp.broadcast_to(part[None], (8, 6, width)), "z")
    part = jnp.sum(part.astype(F32), axis=0).astype(BF16)
    part = exchange(jnp.broadcast_to(part[None], (8, 6, width)), y)
    part = part.reshape(48, width)
    totals = lax.all_gather(part, xc, axis=0, tiled=True)
    return (
        outlook.reshape(1, variables, row_count, lon_count),
        totals[:channels],
        totals[channels : channels + variables],
        totals[channels + variables, 0].astype(F32),
    )


def solution(mesh):
    split = Mesh(mesh.devices.reshape(tuple(PARTS.values())), tuple(PARTS))
    placed = (P(ENS, None, DOM, None), P(), P(), P(None, DOM, None), P(DOM, None))
    return jax.shard_map(
        body,
        mesh=split,
        in_specs=placed,
        out_specs=(P(ENS, None, DOM, None), P(), P(), P()),
        check_vma=False,
    )
```

time: 296 us -> 238 us (0.80)
  waiting for transfers between devices: 86.6 us -> 31.8 us
  blocking collectives: 112 us -> 82 us
  local copies, waits for them, and re-layouts: 15.5 us -> 32.6 us
  starting transfers between devices: 22.4 us -> 33.6 us
    psum x1 -> x0, blocking collectives: 112 us -> none  [body(): lax.psum((grad_one, grad_two, partial_loss), ('ens', 'dom'))]
    all_to_all x0 -> x4, blocking collectives: none -> 82 us  [exchange(): return lax.all_to_all(array, axes, 0, 0, tiled=True)]
    all_gather x1, waiting for transfers between devices: 77.8 us -> 23.9 us  [body(): totals = lax.all_gather(part, xc, axis=0, tiled=True)]
    all_to_all x0 -> x2, starting transfers between devices: none -> 17 us  [exchange(): return lax.all_to_all(array, axes, 0, 0, tiled=True)]
    reduce_sum x2 -> x4, other arithmetic: 12.6 us -> 1.25 us  [the longest x1 0.85 us: body(): partial_loss = jnp.sum(jnp.where(real, score, 0.0)) / mesh_points]
    ppermute x6 -> x4, waiting for transfers between devices: 8.8 us -> 0.64 us  [the longest x2 0.64 us: with_neighbours(): after = lax.ppermute(array[:, :width], DOM, down)]
    all_to_all x0 -> x2, waiting for transfers between devices: none -> 7.23 us  [exchange(): return lax.all_to_all(array, axes, 0, 0, tiled=True)]
    concatenate x7 -> x12, other arithmetic: 9.28 us -> 16.2 us  [the longest x8 13.8 us: with_neighbours(): return jnp.concatenate([before, array, after], axis=1)]
  transfers between devices with their start and end apart: 7 -> 7, of which waited for: 3 -> 3; matrix products, arithmetic and copies ran while one was open for 5% -> 9% of each run, Pallas kernels for 0% -> 0%
where the time goes in v1:
time: 238 us; the launch traced here: 237 us
  blocking collectives  82 us (34%)
  starting transfers between devices  33.6 us (14%)
  other arithmetic  32.9 us (14%)
  local copies, waits for them, and re-layouts  32.6 us (14%)
  waiting for transfers between devices  31.8 us (13%)
  between operations  17.1 us (7%)
  matrix products  7.21 us (3%)
    all_to_all x4, blocking collectives, exchange(): return lax.all_to_all(array, axes, 0, 0, tiled=True)  82 us
    all_gather x1, waiting for transfers between devices, body(): totals = lax.all_gather(part, xc, axis=0, tiled=True)  23.9 us
    all_to_all x2, starting transfers between devices, exchange(): return lax.all_to_all(array, axes, 0, 0, tiled=True)  17 us
    unnamed x58, local copies, waits for them, and re-layouts  13.9 us
    concatenate x8, other arithmetic, with_neighbours(): return jnp.concatenate([before, array, after], axis=1)  13.8 us
    unnamed x20, other arithmetic  9.84 us
    ppermute x2, starting transfers between devices, with_neighbours(): before = lax.ppermute(array[:, array.shape[1] - width:], DOM, up)  9.21 us
    ppermute x2, starting transfers between devices, with_neighbours(): after = lax.ppermute(array[:, :width], DOM, down)  7.42 us
  transfers between devices with their start and end apart: 7, of which 3 were waited for; matrix products, arithmetic and copies ran while one was open for 9% of the time, Pallas kernels for 0%

profile of v1, /device:TPU:1, one launch (start us, length us, event | category | flops | bytes accessed | tf_op | source)
XLA Modules:
  0.0 237.2 jit_solution(4860936856141739908)
XLA Ops:
  7.2 4.7 %collective-permute-start = (bf16[256,2,256]{2,1,0:T(2,128)(2,1)}, bf16[256,2,256]{2,1,0:T(2,128)(2,1)S(1)}, u32[]{:S(2)}, u32[]{:S(2)}) collective-permute-start(bf16[256,2,256]{2,1,0:T(2,128)(2,1)} %bitcast.619), channel_id=1, source_target_pairs={{0,1},{1,2},{2,3},{3,4},{4,5},{5,6},{6,7},{7,8},{8,9},{9,10},{10,1... | collective-permute-start | bytes 786440 | tf_op jit(solution)/shard_map/ppermute | solution.py:50
  11.9 5.5 %collective-permute-start.1 = (bf16[256,2,256]{2,1,0:T(2,128)(2,1)}, bf16[256,2,256]{2,1,0:T(2,128)(2,1)S(1)}, u32[]{:S(2)}, u32[]{:S(2)}) collective-permute-start(bf16[256,2,256]{2,1,0:T(2,128)(2,1)} %bitcast.620), channel_id=1, source_target_pairs={{1,0},{2,1},{3,2},{4,3},{5,4},{6,5},{7,6},{8,7},{9,8},{10,9},{11,1... | collective-permute-start | bytes 786440 | tf_op jit(solution)/shard_map/ppermute | solution.py:51
  17.4 0.7 add_bitcast_fusion
  18.1 1.0 pad.91
  19.2 1.4 copy.13
  20.8 0.8 reshape.115
  22.5 0.8 pad_maximum_fusion
  23.3 0.7 fusion.161
  24.4 3.1 %fusion.14 = (bf16[256,4,255]{2,1,0:T(4,128)(2,1)S(1)}, bf16[256,4,255]{2,1,0:T(4,128)(2,1)S(1)}, bf16[256,4,255]{2,1,0:T(4,128)(2,1)S(1)}, bf16[256,4,255]{2,1,0:T(4,128)(2,1)S(1)}) fusion(bf16[256,2,256]{2,1,0:T(2,128)(2,1)S(1)} %bitcast.623, bf16[256,2,256]{2,1,0:T(2,128)(2,1)S(1)} %collective-permute-done.1, bf16[256,2,256]{2,1,0:T(2,128)(2,1)S(1)} %collective-permute-done), kind=kLoop, calls=%fused_computation.62 | loop fusion | flops 4177920 | bytes 2875392 | tf_op jit(solution)/shard_map/concatenate | solution.py:52
  27.5 1.4 fusion.29
  33.9 1.5 copy.17
  35.5 1.5 fusion.166
  38.3 1.4 copy-done.2
  39.7 0.8 convolution_bitcast_fusion.1
  40.6 0.7 reshape.110
  41.3 7.9 %all-to-all-start = ((f32[8,13,512]{2,1,0:T(8,128)}), f32[8,13,512]{2,1,0:T(8,128)S(1)}, u32[]{:S(2)}, u32[]{:S(2)}) async-start(f32[8,13,512]{2,1,0:T(8,128)} %reshape.110), calls=%async_computation | async-start | bytes 524288 | tf_op jit(solution)/shard_map/all_to_all | solution.py:56
  49.3 3.9 %fusion.32 = (bf16[256,2,255]{2,1,0:T(2,128)(2,1)S(1)}, bf16[256,2,255]{2,1,0:T(2,128)(2,1)S(1)}, bf16[256,2,255]{2,1,0:T(2,128)(2,1)S(1)}, bf16[256,2,255]{2,1,...) fusion(bf16[256,2,256]{2,1,0:T(2,128)(2,1)S(1)} %bitcast.627, ...), kind=kLoop, calls=%fused_computation.88 | loop fusion | flops 2088960 | bytes 2877440 | tf_op jit(solution)/shard_map/concatenate | solution.py:52
  53.1 1.8 fusion.39
  54.9 1.0 pad_maximum_fusion.3
  56.0 1.3 fusion.31
  57.3 1.0 pad_maximum_fusion.5
  58.4 1.0 pad_maximum_fusion.7
  59.8 1.4 copy-done.3
  61.2 0.9 fusion.22
  65.5 0.7 constant_dynamic-update-slice_fusion.2
  66.9 0.7 constant_dynamic-update-slice_fusion
  67.6 9.1 %all-to-all-start.1 = ((bf16[8,13,512]{2,1,0:T(8,128)(2,1)}), bf16[8,13,512]{2,1,0:T(8,128)(2,1)S(1)}, u32[]{:S(2)}, u32[]{:S(2)}) async-start(bf16[8,13,512]{2,1,0:T(8,128)(2,1)} %constant_dynamic-update-slice_fusion), calls=%async_computation.1 | async-start | bytes 262144 | tf_op jit(solution)/shard_map/all_to_all | solution.py:56
  76.6 0.7 constant_dynamic-update-slice_fusion.8
  77.4 0.9 fusion.123
  78.9 7.2 %all-to-all-done.1 = bf16[8,13,512]{2,1,0:T(8,128)(2,1)S(1)} async-done(((bf16[8,13,512]{2,1,0:T(8,128)(2,1)}), bf16[8,13,512]{2,1,0:T(8,128)(2,1)S(1)}, u32[]{:S(2)}, u32[]{:S(2)}) %all-to-all-start.1) | async-done | bytes 106528 | tf_op jit(solution)/shard_map/all_to_all | solution.py:56
  86.4 1.9 collective-permute-start.2
  88.3 4.5 %collective-permute-start.3 = (bf16[100,1,256]{2,1,0:T(2,128)(2,1)S(1)}, bf16[100,1,256]{2,1,0:T(2,128)(2,1)S(1)}, u32[]{:S(2)}, u32[]{:S(2)}) collective-permute-start(bf16[100,1,256]{2,1,0:T(2,128)(2,1)S(1)} %get-tuple-element.68), channel_id=1, source_target_pairs={{0,1},{1,2},{2,3},{3,4},{4,5},{5,6},{6,7},{7,8},{8,9},{9,10},{10,1... | collective-permute-start | bytes 153608 | tf_op jit(solution)/shard_map/ppermute | solution.py:50
  92.8 2.2 convolution_convert_fusion.1
  95.0 1.0 fusion.42
  99.4 1.5 fusion.46
  104.6 7.4 %concatenate.183 = bf16[900,512]{1,0:T(8,128)(2,1)S(1)} concatenate(bf16[100,512]{1,0:T(8,128)(2,1)} %bitcast.678, bf16[100,512]{1,0:T(8,128)(2,1)} %bitcast.679, bf16[100,512]{1,0:T(8,128)(2,1)} %bitcast.680, bf16[100,512]{1,0:T(8,128)(2,1)} %bitcast.676, bf16[100,512]{1,0:T(8,128)(2,1)S(1)} %bitcast.648, bf16[100,512]{1,0:T(8,128)(2,1)} %bitcast.677, ...), dimensions={0} | concatenate | bytes 1843200 | tf_op jit(solution)/shard_map/concatenate | solution.py:38
  112.1 1.9 fusion.25
  114.0 0.8 convolution_convert_fusion
  115.2 25.0 %all_to_all.30 = bf16[8,48,2304]{2,1,0:T(8,128)(2,1)S(1)} all-to-all(bf16[8,48,2304]{2,1,0:T(8,128)(2,1)S(1)} %bitcast.641), channel_id=1, replica_groups=mesh['x'=4,'yh'=2,'z'=8,'yl'=4,'c'=2] {'x','c'}, dimensions={0} | all-to-all | bytes 3538944 | tf_op jit(solution)/shard_map/all_to_all | solution.py:56
  140.6 19.2 %all_to_all.31 = bf16[8,6,2304]{2,1,0:T(8,128)(2,1)S(1)} all-to-all(bf16[8,6,2304]{2,1,0:T(8,128)(2,1)S(1)} %reshape.118), channel_id=1, replica_groups=mesh['x'=4,'yh'=2,'z'=8,'yl'=4,'c'=2] {'yh','yl'}, dimensions={0} | all-to-all | bytes 442368 | tf_op jit(solution)/shard_map/all_to_all | solution.py:56
  159.9 24.1 %all_to_all.32 = bf16[8,6,2304]{2,1,0:T(8,128)(2,1)S(1)} all-to-all(bf16[8,6,2304]{2,1,0:T(8,128)(2,1)S(1)} %broadcast_in_dim.47), channel_id=1, replica_groups=mesh['x'=4,'yh'=2,'z'=8,'yl'=4,'c'=2] {'z'}, dimensions={0} | all-to-all | bytes 442368 | tf_op jit(solution)/shard_map/all_to_all | solution.py:56
  184.2 13.6 %all_to_all.33 = bf16[8,6,2304]{2,1,0:T(8,128)(2,1)S(1)} all-to-all(bf16[8,6,2304]{2,1,0:T(8,128)(2,1)S(1)} %broadcast_in_dim.48), channel_id=1, replica_groups=mesh['x'=4,'yh'=2,'z'=8,'yl'=4,'c'=2] {'yh','yl'}, dimensions={0} | all-to-all | bytes 442368 | tf_op jit(solution)/shard_map/all_to_all | solution.py:56
  197.7 0.8 reshape.119
  198.5 0.8 reshape.108
  199.3 23.9 %all-gather.2.cloned.1.call-done = bf16[384,2304]{1,0:T(8,128)(2,1)} async-done(((bf16[48,2304]{1,0:T(8,128)(2,1)}), bf16[384,2304]{1,0:T(8,128)(2,1)}) %all-gather.2.cloned.1.call-update) | async-done | bytes 1769488 | tf_op jit(solution)/shard_map/all_gather | solution.py:145
  223.2 1.2 slice.497
  225.1 2.4 slice.495
  227.4 1.8 slice.496
  (105 shorter events, 20.6 us)
Async XLA Ops:
  7.2 28.3 %copy-start = (bf16[256,2304]{1,0:T(8,128)(2,1)S(1)}, bf16[256,2304]{1,0:T(8,128)(2,1)}, u32[]{:S(2)}) copy-start(bf16[256,2304]{1,0:T(8,128)(2,1)} %param.6) | copy-start | bytes 3538948
  7.2 14.5 %copy-start.1 = (bf16[1,256,2,256]{3,2,1,0:T(2,128)(2,1)S(1)}, bf16[1,256,2,256]{3,2,1,0:T(2,128)(2,1)}, u32[]{:S(2)}) copy-start(bf16[1,256,2,256]{3,2,1,0:T(2,128)(2,1)} %param.5) | copy-start | bytes 786436
  7.2 14.6 %collective-permute-start = (bf16[256,2,256]{2,1,0:T(2,128)(2,1)}, bf16[256,2,256]{2,1,0:T(2,128)(2,1)S(1)}, u32[]{:S(2)}, u32[]{:S(2)}) collective-permute-start(bf16[256,2,256]{2,1,0:T(2,128)(2,1)} %bitcast.619), channel_id=1, source_target_pairs={{0,1},{1,2},{2,3},{3,4},{4,5},{5,6},{6,7},{7,8},{8,9},{9,10},{10,1... | collective-permute-start | bytes 786440 | tf_op jit(solution)/shard_map/ppermute | solution.py:50
  11.9 10.5 %collective-permute-start.1 = (bf16[256,2,256]{2,1,0:T(2,128)(2,1)}, bf16[256,2,256]{2,1,0:T(2,128)(2,1)S(1)}, u32[]{:S(2)}, u32[]{:S(2)}) collective-permute-start(bf16[256,2,256]{2,1,0:T(2,128)(2,1)} %bitcast.620), channel_id=1, source_target_pairs={{1,0},{2,1},{3,2},{4,3},{5,4},{6,5},{7,6},{8,7},{9,8},{10,9},{11,1... | collective-permute-start | bytes 786440 | tf_op jit(solution)/shard_map/ppermute | solution.py:51
  36.9 1.0 copy-start.5
  37.9 1.8 copy-start.7
  38.3 1.4 copy-start.2
  41.3 20.8 %all-to-all-start = ((f32[8,13,512]{2,1,0:T(8,128)}), f32[8,13,512]{2,1,0:T(8,128)S(1)}, u32[]{:S(2)}, u32[]{:S(2)}) async-start(f32[8,13,512]{2,1,0:T(8,128)} %reshape.110), calls=%async_computation | async-start | bytes 524288 | tf_op jit(solution)/shard_map/all_to_all | solution.py:56
  58.4 1.2 copy-start.6
  59.8 1.4 copy-start.3
  67.6 18.6 %all-to-all-start.1 = ((bf16[8,13,512]{2,1,0:T(8,128)(2,1)}), bf16[8,13,512]{2,1,0:T(8,128)(2,1)S(1)}, u32[]{:S(2)}, u32[]{:S(2)}) async-start(bf16[8,13,512]{2,1,0:T(8,128)(2,1)} %constant_dynamic-update-slice_fusion), calls=%async_computation.1 | async-start | bytes 262144 | tf_op jit(solution)/shard_map/all_to_all | solution.py:56
  76.6 146.6 %all-gather.2.cloned.1.call-start = ((), (), s32[]{:S(2)}) async-start(), calls=%async_computation.6 | async-start | bytes 1990656 | tf_op jit(solution)/shard_map/all_gather | solution.py:145
  86.4 8.6 %collective-permute-start.2 = (bf16[100,1,256]{2,1,0:T(2,128)(2,1)S(1)}, bf16[100,1,256]{2,1,0:T(2,128)(2,1)S(1)}, u32[]{:S(2)}, u32[]{:S(2)}) collective-permute-start(bf16[100,1,256]{2,1,0:T(2,128)(2,1)S(1)} %get-tuple-element.69), channel_id=1, source_target_pairs={{1,0},{2,1},{3,2},{4,3},{5,4},{6,5},{7,6},{8,7},{9,8},{10,9},{11,1... | collective-permute-start | bytes 153608 | tf_op jit(solution)/shard_map/ppermute | solution.py:51
  88.3 6.7 %collective-permute-start.3 = (bf16[100,1,256]{2,1,0:T(2,128)(2,1)S(1)}, bf16[100,1,256]{2,1,0:T(2,128)(2,1)S(1)}, u32[]{:S(2)}, u32[]{:S(2)}) collective-permute-start(bf16[100,1,256]{2,1,0:T(2,128)(2,1)S(1)} %get-tuple-element.68), channel_id=1, source_target_pairs={{0,1},{1,2},{2,3},{3,4},{4,5},{5,6},{6,7},{7,8},{8,9},{9,10},{10,1... | collective-permute-start | bytes 153608 | tf_op jit(solution)/shard_map/ppermute | solution.py:50
  112.1 2.0 copy-start.4
Sparse Core Ops, SparseCore 0:
  198.6 24.5 all-gather.1

commit v2 on v0

v2 whole, which is shorter than its diff:
```python
import jax
import jax.numpy as jnp
from jax import lax
from jax.experimental import pallas as pl
from jax.experimental.pallas import tpu as pltpu
from jax.sharding import Mesh
from jax.sharding import PartitionSpec as P

SOFTNESS = 0.25
LAND_WEIGHT = 2.0
LOSS_SCALE = 65536.0
GELU_A = 0.7978845608028654
GELU_B = 0.044715

ENS = ("x", "yh")
DOM = ("z", "yl", "c")
Y = ("yh", "yl")
PARTS = {"x": 4, "yh": 2, "z": 8, "yl": 4, "c": 2}
F32 = jnp.float32
BF16 = jnp.bfloat16

C = 256
V = 100
LON = 256
ROWS = 2
CELLS = ROWS * LON
MEMBERS = 8
SHARE = 16
VPAD = 112
TAPS = 9
LANES = 128
TILES = TAPS * C // LANES
SECOND = TILES * C
LOSS = SECOND + TILES * VPAD
FLAT = 7168
VMEM = pl.BlockSpec(memory_space=pltpu.VMEM)
SMEM = pl.BlockSpec(memory_space=pltpu.SMEM)
PARAMS = pltpu.CompilerParams(vmem_limit_bytes=40 * 1024 * 1024)
NT = (((1,), (1,)), ((), ()))


def turn(values, shift):
    return values if shift % LON == 0 else pltpu.roll(values, shift % LON, 1)


def dot(a, b):
    return jnp.dot(a, b, preferred_element_type=F32)


def split(total):
    high = total.astype(BF16)
    return high, (total - high.astype(F32)).astype(BF16)


def forward_kernel(ends, before, local, after, w1, w2, hidden, slope, outlook, stack):
    rows = [r[:, i * LON : (i + 1) * LON] for r in (before, local, after) for i in range(2)]
    wide = ROWS + 2
    for a in range(3):
        for i in range(wide):
            stack[a * C : (a + 1) * C, i * LON : (i + 1) * LON] = rows[i + a]
    for i in range(wide):
        lanes = slice(i * LON, (i + 1) * LON)
        pre = None
        for b in range(3):
            taps = jnp.concatenate(
                [w1[:, (3 * a + b) * C : (3 * a + b + 1) * C] for a in range(3)], axis=1
            )
            part = turn(dot(taps, stack[:, lanes]), 1 - b)
            pre = part if pre is None else pre + part
        square = pre * pre
        t = jnp.tanh(GELU_A * pre * (1.0 + GELU_B * square))
        half = 0.5 * (1.0 + t)
        value = pre * half
        if i == 0:
            value = value * ends[0]
        if i == wide - 1:
            value = value * ends[1]
        hidden[:, lanes] = value.astype(BF16)
        if 0 < i < wide - 1:
            own = slice((i - 1) * LON, i * LON)
            slope[:, own] = half + (0.5 * GELU_A) * pre * (1.0 - t * t) * (
                1.0 + 3.0 * GELU_B * square
            )
    outlook[V:, :] = jnp.zeros((MEMBERS * SHARE - V, CELLS), F32)
    for i in range(ROWS):
        total = None
        for b in range(3):
            part = None
            for a in range(3):
                tap = w2[:, (3 * a + b) * C : (3 * a + b + 1) * C]
                term = dot(tap, hidden[:, (i + a) * LON : (i + a + 1) * LON])
                part = term if part is None else part + term
            part = turn(part, 1 - b)
            total = part if total is None else total + part
        outlook[:V, i * LON : (i + 1) * LON] = total


def score_kernel(points, me, every, obs, land, errors, loss):
    area = 1.0 + LAND_WEIGHT * land[...].astype(F32)
    x = [every[p] for p in range(MEMBERS)]
    truth = obs[me[0]]
    count = MEMBERS * (MEMBERS - 1)
    skill = pairs = jnp.zeros((SHARE, CELLS), F32)
    slopes = []
    for p in range(MEMBERS):
        d = x[p] - truth
        square = d * d + SOFTNESS * SOFTNESS
        inverse = lax.rsqrt(square)
        skill = skill + square * inverse
        slopes.append(d * inverse * (1.0 / MEMBERS))
    for p in range(MEMBERS):
        for q in range(p + 1, MEMBERS):
            d = x[p] - x[q]
            square = d * d + SOFTNESS * SOFTNESS
            inverse = lax.rsqrt(square)
            pairs = pairs + square * inverse
            s = d * inverse * (1.0 / count)
            slopes[p] = slopes[p] - s
            slopes[q] = slopes[q] + s
    variable = me[0] * SHARE + lax.broadcasted_iota(jnp.int32, (SHARE, CELLS), 0)
    crps = area * (skill * (1.0 / MEMBERS) - pairs * (1.0 / count))
    crps = jnp.where(variable < V, crps, 0.0)
    loss[...] = jnp.sum(crps, axis=(0, 1), keepdims=True) * (1.0 / points)
    factor = area * (LOSS_SCALE / points)
    for p in range(MEMBERS):
        errors[p] = (factor * slopes[p]).astype(BF16)


def backward_kernel(
    loss, err, err_before, err_after, w_back, slope, hidden, before, local, after, out, e, pg
):
    rows = [err_before[...], err[:VPAD, :LON], err[:VPAD, LON:], err_after[...]]
    for i in range(4):
        row = rows[i].astype(F32)
        for b in range(3):
            e[b * VPAD : (b + 1) * VPAD, i * LON : (i + 1) * LON] = turn(row, b - 1).astype(BF16)
    for i in range(ROWS):
        back = None
        for a in range(3):
            start = (i + 2 - a) * LON
            term = dot(w_back[a], e[:, start : start + LON])
            back = term if back is None else back + term
        own = slice(i * LON, (i + 1) * LON)
        grad = back * slope[:, own]
        for b in range(3):
            pg[b * C : (b + 1) * C, own] = turn(grad, b - 1).astype(BF16)
    for a in range(3):
        if a == 0:
            window = jnp.concatenate([before[:, LON:], local[:, :LON]], axis=1)
        elif a == 1:
            window = local[...]
        else:
            window = jnp.concatenate([local[:, LON:], after[:, :LON]], axis=1)
        for b in range(3):
            first = lax.dot_general(
                pg[b * C : (b + 1) * C, :], window, NT, preferred_element_type=F32
            ).astype(BF16)
            second = lax.dot_general(
                e[b * VPAD : (b + 1) * VPAD, LON : 3 * LON],
                hidden[:, a * LON : a * LON + CELLS],
                NT,
                preferred_element_type=F32,
            ).astype(BF16)
            for part in range(2):
                tile = 2 * (3 * a + b) + part
                lanes = slice(part * LANES, (part + 1) * LANES)
                out[tile * C : (tile + 1) * C, :] = first[:, lanes]
                at = SECOND + tile * VPAD
                out[at : at + VPAD, :] = second[:, lanes]
    high, low = split(jnp.broadcast_to(loss[...], (1, LANES)))
    out[LOSS:, :] = jnp.zeros((FLAT - LOSS, LANES), BF16)
    row = lax.broadcasted_iota(jnp.int32, (16, LANES), 0)
    both = jnp.where(row == 0, high.astype(F32), jnp.where(row == 1, low.astype(F32), 0.0))
    out[LOSS : LOSS + 16, :] = both.astype(BF16)


def sum_kernel(row, holder, parts, out):
    total = parts[0].astype(F32)
    for i in range(1, parts.shape[0]):
        total = total + parts[i].astype(F32)
    copies = out.shape[0]
    value = total.astype(BF16)
    for i in range(copies):
        out[i] = value

    @pl.when(holder[0] == 1)
    def _():
        here = total[row : row + 16]
        loss = here[0:1] + here[1:2]
        high, low = split(loss)
        index = lax.broadcasted_iota(jnp.int32, (16, LANES), 0)
        fixed = jnp.where(index == 0, high.astype(F32), jnp.where(index == 1, low.astype(F32), 0.0))
        for i in range(copies):
            out[i, row : row + 16, :] = fixed.astype(BF16)


def summed(parts, row, holder, copies=1):
    body = lambda *refs: sum_kernel(row, *refs)
    return pl.pallas_call(
        body,
        out_shape=jax.ShapeDtypeStruct((copies,) + parts.shape[1:], BF16),
        in_specs=[SMEM, VMEM],
        out_specs=VMEM,
        compiler_params=PARAMS,
    )(holder, parts)


def last_kernel(halves, first, second, loss):
    flat = lambda at, n: halves[at : at + n, :]
    for tile in range(TILES):
        lanes = slice(tile * LANES, (tile + 1) * LANES)
        first[:, lanes] = flat(tile * C, C)
        second[:, lanes] = flat(SECOND + tile * VPAD, VPAD)[:V]
    here = flat(LOSS, 16).astype(F32)
    loss[...] = here[0:1, 0:1] + here[1:2, 0:1]


def exchange(array, axes):
    return lax.all_to_all(array, axes, 0, 0, tiled=True)


def body(features, w_first, later_kernel_matrix, observed_state, land):
    dom_size = lax.axis_size(DOM)
    dom = lax.axis_index(DOM)
    up = [(i, i + 1) for i in range(dom_size - 1)]
    down = [(j, i) for i, j in up]
    points = float(V * ROWS * dom_size * LON)

    local = features.reshape(C, CELLS)
    before = lax.ppermute(local, DOM, up)
    after = lax.ppermute(local, DOM, down)
    ends = jnp.stack([(dom > 0).astype(F32), (dom < dom_size - 1).astype(F32)])
    hidden, slope, outlook = pl.pallas_call(
        forward_kernel,
        out_shape=(
            jax.ShapeDtypeStruct((C, 4 * LON), BF16),
            jax.ShapeDtypeStruct((C, CELLS), F32),
            jax.ShapeDtypeStruct((MEMBERS * SHARE, CELLS), F32),
        ),
        in_specs=[SMEM] + [VMEM] * 5,
        out_specs=(VMEM,) * 3,
        scratch_shapes=[pltpu.VMEM((3 * C, 4 * LON), BF16)],
        compiler_params=PARAMS,
    )(ends, before, local, after, w_first, later_kernel_matrix)

    every = exchange(outlook.reshape(MEMBERS, SHARE, CELLS), ENS)
    obs = jnp.pad(observed_state.reshape(V, CELLS), ((0, MEMBERS * SHARE - V), (0, 0)))
    me = lax.axis_index(ENS).reshape(1)
    errors, loss = pl.pallas_call(
        lambda *refs: score_kernel(points, *refs),
        out_shape=(
            jax.ShapeDtypeStruct((MEMBERS, SHARE, CELLS), BF16),
            jax.ShapeDtypeStruct((1, 1), F32),
        ),
        in_specs=[SMEM] + [VMEM] * 3,
        out_specs=(VMEM,) * 2,
        compiler_params=PARAMS,
    )(me, every, obs.reshape(MEMBERS, SHARE, CELLS), land.reshape(1, CELLS))
    errors = exchange(errors, ENS).reshape(MEMBERS * SHARE, CELLS)

    err_before = lax.ppermute(errors[:VPAD, LON:], DOM, up)
    err_after = lax.ppermute(errors[:VPAD, :LON], DOM, down)
    w_back = later_kernel_matrix.reshape(V, 3, 3, C)
    w_back = jnp.pad(w_back, ((0, VPAD - V), (0, 0), (0, 0), (0, 0)))
    w_back = w_back.transpose(1, 3, 2, 0).reshape(3, C, 3 * VPAD)
    flat = pl.pallas_call(
        backward_kernel,
        out_shape=jax.ShapeDtypeStruct((FLAT, LANES), BF16),
        in_specs=[VMEM] * 10,
        out_specs=VMEM,
        scratch_shapes=[
            pltpu.VMEM((3 * VPAD, 4 * LON), BF16),
            pltpu.VMEM((3 * C, CELLS), BF16),
        ],
        compiler_params=PARAMS,
    )(loss, errors, err_before, err_after, w_back, slope, hidden, before, local, after)

    holder = jnp.bool_(True)
    row = LOSS
    size = FLAT
    part = flat
    for axes, n in (("c", 2), ("x", 4), (Y, 8)):
        size //= n
        holder = holder & (lax.axis_index(axes) == row // size)
        row %= size
        part = exchange(part.reshape(n, size, LANES), axes)
        flag = holder.astype(jnp.int32).reshape(1)
        part = summed(part, row, flag, 8 if axes == Y else 1)
    part = summed(exchange(part, "z"), row, flag, 8)
    part = exchange(part, Y).reshape(1, 8 * size, LANES)
    part = exchange(jnp.broadcast_to(part, (4, 8 * size, LANES)), "x").reshape(1, 32 * size, LANES)
    part = exchange(jnp.broadcast_to(part, (2, 32 * size, LANES)), "c").reshape(FLAT, LANES)
    first, second, loss = pl.pallas_call(
        last_kernel,
        out_shape=(
            jax.ShapeDtypeStruct((C, TAPS * C), BF16),
            jax.ShapeDtypeStruct((V, TAPS * C), BF16),
            jax.ShapeDtypeStruct((1, 1), F32),
        ),
        in_specs=[VMEM],
        out_specs=(VMEM,) * 3,
        compiler_params=PARAMS,
    )(part)
    return outlook[:V].reshape(1, V, ROWS, LON), first, second, loss.reshape(())


def solution(mesh):
    split_mesh = Mesh(mesh.devices.reshape(tuple(PARTS.values())), tuple(PARTS))
    placed = (P(ENS, None, DOM, None), P(), P(), P(None, DOM, None), P(DOM, None))
    return jax.shard_map(
        body,
        mesh=split_mesh,
        in_specs=placed,
        out_specs=(P(ENS, None, DOM, None), P(), P(), P()),
        check_vma=False,
    )
```

time: 296 us -> 168 us (0.57)
  blocking collectives: 112 us -> 46.8 us
  waiting for transfers between devices: 86.6 us -> 53.1 us
  other arithmetic: 33.5 us -> 0.08 us
  starting transfers between devices: 22.4 us -> 44.6 us
  between operations: 17.1 us -> 0.83 us
  Pallas kernels: 0 us -> 10.5 us
  matrix products: 8.48 us -> 0 us
  local copies, waits for them, and re-layouts: 15.5 us -> 11 us
    psum x1 -> x0, blocking collectives: 112 us -> none  [body(): lax.psum((grad_one, grad_two, partial_loss), ('ens', 'dom'))]
    all_gather x1 -> x0, waiting for transfers between devices: 77.8 us -> none  [body(): lax.all_gather(ensemble_outlook[None], 'ens', axis=0, tiled=True)]
    all_to_all x0 -> x5, waiting for transfers between devices: none -> 48.2 us  [exchange(): return lax.all_to_all(array, axes, 0, 0, tiled=True)]
    all_to_all x0 -> x4, blocking collectives: none -> 46.8 us  [exchange(): return lax.all_to_all(array, axes, 0, 0, tiled=True)]
    all_to_all x0 -> x5, starting transfers between devices: none -> 25.7 us  [exchange(): return lax.all_to_all(array, axes, 0, 0, tiled=True)]
    concatenate x11 -> x0, other arithmetic: 14.5 us -> none  [the longest x6 8.75 us: padded_2(): array = jnp.concatenate([before, array, after], axis=dim)]
    reduce_sum x2 -> x0, other arithmetic: 12.6 us -> none  [the longest x1 9.21 us: probabilistic_skill_total(): jnp.sum(area_factor[None] * (skill - pairs / (members * (members - 1))))]
    pallas_call x0 -> x8, Pallas kernels: none -> 10.5 us  [the longest x1 3.3 us: body(): pl.pallas_call(forward_kernel, out_shape=(jax.ShapeDtypeStruct((C, 4 * LO...]
  transfers between devices with their start and end apart: 7 -> 9, of which waited for: 3 -> 7; matrix products, arithmetic and copies ran while one was open for 5% -> 4% of each run, Pallas kernels for 0% -> 0%
where the time goes in v2:
time: 168 us; the launch traced here: 167 us
  waiting for transfers between devices  53.1 us (32%)
  blocking collectives  46.8 us (28%)
  starting transfers between devices  44.6 us (27%)
  local copies, waits for them, and re-layouts  11 us (7%)
  Pallas kernels  10.5 us (6%)
    all_to_all x5, waiting for transfers between devices, exchange(): return lax.all_to_all(array, axes, 0, 0, tiled=True)  48.2 us
    all_to_all x4, blocking collectives, exchange(): return lax.all_to_all(array, axes, 0, 0, tiled=True)  46.8 us
    all_to_all x5, starting transfers between devices, exchange(): return lax.all_to_all(array, axes, 0, 0, tiled=True)  25.7 us
    ppermute x1, starting transfers between devices, body(): err_before = lax.ppermute(errors[:VPAD, LON:], DOM, up)  6.86 us
    ppermute x1, starting transfers between devices, body(): after = lax.ppermute(local, DOM, down)  5.5 us
    ppermute x1, waiting for transfers between devices, body(): after = lax.ppermute(local, DOM, down)  4.72 us
    ppermute x1, starting transfers between devices, body(): before = lax.ppermute(local, DOM, up)  4.59 us
    unnamed x14, local copies, waits for them, and re-layouts  3.42 us
  transfers between devices with their start and end apart: 9, of which 7 were waited for; matrix products, arithmetic and copies ran while one was open for 4% of the time, Pallas kernels for 0%

profile of v2, /device:TPU:1, one launch (start us, length us, event | category | flops | bytes accessed | tf_op | source)
XLA Modules:
  0.0 166.9 jit_solution(12279089586482655697)
XLA Ops:
  0.6 0.0 copy-start.3
  0.6 1.0 copy.12
  1.7 4.6 %collective-permute-start = (bf16[256,512]{1,0:T(8,128)(2,1)S(1)}, bf16[256,512]{1,0:T(8,128)(2,1)S(1)}, u32[]{:S(2)}, u32[]{:S(2)}) collective-permute-start(bf16[256,512]{1,0:T(8,128)(2,1)S(1)} %bitcast.30), channel_id=1, source_target_pairs={{0,1},{1,2},{2,3},{3,4},{4,5},{5,6},{6,7},{7,8},{8,9},{9,10},{10,1... | collective-permute-start | bytes 786440 | tf_op jit(solution)/shard_map/ppermute | solution.py:230
  6.3 5.5 %collective-permute-start.1 = (bf16[256,512]{1,0:T(8,128)(2,1)S(1)}, bf16[256,512]{1,0:T(8,128)(2,1)S(1)}, u32[]{:S(2)}, u32[]{:S(2)}) collective-permute-start(bf16[256,512]{1,0:T(8,128)(2,1)S(1)} %bitcast.31), channel_id=1, source_target_pairs={{1,0},{2,1},{3,2},{4,3},{5,4},{6,5},{7,6},{8,7},{9,8},{10,9},{11,1... | collective-permute-start | bytes 786440 | tf_op jit(solution)/shard_map/ppermute | solution.py:231
  11.8 0.1 add_convert_fusion.ends
  11.9 0.0 collective-permute-done.before
  11.9 4.7 %collective-permute-done.1.after = bf16[256,512]{1,0:T(8,128)(2,1)S(1)} collective-permute-done((bf16[256,512]{1,0:T(8,128)(2,1)S(1)}, bf16[256,512]{1,0:T(8,128)(2,1)S(1)}, u32[]{:S(2)}, u32[]{:S(2)}) %collective-permute-start.1) | collective-permute-done | bytes 262176 | tf_op jit(solution)/shard_map/ppermute | solution.py:231
  16.6 0.0 copy-start
  16.6 1.0 copy-done
  17.6 0.0 copy-start.2
  17.6 1.3 copy-done.2
  18.9 0.0 copy-start.4
  18.9 3.3 %shard_map.84 = (bf16[256,1024]{1,0:T(8,128)(2,1)S(1)}, f32[256,512]{1,0:T(8,128)S(1)}, f32[128,512]{1,0:T(8,128)}) custom-call(f32[2]{0:T(128)S(1)} %add_convert_fusion.ends, bf16[256,512]{1,0:T(8,128)(2,1)S(1)} %collective-permute-done.before, bf16[256,512]{1,0:T(8,128)(2,1)S(1)} %bitcast.32, bf16[256,512]{1,0:T(8,128)(2,1)S(1)} %collective-permute-done.1.after, ...), custom_call_target="tpu_custom_call" | custom-call | tf_op jit(solution)/shard_map/pallas_call | solution.py:233
  22.2 8.0 %all-to-all-start = ((f32[8,16,512]{2,1,0:T(8,128)}), f32[8,16,512]{2,1,0:T(8,128)S(1)}, u32[]{:S(2)}, u32[]{:S(2)}) async-start(f32[8,16,512]{2,1,0:T(8,128)} %bitcast.6), calls=%async_computation | async-start | bytes 524288 | tf_op jit(solution)/shard_map/all_to_all | solution.py:219
  30.2 0.0 copy-done.3
  30.2 0.1 pad.12
  30.4 0.0 copy-done.4
  30.4 10.0 %all-to-all-done.refs_1_ = f32[8,16,512]{2,1,0:T(8,128)S(1)} async-done(((f32[8,16,512]{2,1,0:T(8,128)}), f32[8,16,512]{2,1,0:T(8,128)S(1)}, u32[]{:S(2)}, u32[]{:S(2)}) %all-to-all-start) | async-done | bytes 262176 | tf_op jit(solution)/shard_map/all_to_all | solution.py:219
  40.4 1.1 shard_map.85
  41.5 3.4 %all-to-all-start.1 = ((bf16[8,16,512]{2,1,0:T(8,128)(2,1)}), bf16[8,16,512]{2,1,0:T(8,128)(2,1)S(1)}, u32[]{:S(2)}, u32[]{:S(2)}) async-start(bf16[8,16,512]{2,1,0:T(8,128)(2,1)} %get-tuple-element.14), calls=%async_computation.1 | async-start | bytes 262144 | tf_op jit(solution)/shard_map/all_to_all | solution.py:219
  44.9 0.0 copy-done.1
  44.9 1.1 reshape.86
  45.9 8.3 %all-to-all-done.1 = bf16[8,16,512]{2,1,0:T(8,128)(2,1)S(1)} async-done(((bf16[8,16,512]{2,1,0:T(8,128)(2,1)}), bf16[8,16,512]{2,1,0:T(8,128)(2,1)S(1)}, u32[]{:S(2)}, u32[]{:S(2)}) %all-to-all-start.1) | async-done | bytes 131104 | tf_op jit(solution)/shard_map/all_to_all | solution.py:219
  54.2 6.9 %collective-permute-start.2 = (bf16[112,256]{1,0:T(8,128)(2,1)S(1)}, bf16[112,256]{1,0:T(8,128)(2,1)S(1)}, u32[]{:S(2)}, u32[]{:S(2)}) collective-permute-start(bf16[112,256]{1,0:T(8,128)(2,1)S(1)} %get-tuple-element.21), channel_id=1, source_target_pairs={{0,1},{1,2},{2,3},{3,4},{4,5},{5,6},{6,7},{7,8},{8,9},{9,10},{10,1... | collective-permute-start | bytes 172040 | tf_op jit(solution)/shard_map/ppermute | solution.py:261
  61.1 1.9 %collective-permute-start.3 = (bf16[112,256]{1,0:T(8,128)(2,1)S(1)}, bf16[112,256]{1,0:T(8,128)(2,1)S(1)}, u32[]{:S(2)}, u32[]{:S(2)}) collective-permute-start(bf16[112,256]{1,0:T(8,128)(2,1)S(1)} %get-tuple-element.20), channel_id=1, source_target_pairs={{1,0},{2,1},{3,2},{4,3},{5,4},{6,5},{7,6},{8,7},{9,8},{10,9},{11,1... | collective-permute-start | bytes 172040 | tf_op jit(solution)/shard_map/ppermute | solution.py:262
  63.0 1.4 pad_bitcast_fusion
  64.4 0.9 copy.10
  65.3 1.4 copy.11.w_back
  66.6 0.0 collective-permute-done.2.err_before
  66.6 0.2 collective-permute-done.3.err_after
  66.8 2.7 %shard_map.86 = bf16[7168,128]{1,0:T(8,128)(2,1)S(1)} custom-call(f32[1,1]{1,0:T(1,128)} %get-tuple-element.13.loss, bf16[128,512]{1,0:T(8,128)(2,1)S(1)} %bitcast.35, bf16[112,256]{1,0:T(8,128)(2,1)S(1)} %collective-permute-done.2.err_before, bf16[112,256]{1,0:T(8,128)(2,1)S(1)} %collective-permute-done.3.err_after, bf16[3,256,336]{2,1,0:T(8,128)(2,1)S(1)} %copy.11.w_back, ...), custom_call_target="tpu_custom_call" | custom-call | tf_op jit(solution)/shard_map/pallas_call | solution.py:266
  69.5 4.8 %all_to_all.45.refs_1_ = bf16[2,3584,128]{2,1,0:T(8,128)(2,1)S(1)} all-to-all(bf16[2,3584,128]{2,1,0:T(8,128)(2,1)S(1)} %bitcast.28), channel_id=1, replica_groups=mesh['x'=4,'yh'=2,'z'=8,'yl'=4,'c'=2] {'c'}, dimensions={0} | all-to-all | bytes 3670016 | tf_op jit(solution)/shard_map/all_to_all | solution.py:219
  74.3 1.1 shard_map.87
  75.4 3.5 %all-to-all-start.3 = ((bf16[4,896,128]{2,1,0:T(8,128)(2,1)}), bf16[4,896,128]{2,1,0:T(8,128)(2,1)S(1)}, u32[]{:S(2)}, u32[]{:S(2)}) async-start(bf16[4,896,128]{2,1,0:T(8,128)(2,1)} %bitcast.12), calls=%async_computation.3 | async-start | bytes 1835008 | tf_op jit(solution)/shard_map/all_to_all | solution.py:219
  79.0 13.4 %all-to-all-done.3.refs_1_ = bf16[4,896,128]{2,1,0:T(8,128)(2,1)S(1)} async-done(((bf16[4,896,128]{2,1,0:T(8,128)(2,1)}), bf16[4,896,128]{2,1,0:T(8,128)(2,1)S(1)}, u32[]{:S(2)}, u32[]{:S(2)}) %all-to-all-start.3) | async-done | bytes 917536 | tf_op jit(solution)/shard_map/all_to_all | solution.py:219
  92.4 0.8 shard_map.88
  93.2 7.3 %all-to-all-start.4 = ((bf16[8,112,128]{2,1,0:T(8,128)(2,1)}), bf16[8,112,128]{2,1,0:T(8,128)(2,1)S(1)}, u32[]{:S(2)}, u32[]{:S(2)}) async-start(bf16[8,112,128]{2,1,0:T(8,128)(2,1)} %bitcast.13), calls=%async_computation.4 | async-start | bytes 458752 | tf_op jit(solution)/shard_map/all_to_all | solution.py:219
  100.5 9.2 %all-to-all-done.4.refs_1_ = bf16[8,112,128]{2,1,0:T(8,128)(2,1)S(1)} async-done(((bf16[8,112,128]{2,1,0:T(8,128)(2,1)}), bf16[8,112,128]{2,1,0:T(8,128)(2,1)S(1)}, u32[]{:S(2)}, u32[]{:S(2)}) %all-to-all-start.4) | async-done | bytes 229408 | tf_op jit(solution)/shard_map/all_to_all | solution.py:219
  109.8 19.4 %all_to_all.46.refs_1_ = bf16[8,112,128]{2,1,0:T(8,128)(2,1)S(1)} all-to-all(bf16[8,112,128]{2,1,0:T(8,128)(2,1)S(1)} %shard_map.89), channel_id=1, replica_groups=mesh['x'=4,'yh'=2,'z'=8,'yl'=4,'c'=2] {'z'}, dimensions={0} | all-to-all | bytes 458752 | tf_op jit(solution)/shard_map/all_to_all | solution.py:219
  129.2 11.6 %all_to_all.47 = bf16[8,112,128]{2,1,0:T(8,128)(2,1)S(1)} all-to-all(bf16[8,112,128]{2,1,0:T(8,128)(2,1)S(1)} %shard_map.90), channel_id=1, replica_groups=mesh['x'=4,'yh'=2,'z'=8,'yl'=4,'c'=2] {'yh','yl'}, dimensions={0} | all-to-all | bytes 458752 | tf_op jit(solution)/shard_map/all_to_all | solution.py:219
  140.8 1.0 broadcast_in_dim.15
  141.8 3.5 %all-to-all-start.7 = ((bf16[4,896,128]{2,1,0:T(8,128)(2,1)}), bf16[4,896,128]{2,1,0:T(8,128)(2,1)S(1)}, u32[]{:S(2)}, u32[]{:S(2)}) async-start(bf16[4,896,128]{2,1,0:T(8,128)(2,1)} %broadcast_in_dim.15), calls=%async_computation.7 | async-start | bytes 1835008 | tf_op jit(solution)/shard_map/all_to_all | solution.py:219
  145.3 0.9 slice.9
  146.3 0.8 reshape.73
  147.1 7.2 %all-to-all-done.7 = bf16[4,896,128]{2,1,0:T(8,128)(2,1)S(1)} async-done(((bf16[4,896,128]{2,1,0:T(8,128)(2,1)}), bf16[4,896,128]{2,1,0:T(8,128)(2,1)S(1)}, u32[]{:S(2)}, u32[]{:S(2)}) %all-to-all-start.7) | async-done | bytes 917536 | tf_op jit(solution)/shard_map/all_to_all | solution.py:219
  154.3 0.1 broadcast_in_dim.17
  154.5 11.0 %all_to_all.48 = bf16[2,3584,128]{2,1,0:T(8,128)(2,1)S(1)} all-to-all(bf16[2,3584,128]{2,1,0:T(8,128)(2,1)S(1)} %broadcast_in_dim.17), channel_id=1, replica_groups=mesh['x'=4,'yh'=2,'z'=8,'yl'=4,'c'=2] {'c'}, dimensions={0} | all-to-all | bytes 3670016 | tf_op jit(solution)/shard_map/all_to_all | solution.py:219
  165.5 1.5 shard_map.91
  (7 shorter events, 0.1 us)
Async XLA Ops:
  0.6 29.6 %copy-start.3 = (f32[100,2,256]{2,1,0:T(2,128)S(1)}, f32[100,2,256]{2,1,0:T(2,128)}, u32[]{:S(2)}) copy-start(f32[100,2,256]{2,1,0:T(2,128)} %param.8) | copy-start | bytes 614404
  1.7 10.2 %collective-permute-start = (bf16[256,512]{1,0:T(8,128)(2,1)S(1)}, bf16[256,512]{1,0:T(8,128)(2,1)S(1)}, u32[]{:S(2)}, u32[]{:S(2)}) collective-permute-start(bf16[256,512]{1,0:T(8,128)(2,1)S(1)} %bitcast.30), channel_id=1, source_target_pairs={{0,1},{1,2},{2,3},{3,4},{4,5},{5,6},{6,7},{7,8},{8,9},{9,10},{10,1... | collective-permute-start | bytes 786440 | tf_op jit(solution)/shard_map/ppermute | solution.py:230
  6.3 10.3 %collective-permute-start.1 = (bf16[256,512]{1,0:T(8,128)(2,1)S(1)}, bf16[256,512]{1,0:T(8,128)(2,1)S(1)}, u32[]{:S(2)}, u32[]{:S(2)}) collective-permute-start(bf16[256,512]{1,0:T(8,128)(2,1)S(1)} %bitcast.31), channel_id=1, source_target_pairs={{1,0},{2,1},{3,2},{4,3},{5,4},{6,5},{7,6},{8,7},{9,8},{10,9},{11,1... | collective-permute-start | bytes 786440 | tf_op jit(solution)/shard_map/ppermute | solution.py:231
  16.6 1.0 copy-start
  17.6 1.3 copy-start.2
  18.9 11.5 %copy-start.4 = (s32[2,256]{1,0:T(2,128)S(1)}, s32[2,256]{1,0:T(2,128)}, u32[]{:S(2)}) copy-start(s32[2,256]{1,0:T(2,128)} %param.9) | copy-start | bytes 6148
  22.2 22.7 %copy-start.1 = (bf16[100,2304]{1,0:T(8,128)(2,1)S(1)}, bf16[100,2304]{1,0:T(8,128)(2,1)}, u32[]{:S(2)}) copy-start(bf16[100,2304]{1,0:T(8,128)(2,1)} %w2.1) | copy-start | bytes 1382404
  22.2 18.2 %all-to-all-start = ((f32[8,16,512]{2,1,0:T(8,128)}), f32[8,16,512]{2,1,0:T(8,128)S(1)}, u32[]{:S(2)}, u32[]{:S(2)}) async-start(f32[8,16,512]{2,1,0:T(8,128)} %bitcast.6), calls=%async_computation | async-start | bytes 524288 | tf_op jit(solution)/shard_map/all_to_all | solution.py:219
  41.5 12.8 %all-to-all-start.1 = ((bf16[8,16,512]{2,1,0:T(8,128)(2,1)}), bf16[8,16,512]{2,1,0:T(8,128)(2,1)S(1)}, u32[]{:S(2)}, u32[]{:S(2)}) async-start(bf16[8,16,512]{2,1,0:T(8,128)(2,1)} %get-tuple-element.14), calls=%async_computation.1 | async-start | bytes 262144 | tf_op jit(solution)/shard_map/all_to_all | solution.py:219
  54.2 12.4 %collective-permute-start.2 = (bf16[112,256]{1,0:T(8,128)(2,1)S(1)}, bf16[112,256]{1,0:T(8,128)(2,1)S(1)}, u32[]{:S(2)}, u32[]{:S(2)}) collective-permute-start(bf16[112,256]{1,0:T(8,128)(2,1)S(1)} %get-tuple-element.21), channel_id=1, source_target_pairs={{0,1},{1,2},{2,3},{3,4},{4,5},{5,6},{6,7},{7,8},{8,9},{9,10},{10,1... | collective-permute-start | bytes 172040 | tf_op jit(solution)/shard_map/ppermute | solution.py:261
  61.1 5.7 %collective-permute-start.3 = (bf16[112,256]{1,0:T(8,128)(2,1)S(1)}, bf16[112,256]{1,0:T(8,128)(2,1)S(1)}, u32[]{:S(2)}, u32[]{:S(2)}) collective-permute-start(bf16[112,256]{1,0:T(8,128)(2,1)S(1)} %get-tuple-element.20), channel_id=1, source_target_pairs={{1,0},{2,1},{3,2},{4,3},{5,4},{6,5},{7,6},{8,7},{9,8},{10,9},{11,1... | collective-permute-start | bytes 172040 | tf_op jit(solution)/shard_map/ppermute | solution.py:262
  75.4 16.9 %all-to-all-start.3 = ((bf16[4,896,128]{2,1,0:T(8,128)(2,1)}), bf16[4,896,128]{2,1,0:T(8,128)(2,1)S(1)}, u32[]{:S(2)}, u32[]{:S(2)}) async-start(bf16[4,896,128]{2,1,0:T(8,128)(2,1)} %bitcast.12), calls=%async_computation.3 | async-start | bytes 1835008 | tf_op jit(solution)/shard_map/all_to_all | solution.py:219
  93.2 16.6 %all-to-all-start.4 = ((bf16[8,112,128]{2,1,0:T(8,128)(2,1)}), bf16[8,112,128]{2,1,0:T(8,128)(2,1)S(1)}, u32[]{:S(2)}, u32[]{:S(2)}) async-start(bf16[8,112,128]{2,1,0:T(8,128)(2,1)} %bitcast.13), calls=%async_computation.4 | async-start | bytes 458752 | tf_op jit(solution)/shard_map/all_to_all | solution.py:219
  141.8 12.5 %all-to-all-start.7 = ((bf16[4,896,128]{2,1,0:T(8,128)(2,1)}), bf16[4,896,128]{2,1,0:T(8,128)(2,1)S(1)}, u32[]{:S(2)}, u32[]{:S(2)}) async-start(bf16[4,896,128]{2,1,0:T(8,128)(2,1)} %broadcast_in_dim.15), calls=%async_computation.7 | async-start | bytes 1835008 | tf_op jit(solution)/shard_map/all_to_all | solution.py:219

commit v3 on v2

--- a/solution.py
+++ b/solution.py
@@ -32,7 +32,8 @@
 TILES = TAPS * C // LANES
 SECOND = TILES * C
 LOSS = SECOND + TILES * VPAD
-FLAT = 7168
+FLAT = 6656
+HALF = FLAT // 2
 VMEM = pl.BlockSpec(memory_space=pltpu.VMEM)
 SMEM = pl.BlockSpec(memory_space=pltpu.SMEM)
 PARAMS = pltpu.CompilerParams(vmem_limit_bytes=40 * 1024 * 1024)
@@ -52,7 +53,19 @@
     return high, (total - high.astype(F32)).astype(BF16)
 
 
-def forward_kernel(ends, before, local, after, w1, w2, hidden, slope, outlook, stack):
+def prepare_kernel(w1, w2, w1_out, w2_out, w_back):
+    w1_out[...] = w1[...]
+    w2_out[...] = w2[...]
+    spare = jnp.zeros((C, VPAD - V), F32)
+    for a in range(3):
+        turned = []
+        for b in range(3):
+            tap = w2[:, (3 * a + b) * C : (3 * a + b + 1) * C].astype(F32)
+            turned += [tap.T, spare]
+        w_back[a] = jnp.concatenate(turned, axis=1).astype(BF16)
+
+
+def forward_kernel(ends, before, local, after, w1, w2, hidden, slope, outlook, sent, stack):
     rows = [r[:, i * LON : (i + 1) * LON] for r in (before, local, after) for i in range(2)]
     wide = ROWS + 2
     for a in range(3):
@@ -81,7 +94,9 @@
             slope[:, own] = half + (0.5 * GELU_A) * pre * (1.0 - t * t) * (
                 1.0 + 3.0 * GELU_B * square
             )
-    outlook[V:, :] = jnp.zeros((MEMBERS * SHARE - V, CELLS), F32)
+    top = V // 16 * 16
+    sent[top:, :] = jnp.zeros((MEMBERS * SHARE - top, CELLS), BF16)
+    spare = jnp.zeros((VPAD - V, LON), F32)
     for i in range(ROWS):
         total = None
         for b in range(3):
@@ -92,12 +107,14 @@
                 part = term if part is None else part + term
             part = turn(part, 1 - b)
             total = part if total is None else total + part
-        outlook[:V, i * LON : (i + 1) * LON] = total
+        lanes = slice(i * LON, (i + 1) * LON)
+        outlook[:, lanes] = total
+        sent[:VPAD, lanes] = jnp.concatenate([total, spare], axis=0).astype(BF16)
 
 
 def score_kernel(points, me, every, obs, land, errors, loss):
     area = 1.0 + LAND_WEIGHT * land[...].astype(F32)
-    x = [every[p] for p in range(MEMBERS)]
+    x = [every[p].astype(F32) for p in range(MEMBERS)]
     truth = obs[me[0]]
     count = MEMBERS * (MEMBERS - 1)
     skill = pairs = jnp.zeros((SHARE, CELLS), F32)
@@ -182,16 +199,18 @@
     value = total.astype(BF16)
     for i in range(copies):
         out[i] = value
+    base = row // 16 * 16 if row + 16 <= total.shape[0] and row % 16 == 0 else 0
+    span = 16 if row % 16 == 0 else total.shape[0]
 
     @pl.when(holder[0] == 1)
     def _():
-        here = total[row : row + 16]
-        loss = here[0:1] + here[1:2]
-        high, low = split(loss)
-        index = lax.broadcasted_iota(jnp.int32, (16, LANES), 0)
-        fixed = jnp.where(index == 0, high.astype(F32), jnp.where(index == 1, low.astype(F32), 0.0))
+        here = total[base : base + span]
+        high, low = split(total[row : row + 1] + total[row + 1 : row + 2])
+        index = lax.broadcasted_iota(jnp.int32, (span, LANES), 0) + base
+        fixed = jnp.where(index == row, high.astype(F32), here)
+        fixed = jnp.where(index == row + 1, low.astype(F32), fixed)
         for i in range(copies):
-            out[i, row : row + 16, :] = fixed.astype(BF16)
+            out[i, base : base + span, :] = fixed.astype(BF16)
 
 
 def summed(parts, row, holder, copies=1):
@@ -205,14 +224,20 @@
     )(holder, parts)
 
 
-def last_kernel(halves, first, second, loss):
-    flat = lambda at, n: halves[at : at + n, :]
-    for tile in range(TILES):
-        lanes = slice(tile * LANES, (tile + 1) * LANES)
-        first[:, lanes] = flat(tile * C, C)
-        second[:, lanes] = flat(SECOND + tile * VPAD, VPAD)[:V]
-    here = flat(LOSS, 16).astype(F32)
-    loss[...] = here[0:1, 0:1] + here[1:2, 0:1]
+def last_kernel(core, own, other, first, second, loss):
+    def assemble(low, high):
+        def flat(at, n):
+            return low[at : at + n, :] if at < HALF else high[at - HALF : at - HALF + n, :]
+
+        for tile in range(TILES):
+            lanes = slice(tile * LANES, (tile + 1) * LANES)
+            first[:, lanes] = flat(tile * C, C)
+            second[:, lanes] = flat(SECOND + tile * VPAD, VPAD)[:V]
+        here = flat(LOSS, 16).astype(F32)
+        loss[...] = here[0:1, 0:1] + here[1:2, 0:1]
+
+    pl.when(core[0] == 0)(lambda: assemble(own, other))
+    pl.when(core[0] == 1)(lambda: assemble(other, own))
 
 
 def exchange(array, axes):
@@ -229,21 +254,33 @@
     local = features.reshape(C, CELLS)
     before = lax.ppermute(local, DOM, up)
     after = lax.ppermute(local, DOM, down)
+    w1, w2, w_back = pl.pallas_call(
+        prepare_kernel,
+        out_shape=(
+            jax.ShapeDtypeStruct((C, TAPS * C), BF16),
+            jax.ShapeDtypeStruct((V, TAPS * C), BF16),
+            jax.ShapeDtypeStruct((3, C, 3 * VPAD), BF16),
+        ),
+        in_specs=[VMEM] * 2,
+        out_specs=(VMEM,) * 3,
+        compiler_params=PARAMS,
+    )(w_first, later_kernel_matrix)
     ends = jnp.stack([(dom > 0).astype(F32), (dom < dom_size - 1).astype(F32)])
-    hidden, slope, outlook = pl.pallas_call(
+    hidden, slope, outlook, sent = pl.pallas_call(
         forward_kernel,
         out_shape=(
             jax.ShapeDtypeStruct((C, 4 * LON), BF16),
             jax.ShapeDtypeStruct((C, CELLS), F32),
-            jax.ShapeDtypeStruct((MEMBERS * SHARE, CELLS), F32),
+            jax.ShapeDtypeStruct((V, CELLS), F32),
+            jax.ShapeDtypeStruct((MEMBERS * SHARE, CELLS), BF16),
         ),
         in_specs=[SMEM] + [VMEM] * 5,
-        out_specs=(VMEM,) * 3,
+        out_specs=(VMEM,) * 4,
         scratch_shapes=[pltpu.VMEM((3 * C, 4 * LON), BF16)],
         compiler_params=PARAMS,
-    )(ends, before, local, after, w_first, later_kernel_matrix)
-
-    every = exchange(outlook.reshape(MEMBERS, SHARE, CELLS), ENS)
+    )(ends, before, local, after, w1, w2)
+
+    every = exchange(sent.reshape(MEMBERS, SHARE, CELLS), ENS)
     obs = jnp.pad(observed_state.reshape(V, CELLS), ((0, MEMBERS * SHARE - V), (0, 0)))
     me = lax.axis_index(ENS).reshape(1)
     errors, loss = pl.pallas_call(
@@ -260,9 +297,6 @@
 
     err_before = lax.ppermute(errors[:VPAD, LON:], DOM, up)
     err_after = lax.ppermute(errors[:VPAD, :LON], DOM, down)
-    w_back = later_kernel_matrix.reshape(V, 3, 3, C)
-    w_back = jnp.pad(w_back, ((0, VPAD - V), (0, 0), (0, 0), (0, 0)))
-    w_back = w_back.transpose(1, 3, 2, 0).reshape(3, C, 3 * VPAD)
     flat = pl.pallas_call(
         backward_kernel,
         out_shape=jax.ShapeDtypeStruct((FLAT, LANES), BF16),
@@ -287,9 +321,10 @@
         flag = holder.astype(jnp.int32).reshape(1)
         part = summed(part, row, flag, 8 if axes == Y else 1)
     part = summed(exchange(part, "z"), row, flag, 8)
-    part = exchange(part, Y).reshape(1, 8 * size, LANES)
-    part = exchange(jnp.broadcast_to(part, (4, 8 * size, LANES)), "x").reshape(1, 32 * size, LANES)
-    part = exchange(jnp.broadcast_to(part, (2, 32 * size, LANES)), "c").reshape(FLAT, LANES)
+    part = exchange(part, Y).reshape(8 * size, LANES)
+    part = lax.all_gather(part, "x", axis=0, tiled=True)
+    other = lax.ppermute(part, "c", [(0, 1), (1, 0)])
+    core = lax.axis_index("c").reshape(1)
     first, second, loss = pl.pallas_call(
         last_kernel,
         out_shape=(
@@ -297,11 +332,11 @@
             jax.ShapeDtypeStruct((V, TAPS * C), BF16),
             jax.ShapeDtypeStruct((1, 1), F32),
         ),
-        in_specs=[VMEM],
+        in_specs=[SMEM, VMEM, VMEM],
         out_specs=(VMEM,) * 3,
         compiler_params=PARAMS,
-    )(part)
-    return outlook[:V].reshape(1, V, ROWS, LON), first, second, loss.reshape(())
+    )(core, part, other)
+    return outlook.reshape(1, V, ROWS, LON), first, second, loss.reshape(())
 
 
 def solution(mesh):

time: 168 us -> 160 us (0.952)
  waiting for transfers between devices: 53.1 us -> 37.7 us
  blocking collectives: 46.8 us -> 58.7 us
  local copies, waits for them, and re-layouts: 11 us -> 4.21 us
  starting transfers between devices: 44.6 us -> 46.7 us
    all_to_all x5 -> x3, waiting for transfers between devices: 48.2 us -> 30.6 us  [exchange(): return lax.all_to_all(array, axes, 0, 0, tiled=True)]
    all_gather x0 -> x1, blocking collectives: none -> 11.9 us  [body(): part = lax.all_gather(part, 'x', axis=0, tiled=True)]
    ppermute x0 -> x1, starting transfers between devices: none -> 9.58 us  [body(): other = lax.ppermute(part, 'c', [(0, 1), (1, 0)])]
    all_to_all x5 -> x3, starting transfers between devices: 25.7 us -> 19.4 us  [exchange(): return lax.all_to_all(array, axes, 0, 0, tiled=True)]
    ppermute x1, waiting for transfers between devices: 0.16 us -> 3.91 us  [body(): err_after = lax.ppermute(errors[:VPAD, :LON], DOM, down)]
    ppermute x1, waiting for transfers between devices: 4.72 us -> 1.98 us  [body(): after = lax.ppermute(local, DOM, down)]
    reshape x3 -> x1, local copies, waits for them, and re-layouts: 3.22 us -> 0.81 us  [body(): return (outlook.reshape(1, V, ROWS, LON), first, second, loss.reshape(()))]
    transpose x2 -> x0, local copies, waits for them, and re-layouts: 2.22 us -> none  [body(): w_back = w_back.transpose(1, 3, 2, 0).reshape(3, C, 3 * VPAD)]
  transfers between devices with their start and end apart: 9 -> 8, of which waited for: 7 -> 6; matrix products, arithmetic and copies ran while one was open for 4% -> 1% of each run, Pallas kernels for 0% -> 0%
where the time goes in v3:
time: 160 us; the launch traced here: 159 us
  blocking collectives  58.7 us (37%)
  starting transfers between devices  46.7 us (29%)
  waiting for transfers between devices  37.7 us (24%)
  Pallas kernels  10.9 us (7%)
  local copies, waits for them, and re-layouts  4.21 us (3%)
    all_to_all x4, blocking collectives, exchange(): return lax.all_to_all(array, axes, 0, 0, tiled=True)  46.9 us
    all_to_all x3, waiting for transfers between devices, exchange(): return lax.all_to_all(array, axes, 0, 0, tiled=True)  30.6 us
    all_to_all x3, starting transfers between devices, exchange(): return lax.all_to_all(array, axes, 0, 0, tiled=True)  19.4 us
    all_gather x1, blocking collectives, body(): part = lax.all_gather(part, 'x', axis=0, tiled=True)  11.9 us
    ppermute x1, starting transfers between devices, body(): other = lax.ppermute(part, 'c', [(0, 1), (1, 0)])  9.58 us
    ppermute x1, starting transfers between devices, body(): err_before = lax.ppermute(errors[:VPAD, LON:], DOM, up)  5.77 us
    ppermute x1, starting transfers between devices, body(): after = lax.ppermute(local, DOM, down)  5.5 us
    ppermute x1, starting transfers between devices, body(): before = lax.ppermute(local, DOM, up)  4.59 us
  transfers between devices with their start and end apart: 8, of which 6 were waited for; matrix products, arithmetic and copies ran while one was open for 1% of the time, Pallas kernels for 0%

profile of v3, /device:TPU:1, one launch (start us, length us, event | category | flops | bytes accessed | tf_op | source)
XLA Modules:
  0.0 159.1 jit_solution(16191670918744677223)
XLA Ops:
  0.6 1.0 copy.9
  1.6 4.6 %collective-permute-start = (bf16[256,512]{1,0:T(8,128)(2,1)S(1)}, bf16[256,512]{1,0:T(8,128)(2,1)S(1)}, u32[]{:S(2)}, u32[]{:S(2)}) collective-permute-start(bf16[256,512]{1,0:T(8,128)(2,1)S(1)} %bitcast.25), channel_id=1, source_target_pairs={{0,1},{1,2},{2,3},{3,4},{4,5},{5,6},{6,7},{7,8},{8,9},{9,10},{10,1... | collective-permute-start | bytes 786440 | tf_op jit(solution)/shard_map/ppermute | solution.py:255
  6.2 5.5 %collective-permute-start.1 = (bf16[256,512]{1,0:T(8,128)(2,1)S(1)}, bf16[256,512]{1,0:T(8,128)(2,1)S(1)}, u32[]{:S(2)}, u32[]{:S(2)}) collective-permute-start(bf16[256,512]{1,0:T(8,128)(2,1)S(1)} %bitcast.26), channel_id=1, source_target_pairs={{1,0},{2,1},{3,2},{4,3},{5,4},{6,5},{7,6},{8,7},{9,8},{10,9},{11,1... | collective-permute-start | bytes 786440 | tf_op jit(solution)/shard_map/ppermute | solution.py:256
  11.7 0.0 copy-start
  11.7 1.3 copy-done
  13.0 0.0 copy-start.1
  13.0 1.0 copy-done.1
  14.0 0.4 shard_map.84
  14.5 0.1 add_convert_fusion.ends
  14.6 0.0 collective-permute-done.before
  14.6 2.0 %collective-permute-done.1.after = bf16[256,512]{1,0:T(8,128)(2,1)S(1)} collective-permute-done((bf16[256,512]{1,0:T(8,128)(2,1)S(1)}, bf16[256,512]{1,0:T(8,128)(2,1)S(1)}, u32[]{:S(2)}, u32[]{:S(2)}) %collective-permute-start.1) | collective-permute-done | bytes 262176 | tf_op jit(solution)/shard_map/ppermute | solution.py:256
  16.5 0.0 copy-start.2
  16.5 3.3 %shard_map.85 = (bf16[256,1024]{1,0:T(8,128)(2,1)S(1)}, f32[256,512]{1,0:T(8,128)S(1)}, f32[100,512]{1,0:T(8,128)S(1)}, bf16[128,512]{1,0:T(8,128)(2,1)}) custom-call(f32[2]{0:T(128)S(1)} %add_convert_fusion.ends, bf16[256,512]{1,0:T(8,128)(2,1)S(1)} %collective-permute-done.before, bf16[256,512]{1,0:T(8,128)(2,1)S(1)} %bitcast.27, ...), custom_call_target="tpu_custom_call" | custom-call | tf_op jit(solution)/shard_map/pallas_call | solution.py:269
  19.8 0.0 copy-start.3
  19.8 8.0 %all-to-all-start = ((bf16[8,16,512]{2,1,0:T(8,128)(2,1)}), bf16[8,16,512]{2,1,0:T(8,128)(2,1)S(1)}, u32[]{:S(2)}, u32[]{:S(2)}) async-start(bf16[8,16,512]{2,1,0:T(8,128)(2,1)} %bitcast.7), calls=%async_computation | async-start | bytes 262144 | tf_op jit(solution)/shard_map/all_to_all | solution.py:244
  27.9 0.0 copy-done.2
  27.9 0.1 pad.7
  28.0 0.0 copy-done.3
  28.0 9.4 %all-to-all-done.refs_1_ = bf16[8,16,512]{2,1,0:T(8,128)(2,1)S(1)} async-done(((bf16[8,16,512]{2,1,0:T(8,128)(2,1)}), bf16[8,16,512]{2,1,0:T(8,128)(2,1)S(1)}, u32[]{:S(2)}, u32[]{:S(2)}) %all-to-all-start) | async-done | bytes 131104 | tf_op jit(solution)/shard_map/all_to_all | solution.py:244
  37.4 1.1 shard_map.86
  38.4 11.9 %all_to_all.35 = bf16[8,16,512]{2,1,0:T(8,128)(2,1)S(1)} all-to-all(bf16[8,16,512]{2,1,0:T(8,128)(2,1)S(1)} %get-tuple-element.21), channel_id=1, replica_groups=mesh['x'=4,'yh'=2,'z'=8,'yl'=4,'c'=2] {'x','yh'}, dimensions={0} | all-to-all | bytes 262144 | tf_op jit(solution)/shard_map/all_to_all | solution.py:244
  50.4 5.8 %collective-permute-start.2 = (bf16[112,256]{1,0:T(8,128)(2,1)S(1)}, bf16[112,256]{1,0:T(8,128)(2,1)S(1)}, u32[]{:S(2)}, u32[]{:S(2)}) collective-permute-start(bf16[112,256]{1,0:T(8,128)(2,1)S(1)} %get-tuple-element.29), channel_id=1, source_target_pairs={{0,1},{1,2},{2,3},{3,4},{4,5},{5,6},{6,7},{7,8},{8,9},{9,10},{10,1... | collective-permute-start | bytes 172040 | tf_op jit(solution)/shard_map/ppermute | solution.py:298
  56.2 1.9 %collective-permute-start.3 = (bf16[112,256]{1,0:T(8,128)(2,1)S(1)}, bf16[112,256]{1,0:T(8,128)(2,1)S(1)}, u32[]{:S(2)}, u32[]{:S(2)}) collective-permute-start(bf16[112,256]{1,0:T(8,128)(2,1)S(1)} %get-tuple-element.28), channel_id=1, source_target_pairs={{1,0},{2,1},{3,2},{4,3},{5,4},{6,5},{7,6},{8,7},{9,8},{10,9},{11,1... | collective-permute-start | bytes 172040 | tf_op jit(solution)/shard_map/ppermute | solution.py:299
  58.1 0.0 collective-permute-done.2.err_before
  58.1 3.9 %collective-permute-done.3.err_after = bf16[112,256]{1,0:T(8,128)(2,1)S(1)} collective-permute-done((bf16[112,256]{1,0:T(8,128)(2,1)S(1)}, bf16[112,256]{1,0:T(8,128)(2,1)S(1)}, u32[]{:S(2)}, u32[]{:S(2)}) %collective-permute-start.3) | collective-permute-done | bytes 57376 | tf_op jit(solution)/shard_map/ppermute | solution.py:299
  62.0 2.7 %shard_map.87 = bf16[6656,128]{1,0:T(8,128)(2,1)S(1)} custom-call(f32[1,1]{1,0:T(1,128)} %get-tuple-element.20.loss, bf16[128,512]{1,0:T(8,128)(2,1)S(1)} %bitcast.30, bf16[112,256]{1,0:T(8,128)(2,1)S(1)} %collective-permute-done.2.err_before, bf16[112,256]{1,0:T(8,128)(2,1)S(1)} %collective-permute-done.3.err_after, ...), custom_call_target="tpu_custom_call" | custom-call | tf_op jit(solution)/shard_map/pallas_call | solution.py:300
  64.7 4.7 %all_to_all.36.refs_1_ = bf16[2,3328,128]{2,1,0:T(8,128)(2,1)S(1)} all-to-all(bf16[2,3328,128]{2,1,0:T(8,128)(2,1)S(1)} %bitcast.24), channel_id=1, replica_groups=mesh['x'=4,'yh'=2,'z'=8,'yl'=4,'c'=2] {'c'}, dimensions={0} | all-to-all | bytes 3407872 | tf_op jit(solution)/shard_map/all_to_all | solution.py:244
  69.4 1.1 shard_map.88
  70.5 3.5 %all-to-all-start.3 = ((bf16[4,832,128]{2,1,0:T(8,128)(2,1)}), bf16[4,832,128]{2,1,0:T(8,128)(2,1)S(1)}, u32[]{:S(2)}, u32[]{:S(2)}) async-start(bf16[4,832,128]{2,1,0:T(8,128)(2,1)} %bitcast.11), calls=%async_computation.3 | async-start | bytes 1703936 | tf_op jit(solution)/shard_map/all_to_all | solution.py:244
  74.0 12.7 %all-to-all-done.3.refs_1_ = bf16[4,832,128]{2,1,0:T(8,128)(2,1)S(1)} async-done(((bf16[4,832,128]{2,1,0:T(8,128)(2,1)}), bf16[4,832,128]{2,1,0:T(8,128)(2,1)S(1)}, u32[]{:S(2)}, u32[]{:S(2)}) %all-to-all-start.3) | async-done | bytes 852000 | tf_op jit(solution)/shard_map/all_to_all | solution.py:244
  86.8 0.8 shard_map.89
  87.5 7.8 %all-to-all-start.4 = ((bf16[8,104,128]{2,1,0:T(8,128)(2,1)}), bf16[8,104,128]{2,1,0:T(8,128)(2,1)S(1)}, u32[]{:S(2)}, u32[]{:S(2)}) async-start(bf16[8,104,128]{2,1,0:T(8,128)(2,1)} %bitcast.12), calls=%async_computation.4 | async-start | bytes 425984 | tf_op jit(solution)/shard_map/all_to_all | solution.py:244
  95.4 8.6 %all-to-all-done.4.refs_1_ = bf16[8,104,128]{2,1,0:T(8,128)(2,1)S(1)} async-done(((bf16[8,104,128]{2,1,0:T(8,128)(2,1)}), bf16[8,104,128]{2,1,0:T(8,128)(2,1)S(1)}, u32[]{:S(2)}, u32[]{:S(2)}) %all-to-all-start.4) | async-done | bytes 213024 | tf_op jit(solution)/shard_map/all_to_all | solution.py:244
  104.0 18.7 %all_to_all.37.refs_1_ = bf16[8,104,128]{2,1,0:T(8,128)(2,1)S(1)} all-to-all(bf16[8,104,128]{2,1,0:T(8,128)(2,1)S(1)} %shard_map.90), channel_id=1, replica_groups=mesh['x'=4,'yh'=2,'z'=8,'yl'=4,'c'=2] {'z'}, dimensions={0} | all-to-all | bytes 425984 | tf_op jit(solution)/shard_map/all_to_all | solution.py:244
  122.7 11.5 %all_to_all.38 = bf16[8,104,128]{2,1,0:T(8,128)(2,1)S(1)} all-to-all(bf16[8,104,128]{2,1,0:T(8,128)(2,1)S(1)} %shard_map.91), channel_id=1, replica_groups=mesh['x'=4,'yh'=2,'z'=8,'yl'=4,'c'=2] {'yh','yl'}, dimensions={0} | all-to-all | bytes 425984 | tf_op jit(solution)/shard_map/all_to_all | solution.py:244
  134.2 11.9 %all_gather.3.own = bf16[3328,128]{1,0:T(8,128)(2,1)S(1)} all-gather(bf16[832,128]{1,0:T(8,128)(2,1)S(1)} %bitcast.35), channel_id=1, replica_groups=mesh['x'=4,'yh'=2,'z'=8,'yl'=4,'c'=2] {'x'}, dimensions={0}, use_global_device_ids=true | all-gather | bytes 1064960 | tf_op jit(solution)/shard_map/all_gather | solution.py:325
  146.1 9.6 %collective-permute-start.4 = (bf16[3328,128]{1,0:T(8,128)(2,1)S(1)}, bf16[3328,128]{1,0:T(8,128)(2,1)S(1)}, u32[]{:S(2)}, u32[]{:S(2)}) collective-permute-start(bf16[3328,128]{1,0:T(8,128)(2,1)S(1)} %all_gather.3.own), channel_id=1, source_target_pairs={{0,1},{1,0},{2,3},{3,2},{4,5},{5,4},{6,7},{7,6},{8,9},{9,8},{10,11... | collective-permute-start | bytes 2555912 | tf_op jit(solution)/shard_map/ppermute | solution.py:326
  155.7 0.8 reshape.66
  156.5 1.2 collective-permute-done.4.other
  157.7 1.5 shard_map.92
  (6 shorter events, 0.1 us)
Async XLA Ops:
  1.6 12.9 %collective-permute-start = (bf16[256,512]{1,0:T(8,128)(2,1)S(1)}, bf16[256,512]{1,0:T(8,128)(2,1)S(1)}, u32[]{:S(2)}, u32[]{:S(2)}) collective-permute-start(bf16[256,512]{1,0:T(8,128)(2,1)S(1)} %bitcast.25), channel_id=1, source_target_pairs={{0,1},{1,2},{2,3},{3,4},{4,5},{5,6},{6,7},{7,8},{8,9},{9,10},{10,1... | collective-permute-start | bytes 786440 | tf_op jit(solution)/shard_map/ppermute | solution.py:255
  6.2 10.3 %collective-permute-start.1 = (bf16[256,512]{1,0:T(8,128)(2,1)S(1)}, bf16[256,512]{1,0:T(8,128)(2,1)S(1)}, u32[]{:S(2)}, u32[]{:S(2)}) collective-permute-start(bf16[256,512]{1,0:T(8,128)(2,1)S(1)} %bitcast.26), channel_id=1, source_target_pairs={{1,0},{2,1},{3,2},{4,3},{5,4},{6,5},{7,6},{8,7},{9,8},{10,9},{11,1... | collective-permute-start | bytes 786440 | tf_op jit(solution)/shard_map/ppermute | solution.py:256
  11.7 1.3 copy-start
  13.0 1.0 copy-start.1
  16.5 11.3 %copy-start.2 = (f32[100,2,256]{2,1,0:T(2,128)S(1)}, f32[100,2,256]{2,1,0:T(2,128)}, u32[]{:S(2)}) copy-start(f32[100,2,256]{2,1,0:T(2,128)} %param.8) | copy-start | bytes 614404
  19.8 8.2 %copy-start.3 = (s32[2,256]{1,0:T(2,128)S(1)}, s32[2,256]{1,0:T(2,128)}, u32[]{:S(2)}) copy-start(s32[2,256]{1,0:T(2,128)} %param.9) | copy-start | bytes 6148
  19.8 17.6 %all-to-all-start = ((bf16[8,16,512]{2,1,0:T(8,128)(2,1)}), bf16[8,16,512]{2,1,0:T(8,128)(2,1)S(1)}, u32[]{:S(2)}, u32[]{:S(2)}) async-start(bf16[8,16,512]{2,1,0:T(8,128)(2,1)} %bitcast.7), calls=%async_computation | async-start | bytes 262144 | tf_op jit(solution)/shard_map/all_to_all | solution.py:244
  50.4 7.7 %collective-permute-start.2 = (bf16[112,256]{1,0:T(8,128)(2,1)S(1)}, bf16[112,256]{1,0:T(8,128)(2,1)S(1)}, u32[]{:S(2)}, u32[]{:S(2)}) collective-permute-start(bf16[112,256]{1,0:T(8,128)(2,1)S(1)} %get-tuple-element.29), channel_id=1, source_target_pairs={{0,1},{1,2},{2,3},{3,4},{4,5},{5,6},{6,7},{7,8},{8,9},{9,10},{10,1... | collective-permute-start | bytes 172040 | tf_op jit(solution)/shard_map/ppermute | solution.py:298
  56.2 5.9 %collective-permute-start.3 = (bf16[112,256]{1,0:T(8,128)(2,1)S(1)}, bf16[112,256]{1,0:T(8,128)(2,1)S(1)}, u32[]{:S(2)}, u32[]{:S(2)}) collective-permute-start(bf16[112,256]{1,0:T(8,128)(2,1)S(1)} %get-tuple-element.28), channel_id=1, source_target_pairs={{1,0},{2,1},{3,2},{4,3},{5,4},{6,5},{7,6},{8,7},{9,8},{10,9},{11,1... | collective-permute-start | bytes 172040 | tf_op jit(solution)/shard_map/ppermute | solution.py:299
  70.5 16.2 %all-to-all-start.3 = ((bf16[4,832,128]{2,1,0:T(8,128)(2,1)}), bf16[4,832,128]{2,1,0:T(8,128)(2,1)S(1)}, u32[]{:S(2)}, u32[]{:S(2)}) async-start(bf16[4,832,128]{2,1,0:T(8,128)(2,1)} %bitcast.11), calls=%async_computation.3 | async-start | bytes 1703936 | tf_op jit(solution)/shard_map/all_to_all | solution.py:244
  87.5 16.4 %all-to-all-start.4 = ((bf16[8,104,128]{2,1,0:T(8,128)(2,1)}), bf16[8,104,128]{2,1,0:T(8,128)(2,1)S(1)}, u32[]{:S(2)}, u32[]{:S(2)}) async-start(bf16[8,104,128]{2,1,0:T(8,128)(2,1)} %bitcast.12), calls=%async_computation.4 | async-start | bytes 425984 | tf_op jit(solution)/shard_map/all_to_all | solution.py:244
  146.1 11.6 %collective-permute-start.4 = (bf16[3328,128]{1,0:T(8,128)(2,1)S(1)}, bf16[3328,128]{1,0:T(8,128)(2,1)S(1)}, u32[]{:S(2)}, u32[]{:S(2)}) collective-permute-start(bf16[3328,128]{1,0:T(8,128)(2,1)S(1)} %all_gather.3.own), channel_id=1, source_target_pairs={{0,1},{1,0},{2,3},{3,2},{4,5},{5,4},{6,7},{7,6},{8,9},{9,8},{10,11... | collective-permute-start | bytes 2555912 | tf_op jit(solution)/shard_map/ppermute | solution.py:326

commit v4 on v3

--- a/solution.py
+++ b/solution.py
@@ -48,6 +48,11 @@
     return jnp.dot(a, b, preferred_element_type=F32)
 
 
+def by_side(core, across, beside, use):
+    pl.when(core[0] == 0)(lambda: use(across, beside) and None)
+    pl.when(core[0] == 1)(lambda: use(beside, across) and None)
+
+
 def split(total):
     high = total.astype(BF16)
     return high, (total - high.astype(F32)).astype(BF16)
@@ -65,12 +70,18 @@
         w_back[a] = jnp.concatenate(turned, axis=1).astype(BF16)
 
 
-def forward_kernel(ends, before, local, after, w1, w2, hidden, slope, outlook, sent, stack):
-    rows = [r[:, i * LON : (i + 1) * LON] for r in (before, local, after) for i in range(2)]
+def forward_kernel(core, ends, across, local, beside, w1, w2, hidden, slope, outlook, sent, stack):
     wide = ROWS + 2
-    for a in range(3):
-        for i in range(wide):
-            stack[a * C : (a + 1) * C, i * LON : (i + 1) * LON] = rows[i + a]
+
+    def fill(chosen, ref):
+        for a in range(3):
+            for i in range(wide):
+                if (i + a) // 2 == chosen:
+                    row = ref[:, (i + a) % 2 * LON : ((i + a) % 2 + 1) * LON]
+                    stack[a * C : (a + 1) * C, i * LON : (i + 1) * LON] = row
+
+    fill(1, local)
+    by_side(core, across, beside, lambda before, after: (fill(0, before), fill(2, after)))
     for i in range(wide):
         lanes = slice(i * LON, (i + 1) * LON)
         pre = None
@@ -144,13 +155,22 @@
 
 
 def backward_kernel(
-    loss, err, err_before, err_after, w_back, slope, hidden, before, local, after, out, e, pg
+    core, loss, err, err_across, err_beside, w_back, slope, hidden, across, local, beside, out, e, pg, ends
 ):
-    rows = [err_before[...], err[:VPAD, :LON], err[:VPAD, LON:], err_after[...]]
-    for i in range(4):
-        row = rows[i].astype(F32)
+    def fill(i, row):
+        row = row.astype(F32)
         for b in range(3):
             e[b * VPAD : (b + 1) * VPAD, i * LON : (i + 1) * LON] = turn(row, b - 1).astype(BF16)
+
+    fill(1, err[:VPAD, :LON])
+    fill(2, err[:VPAD, LON:])
+    by_side(core, err_across, err_beside, lambda u, d: (fill(0, u[...]), fill(3, d[...])))
+
+    def fill_ends(before, after):
+        ends[:, :LON] = before[:, LON:]
+        ends[:, LON:] = after[:, :LON]
+
+    by_side(core, across, beside, fill_ends)
     for i in range(ROWS):
         back = None
         for a in range(3):
@@ -163,11 +183,11 @@
             pg[b * C : (b + 1) * C, own] = turn(grad, b - 1).astype(BF16)
     for a in range(3):
         if a == 0:
-            window = jnp.concatenate([before[:, LON:], local[:, :LON]], axis=1)
+            window = jnp.concatenate([ends[:, :LON], local[:, :LON]], axis=1)
         elif a == 1:
             window = local[...]
         else:
-            window = jnp.concatenate([local[:, LON:], after[:, :LON]], axis=1)
+            window = jnp.concatenate([local[:, LON:], ends[:, LON:]], axis=1)
         for b in range(3):
             first = lax.dot_general(
                 pg[b * C : (b + 1) * C, :], window, NT, preferred_element_type=F32
@@ -224,20 +244,14 @@
     )(holder, parts)
 
 
-def last_kernel(core, own, other, first, second, loss):
-    def assemble(low, high):
-        def flat(at, n):
-            return low[at : at + n, :] if at < HALF else high[at - HALF : at - HALF + n, :]
-
-        for tile in range(TILES):
-            lanes = slice(tile * LANES, (tile + 1) * LANES)
-            first[:, lanes] = flat(tile * C, C)
-            second[:, lanes] = flat(SECOND + tile * VPAD, VPAD)[:V]
-        here = flat(LOSS, 16).astype(F32)
-        loss[...] = here[0:1, 0:1] + here[1:2, 0:1]
-
-    pl.when(core[0] == 0)(lambda: assemble(own, other))
-    pl.when(core[0] == 1)(lambda: assemble(other, own))
+def last_kernel(sums, first, second, loss):
+    for tile in range(TILES):
+        lanes = slice(tile * LANES, (tile + 1) * LANES)
+        first[:, lanes] = sums[tile * C : (tile + 1) * C, :]
+        at = SECOND + tile * VPAD
+        second[:, lanes] = sums[at : at + VPAD, :][:V]
+    here = sums[LOSS : LOSS + 16, :].astype(F32)
+    loss[...] = here[0:1, 0:1] + here[1:2, 0:1]
 
 
 def exchange(array, axes):
@@ -247,13 +261,16 @@
 def body(features, w_first, later_kernel_matrix, observed_state, land):
     dom_size = lax.axis_size(DOM)
     dom = lax.axis_index(DOM)
-    up = [(i, i + 1) for i in range(dom_size - 1)]
-    down = [(j, i) for i, j in up]
+    chips = [(i, i + 1) for i in range(1, dom_size - 1, 2)]
+    chips += [(j, i) for i, j in chips]
+    cores = [(i, i ^ 1) for i in range(dom_size)]
+    side = lax.axis_index("c")
+    core = side.reshape(1)
     points = float(V * ROWS * dom_size * LON)
 
     local = features.reshape(C, CELLS)
-    before = lax.ppermute(local, DOM, up)
-    after = lax.ppermute(local, DOM, down)
+    across = lax.ppermute(local, DOM, chips)
+    beside = lax.ppermute(local, DOM, cores)
     w1, w2, w_back = pl.pallas_call(
         prepare_kernel,
         out_shape=(
@@ -274,13 +291,14 @@
             jax.ShapeDtypeStruct((V, CELLS), F32),
             jax.ShapeDtypeStruct((MEMBERS * SHARE, CELLS), BF16),
         ),
-        in_specs=[SMEM] + [VMEM] * 5,
+        in_specs=[SMEM] * 2 + [VMEM] * 5,
         out_specs=(VMEM,) * 4,
         scratch_shapes=[pltpu.VMEM((3 * C, 4 * LON), BF16)],
         compiler_params=PARAMS,
-    )(ends, before, local, after, w1, w2)
+    )(core, ends, across, local, beside, w1, w2)
 
     every = exchange(sent.reshape(MEMBERS, SHARE, CELLS), ENS)
+    every, outlook = lax.optimization_barrier((every, outlook.reshape(1, V, ROWS, LON)))
     obs = jnp.pad(observed_state.reshape(V, CELLS), ((0, MEMBERS * SHARE - V), (0, 0)))
     me = lax.axis_index(ENS).reshape(1)
     errors, loss = pl.pallas_call(
@@ -295,19 +313,21 @@
     )(me, every, obs.reshape(MEMBERS, SHARE, CELLS), land.reshape(1, CELLS))
     errors = exchange(errors, ENS).reshape(MEMBERS * SHARE, CELLS)
 
-    err_before = lax.ppermute(errors[:VPAD, LON:], DOM, up)
-    err_after = lax.ppermute(errors[:VPAD, :LON], DOM, down)
+    edge = lambda at: lax.dynamic_slice(errors, (0, at * LON), (VPAD, LON))
+    err_across = lax.ppermute(edge(side), DOM, chips)
+    err_beside = lax.ppermute(edge(1 - side), DOM, cores)
     flat = pl.pallas_call(
         backward_kernel,
         out_shape=jax.ShapeDtypeStruct((FLAT, LANES), BF16),
-        in_specs=[VMEM] * 10,
+        in_specs=[SMEM] + [VMEM] * 10,
         out_specs=VMEM,
         scratch_shapes=[
             pltpu.VMEM((3 * VPAD, 4 * LON), BF16),
             pltpu.VMEM((3 * C, CELLS), BF16),
+            pltpu.VMEM((C, CELLS), BF16),
         ],
         compiler_params=PARAMS,
-    )(loss, errors, err_before, err_after, w_back, slope, hidden, before, local, after)
+    )(core, loss, errors, err_across, err_beside, w_back, slope, hidden, across, local, beside)
 
     holder = jnp.bool_(True)
     row = LOSS
@@ -323,8 +343,7 @@
     part = summed(exchange(part, "z"), row, flag, 8)
     part = exchange(part, Y).reshape(8 * size, LANES)
     part = lax.all_gather(part, "x", axis=0, tiled=True)
-    other = lax.ppermute(part, "c", [(0, 1), (1, 0)])
-    core = lax.axis_index("c").reshape(1)
+    part = exchange(jnp.broadcast_to(part[None], (2, HALF, LANES)), "c").reshape(FLAT, LANES)
     first, second, loss = pl.pallas_call(
         last_kernel,
         out_shape=(
@@ -332,11 +351,11 @@
             jax.ShapeDtypeStruct((V, TAPS * C), BF16),
             jax.ShapeDtypeStruct((1, 1), F32),
         ),
-        in_specs=[SMEM, VMEM, VMEM],
+        in_specs=[VMEM],
         out_specs=(VMEM,) * 3,
         compiler_params=PARAMS,
-    )(core, part, other)
-    return outlook.reshape(1, V, ROWS, LON), first, second, loss.reshape(())
+    )(part)
+    return outlook, first, second, loss.reshape(())
 
 
 def solution(mesh):

time: 160 us -> 157 us (0.981)
  starting transfers between devices: 46.7 us -> 37.7 us
  blocking collectives: 58.7 us -> 62 us
  waiting for transfers between devices: 37.7 us -> 40.4 us
    ppermute x5 -> x4, starting transfers between devices: 27.4 us -> 16.8 us  [the longest x1 5.44 us: body(): err_across = lax.ppermute(edge(side), DOM, chips)]
    all_to_all x3 -> x4, waiting for transfers between devices: 30.6 us -> 39.2 us  [exchange(): return lax.all_to_all(array, axes, 0, 0, tiled=True)]
    ppermute x5 -> x4, waiting for transfers between devices: 7.07 us -> 1.2 us  [the longest x1 1.2 us: body(): err_beside = lax.ppermute(edge(1 - side), DOM, cores)]
    all_to_all x4, blocking collectives: 46.9 us -> 50.1 us  [exchange(): return lax.all_to_all(array, axes, 0, 0, tiled=True)]
    all_to_all x3 -> x4, starting transfers between devices: 19.4 us -> 20.9 us  [exchange(): return lax.all_to_all(array, axes, 0, 0, tiled=True)]
  transfers between devices with their start and end apart: 8 -> 8, of which waited for: 6 -> 5; matrix products, arithmetic and copies ran while one was open for 1% -> 1% of each run, Pallas kernels for 0% -> 0%
where the time goes in v4:
time: 157 us
  blocking collectives  62 us (39%)
  waiting for transfers between devices  40.4 us (26%)
  starting transfers between devices  37.7 us (24%)
  Pallas kernels  11.2 us (7%)
  local copies, waits for them, and re-layouts  4.32 us (3%)
    all_to_all x4, blocking collectives, exchange(): return lax.all_to_all(array, axes, 0, 0, tiled=True)  50.1 us
    all_to_all x4, waiting for transfers between devices, exchange(): return lax.all_to_all(array, axes, 0, 0, tiled=True)  39.2 us
    all_to_all x4, starting transfers between devices, exchange(): return lax.all_to_all(array, axes, 0, 0, tiled=True)  20.9 us
    all_gather x1, blocking collectives, body(): part = lax.all_gather(part, 'x', axis=0, tiled=True)  12 us
    ppermute x1, starting transfers between devices, body(): err_across = lax.ppermute(edge(side), DOM, chips)  5.44 us
    ppermute x1, starting transfers between devices, body(): beside = lax.ppermute(local, DOM, cores)  4.87 us
    ppermute x1, starting transfers between devices, body(): across = lax.ppermute(local, DOM, chips)  4.59 us
    pallas_call x1, Pallas kernels, body(): pl.pallas_call(forward_kernel, out_shape=(jax.ShapeDtypeStruct((C, 4 * LO...  3.47 us
  transfers between devices with their start and end apart: 8, of which 5 were waited for; matrix products, arithmetic and copies ran while one was open for 1% of the time, Pallas kernels for 0%

profile of v4, /device:TPU:1, one launch (start us, length us, event | category | flops | bytes accessed | tf_op | source)
XLA Modules:
  0.0 156.6 jit_solution(551393868785390693)
XLA Ops:
  0.6 1.0 copy.9
  1.6 4.6 %collective-permute-start = (bf16[256,512]{1,0:T(8,128)(2,1)S(1)}, bf16[256,512]{1,0:T(8,128)(2,1)S(1)}, u32[]{:S(2)}, u32[]{:S(2)}) collective-permute-start(bf16[256,512]{1,0:T(8,128)(2,1)S(1)} %bitcast.27), channel_id=1, source_target_pairs={{1,2},{3,4},{5,6},{7,8},{9,10},{11,12},{13,14},{15,16},{17,18},{19... | collective-permute-start | bytes 786440 | tf_op jit(solution)/shard_map/ppermute | solution.py:272
  6.2 4.9 %collective-permute-start.1 = (bf16[256,512]{1,0:T(8,128)(2,1)S(1)}, bf16[256,512]{1,0:T(8,128)(2,1)S(1)}, u32[]{:S(2)}, u32[]{:S(2)}) collective-permute-start(bf16[256,512]{1,0:T(8,128)(2,1)S(1)} %bitcast.28), channel_id=1, source_target_pairs={{0,1},{1,0},{2,3},{3,2},{4,5},{5,4},{6,7},{7,6},{8,9},{9,8},{10,11... | collective-permute-start | bytes 786440 | tf_op jit(solution)/shard_map/ppermute | solution.py:273
  11.1 0.0 copy-start
  11.1 1.3 copy-done
  12.4 0.0 copy-start.1
  12.4 1.0 copy-done.1
  13.4 0.4 shard_map.84
  13.8 0.0 copy-start.2
  13.9 0.1 add_convert_fusion.ends
  13.9 0.0 collective-permute-done.across
  13.9 0.0 collective-permute-done.1.beside
  13.9 0.0 copy-start.3
  13.9 3.5 %shard_map.85 = (bf16[256,1024]{1,0:T(8,128)(2,1)S(1)}, f32[256,512]{1,0:T(8,128)S(1)}, f32[100,512]{1,0:T(8,128)S(1)}, bf16[128,512]{1,0:T(8,128)(2,1)}) custom-call(s32[1]{0:T(128)} %bitcast.core, f32[2]{0:T(128)S(1)} %add_convert_fusion.ends, bf16[256,512]{1,0:T(8,128)(2,1)S(1)} %collective-permute-done.across, bf16[256,512]{1,0:T(8,128)(2,1)S(1)} %bitcast.29, ...), custom_call_target="tpu_custom_call" | custom-call | tf_op jit(solution)/shard_map/pallas_call | solution.py:286
  17.4 5.5 %all-to-all-start = ((bf16[8,16,512]{2,1,0:T(8,128)(2,1)}), bf16[8,16,512]{2,1,0:T(8,128)(2,1)S(1)}, u32[]{:S(2)}, u32[]{:S(2)}) async-start(bf16[8,16,512]{2,1,0:T(8,128)(2,1)} %bitcast.3), calls=%async_computation | async-start | bytes 262144 | tf_op jit(solution)/shard_map/all_to_all | solution.py:258
  22.9 0.0 copy-done.2
  22.9 0.1 pad.7
  23.0 0.0 copy-done.3
  23.1 0.8 reshape.72
  23.9 8.6 %all-to-all-done.refs_1_ = bf16[8,16,512]{2,1,0:T(8,128)(2,1)S(1)} async-done(((bf16[8,16,512]{2,1,0:T(8,128)(2,1)}), bf16[8,16,512]{2,1,0:T(8,128)(2,1)S(1)}, u32[]{:S(2)}, u32[]{:S(2)}) %all-to-all-start) | async-done | bytes 131104 | tf_op jit(solution)/shard_map/all_to_all | solution.py:258
  32.5 1.1 shard_map.86
  33.6 3.4 %all-to-all-start.1 = ((bf16[8,16,512]{2,1,0:T(8,128)(2,1)}), bf16[8,16,512]{2,1,0:T(8,128)(2,1)S(1)}, u32[]{:S(2)}, u32[]{:S(2)}) async-start(bf16[8,16,512]{2,1,0:T(8,128)(2,1)} %get-tuple-element.25), calls=%async_computation.1 | async-start | bytes 262144 | tf_op jit(solution)/shard_map/all_to_all | solution.py:258
  36.9 9.4 %all-to-all-done.1 = bf16[8,16,512]{2,1,0:T(8,128)(2,1)S(1)} async-done(((bf16[8,16,512]{2,1,0:T(8,128)(2,1)}), bf16[8,16,512]{2,1,0:T(8,128)(2,1)S(1)}, u32[]{:S(2)}, u32[]{:S(2)}) %all-to-all-start.1) | async-done | bytes 131104 | tf_op jit(solution)/shard_map/all_to_all | solution.py:258
  46.3 5.4 %collective-permute-start.2 = (bf16[112,256]{1,0:T(8,128)(2,1)S(1)}, bf16[112,256]{1,0:T(8,128)(2,1)S(1)}, u32[]{:S(2)}, u32[]{:S(2)}) collective-permute-start(bf16[112,256]{1,0:T(8,128)(2,1)S(1)} %get-tuple-element.33), channel_id=1, source_target_pairs={{1,2},{3,4},{5,6},{7,8},{9,10},{11,12},{13,14},{15,16},{17,18},{19... | collective-permute-start | bytes 172040 | tf_op jit(solution)/shard_map/ppermute | solution.py:317
  51.8 1.9 %collective-permute-start.3 = (bf16[112,256]{1,0:T(8,128)(2,1)S(1)}, bf16[112,256]{1,0:T(8,128)(2,1)S(1)}, u32[]{:S(2)}, u32[]{:S(2)}) collective-permute-start(bf16[112,256]{1,0:T(8,128)(2,1)S(1)} %get-tuple-element.32), channel_id=1, source_target_pairs={{0,1},{1,0},{2,3},{3,2},{4,5},{5,4},{6,7},{7,6},{8,9},{9,8},{10,11... | collective-permute-start | bytes 172040 | tf_op jit(solution)/shard_map/ppermute | solution.py:318
  53.7 0.0 collective-permute-done.2.err_across
  53.7 1.2 collective-permute-done.3.err_beside
  54.9 2.7 %shard_map.87 = bf16[6656,128]{1,0:T(8,128)(2,1)S(1)} custom-call(s32[1]{0:T(128)} %bitcast.core, f32[1,1]{1,0:T(1,128)} %get-tuple-element.24.loss, bf16[128,512]{1,0:T(8,128)(2,1)S(1)} %bitcast.32, bf16[112,256]{1,0:T(8,128)(2,1)S(1)} %collective-permute-done.2.err_across, bf16[112,256]{1,0:T(8,128)(2,1)S(1)} %collective-permute-done.3.err_beside, ...), custom_call_target="tpu_custom_call" | custom-call | tf_op jit(solution)/shard_map/pallas_call | solution.py:319
  57.7 4.9 %all_to_all.40.refs_1_ = bf16[2,3328,128]{2,1,0:T(8,128)(2,1)S(1)} all-to-all(bf16[2,3328,128]{2,1,0:T(8,128)(2,1)S(1)} %bitcast.25), channel_id=1, replica_groups=mesh['x'=4,'yh'=2,'z'=8,'yl'=4,'c'=2] {'c'}, dimensions={0} | all-to-all | bytes 3407872 | tf_op jit(solution)/shard_map/all_to_all | solution.py:258
  62.6 1.1 shard_map.88
  63.7 3.5 %all-to-all-start.3 = ((bf16[4,832,128]{2,1,0:T(8,128)(2,1)}), bf16[4,832,128]{2,1,0:T(8,128)(2,1)S(1)}, u32[]{:S(2)}, u32[]{:S(2)}) async-start(bf16[4,832,128]{2,1,0:T(8,128)(2,1)} %bitcast.11), calls=%async_computation.3 | async-start | bytes 1703936 | tf_op jit(solution)/shard_map/all_to_all | solution.py:258
  67.2 12.7 %all-to-all-done.3.refs_1_ = bf16[4,832,128]{2,1,0:T(8,128)(2,1)S(1)} async-done(((bf16[4,832,128]{2,1,0:T(8,128)(2,1)}), bf16[4,832,128]{2,1,0:T(8,128)(2,1)S(1)}, u32[]{:S(2)}, u32[]{:S(2)}) %all-to-all-start.3) | async-done | bytes 852000 | tf_op jit(solution)/shard_map/all_to_all | solution.py:258
  79.9 0.8 shard_map.89
  80.7 8.6 %all-to-all-start.4 = ((bf16[8,104,128]{2,1,0:T(8,128)(2,1)}), bf16[8,104,128]{2,1,0:T(8,128)(2,1)S(1)}, u32[]{:S(2)}, u32[]{:S(2)}) async-start(bf16[8,104,128]{2,1,0:T(8,128)(2,1)} %bitcast.12), calls=%async_computation.4 | async-start | bytes 425984 | tf_op jit(solution)/shard_map/all_to_all | solution.py:258
  89.2 8.6 %all-to-all-done.4.refs_1_ = bf16[8,104,128]{2,1,0:T(8,128)(2,1)S(1)} async-done(((bf16[8,104,128]{2,1,0:T(8,128)(2,1)}), bf16[8,104,128]{2,1,0:T(8,128)(2,1)S(1)}, u32[]{:S(2)}, u32[]{:S(2)}) %all-to-all-start.4) | async-done | bytes 213024 | tf_op jit(solution)/shard_map/all_to_all | solution.py:258
  97.8 21.6 %all_to_all.41.refs_1_ = bf16[8,104,128]{2,1,0:T(8,128)(2,1)S(1)} all-to-all(bf16[8,104,128]{2,1,0:T(8,128)(2,1)S(1)} %shard_map.90), channel_id=1, replica_groups=mesh['x'=4,'yh'=2,'z'=8,'yl'=4,'c'=2] {'z'}, dimensions={0} | all-to-all | bytes 425984 | tf_op jit(solution)/shard_map/all_to_all | solution.py:258
  119.5 11.3 %all_to_all.42 = bf16[8,104,128]{2,1,0:T(8,128)(2,1)S(1)} all-to-all(bf16[8,104,128]{2,1,0:T(8,128)(2,1)S(1)} %shard_map.91), channel_id=1, replica_groups=mesh['x'=4,'yh'=2,'z'=8,'yl'=4,'c'=2] {'yh','yl'}, dimensions={0} | all-to-all | bytes 425984 | tf_op jit(solution)/shard_map/all_to_all | solution.py:258
  130.8 12.0 %all_gather.3 = bf16[3328,128]{1,0:T(8,128)(2,1)S(1)} all-gather(bf16[832,128]{1,0:T(8,128)(2,1)S(1)} %bitcast.37), channel_id=1, replica_groups=mesh['x'=4,'yh'=2,'z'=8,'yl'=4,'c'=2] {'x'}, dimensions={0}, use_global_device_ids=true | all-gather | bytes 1064960 | tf_op jit(solution)/shard_map/all_gather | solution.py:345
  142.7 0.1 broadcast_in_dim.2
  142.8 12.3 %all_to_all.43 = bf16[2,3328,128]{2,1,0:T(8,128)(2,1)S(1)} all-to-all(bf16[2,3328,128]{2,1,0:T(8,128)(2,1)S(1)} %broadcast_in_dim.2), channel_id=1, replica_groups=mesh['x'=4,'yh'=2,'z'=8,'yl'=4,'c'=2] {'c'}, dimensions={0} | all-to-all | bytes 3407872 | tf_op jit(solution)/shard_map/all_to_all | solution.py:258
  155.1 1.5 shard_map.92
  (6 shorter events, 0.1 us)
Async XLA Ops:
  1.6 12.3 %collective-permute-start = (bf16[256,512]{1,0:T(8,128)(2,1)S(1)}, bf16[256,512]{1,0:T(8,128)(2,1)S(1)}, u32[]{:S(2)}, u32[]{:S(2)}) collective-permute-start(bf16[256,512]{1,0:T(8,128)(2,1)S(1)} %bitcast.27), channel_id=1, source_target_pairs={{1,2},{3,4},{5,6},{7,8},{9,10},{11,12},{13,14},{15,16},{17,18},{19... | collective-permute-start | bytes 786440 | tf_op jit(solution)/shard_map/ppermute | solution.py:272
  6.2 7.7 %collective-permute-start.1 = (bf16[256,512]{1,0:T(8,128)(2,1)S(1)}, bf16[256,512]{1,0:T(8,128)(2,1)S(1)}, u32[]{:S(2)}, u32[]{:S(2)}) collective-permute-start(bf16[256,512]{1,0:T(8,128)(2,1)S(1)} %bitcast.28), channel_id=1, source_target_pairs={{0,1},{1,0},{2,3},{3,2},{4,5},{5,4},{6,7},{7,6},{8,9},{9,8},{10,11... | collective-permute-start | bytes 786440 | tf_op jit(solution)/shard_map/ppermute | solution.py:273
  11.1 1.3 copy-start
  12.4 1.0 copy-start.1
  13.8 9.1 %copy-start.2 = (f32[100,2,256]{2,1,0:T(2,128)S(1)}, f32[100,2,256]{2,1,0:T(2,128)}, u32[]{:S(2)}) copy-start(f32[100,2,256]{2,1,0:T(2,128)} %param.8) | copy-start | bytes 614404
  13.9 9.1 %copy-start.3 = (s32[2,256]{1,0:T(2,128)S(1)}, s32[2,256]{1,0:T(2,128)}, u32[]{:S(2)}) copy-start(s32[2,256]{1,0:T(2,128)} %param.9) | copy-start | bytes 6148
  17.4 15.0 %all-to-all-start = ((bf16[8,16,512]{2,1,0:T(8,128)(2,1)}), bf16[8,16,512]{2,1,0:T(8,128)(2,1)S(1)}, u32[]{:S(2)}, u32[]{:S(2)}) async-start(bf16[8,16,512]{2,1,0:T(8,128)(2,1)} %bitcast.3), calls=%async_computation | async-start | bytes 262144 | tf_op jit(solution)/shard_map/all_to_all | solution.py:258
  33.6 12.8 %all-to-all-start.1 = ((bf16[8,16,512]{2,1,0:T(8,128)(2,1)}), bf16[8,16,512]{2,1,0:T(8,128)(2,1)S(1)}, u32[]{:S(2)}, u32[]{:S(2)}) async-start(bf16[8,16,512]{2,1,0:T(8,128)(2,1)} %get-tuple-element.25), calls=%async_computation.1 | async-start | bytes 262144 | tf_op jit(solution)/shard_map/all_to_all | solution.py:258
  46.3 7.4 %collective-permute-start.2 = (bf16[112,256]{1,0:T(8,128)(2,1)S(1)}, bf16[112,256]{1,0:T(8,128)(2,1)S(1)}, u32[]{:S(2)}, u32[]{:S(2)}) collective-permute-start(bf16[112,256]{1,0:T(8,128)(2,1)S(1)} %get-tuple-element.33), channel_id=1, source_target_pairs={{1,2},{3,4},{5,6},{7,8},{9,10},{11,12},{13,14},{15,16},{17,18},{19... | collective-permute-start | bytes 172040 | tf_op jit(solution)/shard_map/ppermute | solution.py:317
  51.8 3.1 %collective-permute-start.3 = (bf16[112,256]{1,0:T(8,128)(2,1)S(1)}, bf16[112,256]{1,0:T(8,128)(2,1)S(1)}, u32[]{:S(2)}, u32[]{:S(2)}) collective-permute-start(bf16[112,256]{1,0:T(8,128)(2,1)S(1)} %get-tuple-element.32), channel_id=1, source_target_pairs={{0,1},{1,0},{2,3},{3,2},{4,5},{5,4},{6,7},{7,6},{8,9},{9,8},{10,11... | collective-permute-start | bytes 172040 | tf_op jit(solution)/shard_map/ppermute | solution.py:318
  63.7 16.2 %all-to-all-start.3 = ((bf16[4,832,128]{2,1,0:T(8,128)(2,1)}), bf16[4,832,128]{2,1,0:T(8,128)(2,1)S(1)}, u32[]{:S(2)}, u32[]{:S(2)}) async-start(bf16[4,832,128]{2,1,0:T(8,128)(2,1)} %bitcast.11), calls=%async_computation.3 | async-start | bytes 1703936 | tf_op jit(solution)/shard_map/all_to_all | solution.py:258
  80.7 17.1 %all-to-all-start.4 = ((bf16[8,104,128]{2,1,0:T(8,128)(2,1)}), bf16[8,104,128]{2,1,0:T(8,128)(2,1)S(1)}, u32[]{:S(2)}, u32[]{:S(2)}) async-start(bf16[8,104,128]{2,1,0:T(8,128)(2,1)} %bitcast.12), calls=%async_computation.4 | async-start | bytes 425984 | tf_op jit(solution)/shard_map/all_to_all | solution.py:258

commit v5 on v4

--- a/solution.py
+++ b/solution.py
@@ -244,14 +244,20 @@
     )(holder, parts)
 
 
-def last_kernel(sums, first, second, loss):
-    for tile in range(TILES):
-        lanes = slice(tile * LANES, (tile + 1) * LANES)
-        first[:, lanes] = sums[tile * C : (tile + 1) * C, :]
-        at = SECOND + tile * VPAD
-        second[:, lanes] = sums[at : at + VPAD, :][:V]
-    here = sums[LOSS : LOSS + 16, :].astype(F32)
-    loss[...] = here[0:1, 0:1] + here[1:2, 0:1]
+def last_kernel(core, own, other, first, second, loss):
+    def assemble(low, high):
+        def flat(at, n):
+            return low[at : at + n, :] if at < HALF else high[at - HALF : at - HALF + n, :]
+
+        for tile in range(TILES):
+            lanes = slice(tile * LANES, (tile + 1) * LANES)
+            first[:, lanes] = flat(tile * C, C)
+            second[:, lanes] = flat(SECOND + tile * VPAD, VPAD)[:V]
+        here = flat(LOSS, 16).astype(F32)
+        loss[...] = here[0:1, 0:1] + here[1:2, 0:1]
+
+    pl.when(core[0] == 0)(lambda: assemble(own, other))
+    pl.when(core[0] == 1)(lambda: assemble(other, own))
 
 
 def exchange(array, axes):
@@ -283,6 +289,14 @@
         compiler_params=PARAMS,
     )(w_first, later_kernel_matrix)
     ends = jnp.stack([(dom > 0).astype(F32), (dom < dom_size - 1).astype(F32)])
+    obs = jnp.pad(observed_state.reshape(V, CELLS), ((0, MEMBERS * SHARE - V), (0, 0)))
+    obs = obs.reshape(MEMBERS, SHARE, CELLS)
+    area = land.reshape(1, CELLS)
+    me = lax.axis_index(ENS).reshape(1)
+    upper = side == 0
+    across, obs, area, me, upper, ends = lax.optimization_barrier(
+        (across, obs, area, me, upper, ends)
+    )
     hidden, slope, outlook, sent = pl.pallas_call(
         forward_kernel,
         out_shape=(
@@ -298,9 +312,6 @@
     )(core, ends, across, local, beside, w1, w2)
 
     every = exchange(sent.reshape(MEMBERS, SHARE, CELLS), ENS)
-    every, outlook = lax.optimization_barrier((every, outlook.reshape(1, V, ROWS, LON)))
-    obs = jnp.pad(observed_state.reshape(V, CELLS), ((0, MEMBERS * SHARE - V), (0, 0)))
-    me = lax.axis_index(ENS).reshape(1)
     errors, loss = pl.pallas_call(
         lambda *refs: score_kernel(points, *refs),
         out_shape=(
@@ -310,12 +321,14 @@
         in_specs=[SMEM] + [VMEM] * 3,
         out_specs=(VMEM,) * 2,
         compiler_params=PARAMS,
-    )(me, every, obs.reshape(MEMBERS, SHARE, CELLS), land.reshape(1, CELLS))
+    )(me, every, obs, area)
     errors = exchange(errors, ENS).reshape(MEMBERS * SHARE, CELLS)
 
-    edge = lambda at: lax.dynamic_slice(errors, (0, at * LON), (VPAD, LON))
-    err_across = lax.ppermute(edge(side), DOM, chips)
-    err_beside = lax.ppermute(edge(1 - side), DOM, cores)
+    first, last = errors[:VPAD, :LON], errors[:VPAD, LON:]
+    err_across = lax.ppermute(jnp.where(upper, first, last), DOM, chips)
+    err_beside = lax.ppermute(jnp.where(upper, last, first), DOM, cores)
+    outlook = outlook.reshape(1, V, ROWS, LON)
+    err_across, outlook = lax.optimization_barrier((err_across, outlook))
     flat = pl.pallas_call(
         backward_kernel,
         out_shape=jax.ShapeDtypeStruct((FLAT, LANES), BF16),
@@ -329,21 +342,24 @@
         compiler_params=PARAMS,
     )(core, loss, errors, err_across, err_beside, w_back, slope, hidden, across, local, beside)
 
+    stages = (("c", 2), ("x", 4), (Y, 8))
     holder = jnp.bool_(True)
-    row = LOSS
-    size = FLAT
-    part = flat
-    for axes, n in (("c", 2), ("x", 4), (Y, 8)):
+    row, size = LOSS, FLAT
+    flags, places = [], []
+    for axes, n in stages:
         size //= n
         holder = holder & (lax.axis_index(axes) == row // size)
         row %= size
+        flags.append(holder.astype(jnp.int32).reshape(1))
+        places.append((row, size))
+    part, flags = lax.optimization_barrier((flat, flags))
+    for (axes, n), flag, (row, size) in zip(stages, flags, places):
         part = exchange(part.reshape(n, size, LANES), axes)
-        flag = holder.astype(jnp.int32).reshape(1)
         part = summed(part, row, flag, 8 if axes == Y else 1)
     part = summed(exchange(part, "z"), row, flag, 8)
     part = exchange(part, Y).reshape(8 * size, LANES)
     part = lax.all_gather(part, "x", axis=0, tiled=True)
-    part = exchange(jnp.broadcast_to(part[None], (2, HALF, LANES)), "c").reshape(FLAT, LANES)
+    other = lax.ppermute(part, "c", [(0, 1), (1, 0)])
     first, second, loss = pl.pallas_call(
         last_kernel,
         out_shape=(
@@ -351,10 +367,10 @@
             jax.ShapeDtypeStruct((V, TAPS * C), BF16),
             jax.ShapeDtypeStruct((1, 1), F32),
         ),
-        in_specs=[VMEM],
+        in_specs=[SMEM, VMEM, VMEM],
         out_specs=(VMEM,) * 3,
         compiler_params=PARAMS,
-    )(part)
+    )(core, part, other)
     return outlook, first, second, loss.reshape(())
 
 

time: 157 us -> 150 us (0.955)
  blocking collectives: 62 us -> 108 us
  waiting for transfers between devices: 40.4 us -> 2.36 us
  starting transfers between devices: 37.7 us -> 26 us
  Pallas kernels: 11.2 us -> 8.88 us
    all_to_all x4 -> x7, blocking collectives: 50.1 us -> 96.2 us  [exchange(): return lax.all_to_all(array, axes, 0, 0, tiled=True)]
    all_to_all x4 -> x0, waiting for transfers between devices: 39.2 us -> none  [exchange(): return lax.all_to_all(array, axes, 0, 0, tiled=True)]
    all_to_all x4 -> x0, starting transfers between devices: 20.9 us -> none  [exchange(): return lax.all_to_all(array, axes, 0, 0, tiled=True)]
    ppermute x2 -> x3, starting transfers between devices: 7.36 us -> 16.5 us  [the longest x1 9.52 us: body(): other = lax.ppermute(part, 'c', [(0, 1), (1, 0)])]
    pallas_call x4, Pallas kernels: 1.96 us -> 0.38 us  [summed(): pl.pallas_call(body, out_shape=jax.ShapeDtypeStruct((copies,) + parts.sha...]
    unnamed x12 -> x8, local copies, waits for them, and re-layouts: 3.38 us -> 2.82 us
  transfers between devices with their start and end apart: 8 -> 5, of which waited for: 5 -> 2; matrix products, arithmetic and copies ran while one was open for 1% -> 2% of each run, Pallas kernels for 0% -> 0%
where the time goes in v5:
time: 150 us
  blocking collectives  108 us (72%)
  starting transfers between devices  26 us (17%)
  Pallas kernels  8.88 us (6%)
  local copies, waits for them, and re-layouts  3.64 us (2%)
  waiting for transfers between devices  2.36 us (2%)
    all_to_all x7, blocking collectives, exchange(): return lax.all_to_all(array, axes, 0, 0, tiled=True)  96.2 us
    all_gather x1, blocking collectives, body(): part = lax.all_gather(part, 'x', axis=0, tiled=True)  11.9 us
    ppermute x1, starting transfers between devices, body(): other = lax.ppermute(part, 'c', [(0, 1), (1, 0)])  9.52 us
    ppermute x1, starting transfers between devices, body(): err_across = lax.ppermute(jnp.where(upper, first, last), DOM, chips)  5.09 us
    ppermute x1, starting transfers between devices, body(): beside = lax.ppermute(local, DOM, cores)  4.87 us
    ppermute x1, starting transfers between devices, body(): across = lax.ppermute(local, DOM, chips)  4.59 us
  transfers between devices with their start and end apart: 5, of which 2 were waited for; matrix products, arithmetic and copies ran while one was open for 2% of the time, Pallas kernels for 0%

profile of v5, /device:TPU:1, one launch (start us, length us, event | category | flops | bytes accessed | tf_op | source)
XLA Modules:
  0.0 149.9 jit_solution(1319878059644328590)
XLA Ops:
  0.6 0.0 copy-start.1
  0.6 0.0 copy-start
  0.7 1.1 copy.9
  1.8 4.6 %collective-permute-start = (bf16[256,512]{1,0:T(8,128)(2,1)S(1)}, bf16[256,512]{1,0:T(8,128)(2,1)S(1)}, u32[]{:S(2)}, u32[]{:S(2)}) collective-permute-start(bf16[256,512]{1,0:T(8,128)(2,1)S(1)} %bitcast.26), channel_id=1, source_target_pairs={{1,2},{3,4},{5,6},{7,8},{9,10},{11,12},{13,14},{15,16},{17,18},{19... | collective-permute-start | bytes 786440 | tf_op jit(solution)/shard_map/ppermute | solution.py:278
  6.4 4.9 %collective-permute-start.1 = (bf16[256,512]{1,0:T(8,128)(2,1)S(1)}, bf16[256,512]{1,0:T(8,128)(2,1)S(1)}, u32[]{:S(2)}, u32[]{:S(2)}) collective-permute-start(bf16[256,512]{1,0:T(8,128)(2,1)S(1)} %bitcast.27), channel_id=1, source_target_pairs={{0,1},{1,0},{2,3},{3,2},{4,5},{5,4},{6,7},{7,6},{8,9},{9,8},{10,11... | collective-permute-start | bytes 786440 | tf_op jit(solution)/shard_map/ppermute | solution.py:279
  11.3 0.7 copy.11
  11.9 1.0 pad.7
  13.0 0.0 copy-done.1
  13.0 0.0 copy-done
  13.0 0.4 shard_map.84
  13.5 0.1 add_convert_fusion.ends
  13.5 0.0 collective-permute-done.across
  13.5 0.0 collective-permute-done.1.beside
  13.5 2.7 %shard_map.85 = (bf16[256,1024]{1,0:T(8,128)(2,1)S(1)}, f32[256,512]{1,0:T(8,128)S(1)}, f32[100,512]{1,0:T(8,128)S(1)}, bf16[128,512]{1,0:T(8,128)(2,1)S(1)}) custom-call(s32[1]{0:T(128)} %bitcast.4.core, f32[2]{0:T(128)S(1)} %add_convert_fusion.ends, bf16[256,512]{1,0:T(8,128)(2,1)S(1)} %collective-permute-done.across, bf16[256,512]{1,0:T(8,128)(2,1)S(1)} %bitcast.28, ...), custom_call_target="tpu_custom_call" | custom-call | tf_op jit(solution)/shard_map/pallas_call | solution.py:300
  16.3 15.7 %all_to_all.35.refs_1_ = bf16[8,16,512]{2,1,0:T(8,128)(2,1)S(1)} all-to-all(bf16[8,16,512]{2,1,0:T(8,128)(2,1)S(1)} %bitcast.34), channel_id=1, replica_groups=mesh['x'=4,'yh'=2,'z'=8,'yl'=4,'c'=2] {'x','yh'}, dimensions={0} | all-to-all | bytes 262144 | tf_op jit(solution)/shard_map/all_to_all | solution.py:264
  32.0 1.1 shard_map.86
  33.1 11.8 %all_to_all.36 = bf16[8,16,512]{2,1,0:T(8,128)(2,1)S(1)} all-to-all(bf16[8,16,512]{2,1,0:T(8,128)(2,1)S(1)} %get-tuple-element.37), channel_id=1, replica_groups=mesh['x'=4,'yh'=2,'z'=8,'yl'=4,'c'=2] {'x','yh'}, dimensions={0} | all-to-all | bytes 262144 | tf_op jit(solution)/shard_map/all_to_all | solution.py:264
  44.9 5.1 %collective-permute-start.2 = (bf16[112,256]{1,0:T(8,128)(2,1)S(1)}, bf16[112,256]{1,0:T(8,128)(2,1)S(1)}, u32[]{:S(2)}, u32[]{:S(2)}) collective-permute-start(bf16[112,256]{1,0:T(8,128)(2,1)S(1)} %get-tuple-element.53), channel_id=1, source_target_pairs={{1,2},{3,4},{5,6},{7,8},{9,10},{11,12},{13,14},{15,16},{17,18},{19... | collective-permute-start | bytes 172040 | tf_op jit(solution)/shard_map/ppermute | solution.py:328
  50.0 1.9 %collective-permute-start.3 = (bf16[112,256]{1,0:T(8,128)(2,1)S(1)}, bf16[112,256]{1,0:T(8,128)(2,1)S(1)}, u32[]{:S(2)}, u32[]{:S(2)}) collective-permute-start(bf16[112,256]{1,0:T(8,128)(2,1)S(1)} %get-tuple-element.52), channel_id=1, source_target_pairs={{0,1},{1,0},{2,3},{3,2},{4,5},{5,4},{6,7},{7,6},{8,9},{9,8},{10,11... | collective-permute-start | bytes 172040 | tf_op jit(solution)/shard_map/ppermute | solution.py:329
  52.0 0.8 reshape.76
  52.8 0.0 collective-permute-done.2.err_across
  52.8 0.4 collective-permute-done.3.err_beside
  53.2 2.8 %shard_map.87 = bf16[6656,128]{1,0:T(8,128)(2,1)S(1)} custom-call(s32[1]{0:T(128)} %bitcast.4.core, f32[1,1]{1,0:T(1,128)} %get-tuple-element.40.loss, bf16[128,512]{1,0:T(8,128)(2,1)S(1)} %bitcast.31, bf16[112,256]{1,0:T(8,128)(2,1)S(1)} %collective-permute-done.2.err_across, bf16[112,256]{1,0:T(8,128)(2,1)S(1)} %collective-permute-done.3.err_beside, ...), custom_call_target="tpu_custom_call" | custom-call | tf_op jit(solution)/shard_map/pallas_call | solution.py:332
  56.0 4.9 %all_to_all.37.refs_1_ = bf16[2,3328,128]{2,1,0:T(8,128)(2,1)S(1)} all-to-all(bf16[2,3328,128]{2,1,0:T(8,128)(2,1)S(1)} %bitcast.24), channel_id=1, replica_groups=mesh['x'=4,'yh'=2,'z'=8,'yl'=4,'c'=2] {'c'}, dimensions={0} | all-to-all | bytes 3407872 | tf_op jit(solution)/shard_map/all_to_all | solution.py:264
  60.9 0.2 shard_map.88
  61.1 14.8 %all_to_all.38.refs_1_ = bf16[4,832,128]{2,1,0:T(8,128)(2,1)S(1)} all-to-all(bf16[4,832,128]{2,1,0:T(8,128)(2,1)S(1)} %bitcast.25), channel_id=1, replica_groups=mesh['x'=4,'yh'=2,'z'=8,'yl'=4,'c'=2] {'x'}, dimensions={0} | all-to-all | bytes 1703936 | tf_op jit(solution)/shard_map/all_to_all | solution.py:264
  75.9 0.1 shard_map.89
  76.0 17.1 %all_to_all.39.refs_1_ = bf16[8,104,128]{2,1,0:T(8,128)(2,1)S(1)} all-to-all(bf16[8,104,128]{2,1,0:T(8,128)(2,1)S(1)} %bitcast.33), channel_id=1, replica_groups=mesh['x'=4,'yh'=2,'z'=8,'yl'=4,'c'=2] {'yh','yl'}, dimensions={0} | all-to-all | bytes 425984 | tf_op jit(solution)/shard_map/all_to_all | solution.py:264
  93.2 20.3 %all_to_all.40.refs_1_ = bf16[8,104,128]{2,1,0:T(8,128)(2,1)S(1)} all-to-all(bf16[8,104,128]{2,1,0:T(8,128)(2,1)S(1)} %shard_map.90), channel_id=1, replica_groups=mesh['x'=4,'yh'=2,'z'=8,'yl'=4,'c'=2] {'z'}, dimensions={0} | all-to-all | bytes 425984 | tf_op jit(solution)/shard_map/all_to_all | solution.py:264
  113.5 11.5 %all_to_all.41 = bf16[8,104,128]{2,1,0:T(8,128)(2,1)S(1)} all-to-all(bf16[8,104,128]{2,1,0:T(8,128)(2,1)S(1)} %shard_map.91), channel_id=1, replica_groups=mesh['x'=4,'yh'=2,'z'=8,'yl'=4,'c'=2] {'yh','yl'}, dimensions={0} | all-to-all | bytes 425984 | tf_op jit(solution)/shard_map/all_to_all | solution.py:264
  125.0 11.9 %all_gather.3.own = bf16[3328,128]{1,0:T(8,128)(2,1)S(1)} all-gather(bf16[832,128]{1,0:T(8,128)(2,1)S(1)} %bitcast.38), channel_id=1, replica_groups=mesh['x'=4,'yh'=2,'z'=8,'yl'=4,'c'=2] {'x'}, dimensions={0}, use_global_device_ids=true | all-gather | bytes 1064960 | tf_op jit(solution)/shard_map/all_gather | solution.py:361
  136.9 9.5 %collective-permute-start.4 = (bf16[3328,128]{1,0:T(8,128)(2,1)S(1)}, bf16[3328,128]{1,0:T(8,128)(2,1)S(1)}, u32[]{:S(2)}, u32[]{:S(2)}) collective-permute-start(bf16[3328,128]{1,0:T(8,128)(2,1)S(1)} %all_gather.3.own), channel_id=1, source_target_pairs={{0,1},{1,0},{2,3},{3,2},{4,5},{5,4},{6,7},{7,6},{8,9},{9,8},{10,11... | collective-permute-start | bytes 2555912 | tf_op jit(solution)/shard_map/ppermute | solution.py:362
  146.5 2.0 %collective-permute-done.4.other = bf16[3328,128]{1,0:T(8,128)(2,1)S(1)} collective-permute-done((bf16[3328,128]{1,0:T(8,128)(2,1)S(1)}, bf16[3328,128]{1,0:T(8,128)(2,1)S(1)}, u32[]{:S(2)}, u32[]{:S(2)}) %collective-permute-start.4) | collective-permute-done | bytes 852000 | tf_op jit(solution)/shard_map/ppermute | solution.py:362
  148.4 1.5 shard_map.92
  (5 shorter events, 0.1 us)
Async XLA Ops:
  0.6 12.4 %copy-start.1 = (bf16[100,2304]{1,0:T(8,128)(2,1)S(1)}, bf16[100,2304]{1,0:T(8,128)(2,1)}, u32[]{:S(2)}) copy-start(bf16[100,2304]{1,0:T(8,128)(2,1)} %w2.1) | copy-start | bytes 1382404
  0.6 12.4 %copy-start = (bf16[256,2304]{1,0:T(8,128)(2,1)S(1)}, bf16[256,2304]{1,0:T(8,128)(2,1)}, u32[]{:S(2)}) copy-start(bf16[256,2304]{1,0:T(8,128)(2,1)} %w1.1) | copy-start | bytes 3538948
  1.8 11.8 %collective-permute-start = (bf16[256,512]{1,0:T(8,128)(2,1)S(1)}, bf16[256,512]{1,0:T(8,128)(2,1)S(1)}, u32[]{:S(2)}, u32[]{:S(2)}) collective-permute-start(bf16[256,512]{1,0:T(8,128)(2,1)S(1)} %bitcast.26), channel_id=1, source_target_pairs={{1,2},{3,4},{5,6},{7,8},{9,10},{11,12},{13,14},{15,16},{17,18},{19... | collective-permute-start | bytes 786440 | tf_op jit(solution)/shard_map/ppermute | solution.py:278
  6.4 7.2 %collective-permute-start.1 = (bf16[256,512]{1,0:T(8,128)(2,1)S(1)}, bf16[256,512]{1,0:T(8,128)(2,1)S(1)}, u32[]{:S(2)}, u32[]{:S(2)}) collective-permute-start(bf16[256,512]{1,0:T(8,128)(2,1)S(1)} %bitcast.27), channel_id=1, source_target_pairs={{0,1},{1,0},{2,3},{3,2},{4,5},{5,4},{6,7},{7,6},{8,9},{9,8},{10,11... | collective-permute-start | bytes 786440 | tf_op jit(solution)/shard_map/ppermute | solution.py:279
  44.9 7.9 %collective-permute-start.2 = (bf16[112,256]{1,0:T(8,128)(2,1)S(1)}, bf16[112,256]{1,0:T(8,128)(2,1)S(1)}, u32[]{:S(2)}, u32[]{:S(2)}) collective-permute-start(bf16[112,256]{1,0:T(8,128)(2,1)S(1)} %get-tuple-element.53), channel_id=1, source_target_pairs={{1,2},{3,4},{5,6},{7,8},{9,10},{11,12},{13,14},{15,16},{17,18},{19... | collective-permute-start | bytes 172040 | tf_op jit(solution)/shard_map/ppermute | solution.py:328
  50.0 3.1 %collective-permute-start.3 = (bf16[112,256]{1,0:T(8,128)(2,1)S(1)}, bf16[112,256]{1,0:T(8,128)(2,1)S(1)}, u32[]{:S(2)}, u32[]{:S(2)}) collective-permute-start(bf16[112,256]{1,0:T(8,128)(2,1)S(1)} %get-tuple-element.52), channel_id=1, source_target_pairs={{0,1},{1,0},{2,3},{3,2},{4,5},{5,4},{6,7},{7,6},{8,9},{9,8},{10,11... | collective-permute-start | bytes 172040 | tf_op jit(solution)/shard_map/ppermute | solution.py:329
  136.9 11.5 %collective-permute-start.4 = (bf16[3328,128]{1,0:T(8,128)(2,1)S(1)}, bf16[3328,128]{1,0:T(8,128)(2,1)S(1)}, u32[]{:S(2)}, u32[]{:S(2)}) collective-permute-start(bf16[3328,128]{1,0:T(8,128)(2,1)S(1)} %all_gather.3.own), channel_id=1, source_target_pairs={{0,1},{1,0},{2,3},{3,2},{4,5},{5,4},{6,7},{7,6},{8,9},{9,8},{10,11... | collective-permute-start | bytes 2555912 | tf_op jit(solution)/shard_map/ppermute | solution.py:362

commit v6 on v5

--- a/solution.py
+++ b/solution.py
@@ -100,11 +100,12 @@
         if i == wide - 1:
             value = value * ends[1]
         hidden[:, lanes] = value.astype(BF16)
-        if 0 < i < wide - 1:
-            own = slice((i - 1) * LON, i * LON)
-            slope[:, own] = half + (0.5 * GELU_A) * pre * (1.0 - t * t) * (
-                1.0 + 3.0 * GELU_B * square
-            )
+        steep = half + (0.5 * GELU_A) * pre * (1.0 - t * t) * (1.0 + 3.0 * GELU_B * square)
+        if i == 0:
+            steep = steep * ends[0]
+        if i == wide - 1:
+            steep = steep * ends[1]
+        slope[:, lanes] = steep
     top = V // 16 * 16
     sent[top:, :] = jnp.zeros((MEMBERS * SHARE - top, CELLS), BF16)
     spare = jnp.zeros((VPAD - V, LON), F32)
@@ -155,45 +156,38 @@
 
 
 def backward_kernel(
-    core, loss, err, err_across, err_beside, w_back, slope, hidden, across, local, beside, out, e, pg, ends
+    core, loss, err, w_back, slope, hidden, across, local, beside, out, e, pg, trunk
 ):
-    def fill(i, row):
-        row = row.astype(F32)
+    trunk[:, 2 * LON : 4 * LON] = local[...]
+
+    def fill(before, after):
+        trunk[:, : 2 * LON] = before[...]
+        trunk[:, 4 * LON :] = after[...]
+
+    by_side(core, across, beside, fill)
+    for i in range(ROWS):
+        row = err[:VPAD, i * LON : (i + 1) * LON].astype(F32)
         for b in range(3):
             e[b * VPAD : (b + 1) * VPAD, i * LON : (i + 1) * LON] = turn(row, b - 1).astype(BF16)
-
-    fill(1, err[:VPAD, :LON])
-    fill(2, err[:VPAD, LON:])
-    by_side(core, err_across, err_beside, lambda u, d: (fill(0, u[...]), fill(3, d[...])))
-
-    def fill_ends(before, after):
-        ends[:, :LON] = before[:, LON:]
-        ends[:, LON:] = after[:, :LON]
-
-    by_side(core, across, beside, fill_ends)
-    for i in range(ROWS):
+    wide = ROWS + 2
+    for i in range(wide):
         back = None
         for a in range(3):
-            start = (i + 2 - a) * LON
-            term = dot(w_back[a], e[:, start : start + LON])
-            back = term if back is None else back + term
-        own = slice(i * LON, (i + 1) * LON)
-        grad = back * slope[:, own]
-        for b in range(3):
-            pg[b * C : (b + 1) * C, own] = turn(grad, b - 1).astype(BF16)
+            if 0 <= i - a < ROWS:
+                term = dot(w_back[a], e[:, (i - a) * LON : (i - a + 1) * LON])
+                back = term if back is None else back + term
+        lanes = slice(i * LON, (i + 1) * LON)
+        grad = back * slope[:, lanes]
+        for b in range(3):
+            pg[b * C : (b + 1) * C, lanes] = turn(grad, b - 1).astype(BF16)
     for a in range(3):
-        if a == 0:
-            window = jnp.concatenate([ends[:, :LON], local[:, :LON]], axis=1)
-        elif a == 1:
-            window = local[...]
-        else:
-            window = jnp.concatenate([local[:, LON:], ends[:, LON:]], axis=1)
+        window = trunk[:, a * LON : (a + wide) * LON]
         for b in range(3):
             first = lax.dot_general(
                 pg[b * C : (b + 1) * C, :], window, NT, preferred_element_type=F32
             ).astype(BF16)
             second = lax.dot_general(
-                e[b * VPAD : (b + 1) * VPAD, LON : 3 * LON],
+                e[b * VPAD : (b + 1) * VPAD, :],
                 hidden[:, a * LON : a * LON + CELLS],
                 NT,
                 preferred_element_type=F32,
@@ -293,55 +287,6 @@
     obs = obs.reshape(MEMBERS, SHARE, CELLS)
     area = land.reshape(1, CELLS)
     me = lax.axis_index(ENS).reshape(1)
-    upper = side == 0
-    across, obs, area, me, upper, ends = lax.optimization_barrier(
-        (across, obs, area, me, upper, ends)
-    )
-    hidden, slope, outlook, sent = pl.pallas_call(
-        forward_kernel,
-        out_shape=(
-            jax.ShapeDtypeStruct((C, 4 * LON), BF16),
-            jax.ShapeDtypeStruct((C, CELLS), F32),
-            jax.ShapeDtypeStruct((V, CELLS), F32),
-            jax.ShapeDtypeStruct((MEMBERS * SHARE, CELLS), BF16),
-        ),
-        in_specs=[SMEM] * 2 + [VMEM] * 5,
-        out_specs=(VMEM,) * 4,
-        scratch_shapes=[pltpu.VMEM((3 * C, 4 * LON), BF16)],
-        compiler_params=PARAMS,
-    )(core, ends, across, local, beside, w1, w2)
-
-    every = exchange(sent.reshape(MEMBERS, SHARE, CELLS), ENS)
-    errors, loss = pl.pallas_call(
-        lambda *refs: score_kernel(points, *refs),
-        out_shape=(
-            jax.ShapeDtypeStruct((MEMBERS, SHARE, CELLS), BF16),
-            jax.ShapeDtypeStruct((1, 1), F32),
-        ),
-        in_specs=[SMEM] + [VMEM] * 3,
-        out_specs=(VMEM,) * 2,
-        compiler_params=PARAMS,
-    )(me, every, obs, area)
-    errors = exchange(errors, ENS).reshape(MEMBERS * SHARE, CELLS)
-
-    first, last = errors[:VPAD, :LON], errors[:VPAD, LON:]
-    err_across = lax.ppermute(jnp.where(upper, first, last), DOM, chips)
-    err_beside = lax.ppermute(jnp.where(upper, last, first), DOM, cores)
-    outlook = outlook.reshape(1, V, ROWS, LON)
-    err_across, outlook = lax.optimization_barrier((err_across, outlook))
-    flat = pl.pallas_call(
-        backward_kernel,
-        out_shape=jax.ShapeDtypeStruct((FLAT, LANES), BF16),
-        in_specs=[SMEM] + [VMEM] * 10,
-        out_specs=VMEM,
-        scratch_shapes=[
-            pltpu.VMEM((3 * VPAD, 4 * LON), BF16),
-            pltpu.VMEM((3 * C, CELLS), BF16),
-            pltpu.VMEM((C, CELLS), BF16),
-        ],
-        compiler_params=PARAMS,
-    )(core, loss, errors, err_across, err_beside, w_back, slope, hidden, across, local, beside)
-
     stages = (("c", 2), ("x", 4), (Y, 8))
     holder = jnp.bool_(True)
     row, size = LOSS, FLAT
@@ -352,7 +297,50 @@
         row %= size
         flags.append(holder.astype(jnp.int32).reshape(1))
         places.append((row, size))
-    part, flags = lax.optimization_barrier((flat, flags))
+    across, obs, area, me, ends, flags = lax.optimization_barrier(
+        (across, obs, area, me, ends, flags)
+    )
+    hidden, slope, outlook, sent = pl.pallas_call(
+        forward_kernel,
+        out_shape=(
+            jax.ShapeDtypeStruct((C, 4 * LON), BF16),
+            jax.ShapeDtypeStruct((C, 4 * LON), F32),
+            jax.ShapeDtypeStruct((V, CELLS), F32),
+            jax.ShapeDtypeStruct((MEMBERS * SHARE, CELLS), BF16),
+        ),
+        in_specs=[SMEM] * 2 + [VMEM] * 5,
+        out_specs=(VMEM,) * 4,
+        scratch_shapes=[pltpu.VMEM((3 * C, 4 * LON), BF16)],
+        compiler_params=PARAMS,
+    )(core, ends, across, local, beside, w1, w2)
+
+    every = exchange(sent.reshape(MEMBERS, SHARE, CELLS), ENS)
+    errors, loss = pl.pallas_call(
+        lambda *refs: score_kernel(points, *refs),
+        out_shape=(
+            jax.ShapeDtypeStruct((MEMBERS, SHARE, CELLS), BF16),
+            jax.ShapeDtypeStruct((1, 1), F32),
+        ),
+        in_specs=[SMEM] + [VMEM] * 3,
+        out_specs=(VMEM,) * 2,
+        compiler_params=PARAMS,
+    )(me, every, obs, area)
+    errors = exchange(errors, ENS).reshape(MEMBERS * SHARE, CELLS)
+
+    flat = pl.pallas_call(
+        backward_kernel,
+        out_shape=jax.ShapeDtypeStruct((FLAT, LANES), BF16),
+        in_specs=[SMEM] + [VMEM] * 8,
+        out_specs=VMEM,
+        scratch_shapes=[
+            pltpu.VMEM((3 * VPAD, CELLS), BF16),
+            pltpu.VMEM((3 * C, 4 * LON), BF16),
+            pltpu.VMEM((C, 6 * LON), BF16),
+        ],
+        compiler_params=PARAMS,
+    )(core, loss, errors, w_back, slope, hidden, across, local, beside)
+
+    part = flat
     for (axes, n), flag, (row, size) in zip(stages, flags, places):
         part = exchange(part.reshape(n, size, LANES), axes)
         part = summed(part, row, flag, 8 if axes == Y else 1)
@@ -360,6 +348,7 @@
     part = exchange(part, Y).reshape(8 * size, LANES)
     part = lax.all_gather(part, "x", axis=0, tiled=True)
     other = lax.ppermute(part, "c", [(0, 1), (1, 0)])
+    other, outlook = lax.optimization_barrier((other, outlook.reshape(1, V, ROWS, LON)))
     first, second, loss = pl.pallas_call(
         last_kernel,
         out_shape=(

time: 150 us -> 142 us (0.947)
  starting transfers between devices: 26 us -> 19 us
    ppermute x2 -> x0, starting transfers between devices: 7.01 us -> none  [the longest x1 5.09 us: body(): err_across = lax.ppermute(jnp.where(upper, first, last), DOM, chips)]
  transfers between devices with their start and end apart: 5 -> 3, of which waited for: 2 -> 1; matrix products, arithmetic and copies ran while one was open for 2% -> 2% of each run, Pallas kernels for 0% -> 0%
where the time goes in v6:
time: 142 us; the launch traced here: 141 us
  blocking collectives  107 us (75%)
  starting transfers between devices  19 us (13%)
  Pallas kernels  9.52 us (7%)
  local copies, waits for them, and re-layouts  3.64 us (3%)
    all_to_all x7, blocking collectives, exchange(): return lax.all_to_all(array, axes, 0, 0, tiled=True)  95 us
    all_gather x1, blocking collectives, body(): part = lax.all_gather(part, 'x', axis=0, tiled=True)  11.9 us
    ppermute x1, starting transfers between devices, body(): other = lax.ppermute(part, 'c', [(0, 1), (1, 0)])  9.52 us
    ppermute x1, starting transfers between devices, body(): beside = lax.ppermute(local, DOM, cores)  4.87 us
    ppermute x1, starting transfers between devices, body(): across = lax.ppermute(local, DOM, chips)  4.59 us
    pallas_call x1, Pallas kernels, body(): pl.pallas_call(backward_kernel, out_shape=jax.ShapeDtypeStruct((FLAT, LAN...  3.34 us
    pallas_call x1, Pallas kernels, body(): pl.pallas_call(forward_kernel, out_shape=(jax.ShapeDtypeStruct((C, 4 * LO...  2.85 us
  transfers between devices with their start and end apart: 3, of which 1 were waited for; matrix products, arithmetic and copies ran while one was open for 2% of the time, Pallas kernels for 0%

profile of v6, /device:TPU:1, one launch (start us, length us, event | category | flops | bytes accessed | tf_op | source)
XLA Modules:
  0.0 141.1 jit_solution(16522366759541864269)
XLA Ops:
  0.6 0.0 copy-start.1
  0.6 0.0 copy-start
  0.7 1.1 copy.9
  1.8 4.6 %collective-permute-start = (bf16[256,512]{1,0:T(8,128)(2,1)S(1)}, bf16[256,512]{1,0:T(8,128)(2,1)S(1)}, u32[]{:S(2)}, u32[]{:S(2)}) collective-permute-start(bf16[256,512]{1,0:T(8,128)(2,1)S(1)} %bitcast.26), channel_id=1, source_target_pairs={{1,2},{3,4},{5,6},{7,8},{9,10},{11,12},{13,14},{15,16},{17,18},{19... | collective-permute-start | bytes 786440 | tf_op jit(solution)/shard_map/ppermute | solution.py:272
  6.4 4.9 %collective-permute-start.1 = (bf16[256,512]{1,0:T(8,128)(2,1)S(1)}, bf16[256,512]{1,0:T(8,128)(2,1)S(1)}, u32[]{:S(2)}, u32[]{:S(2)}) collective-permute-start(bf16[256,512]{1,0:T(8,128)(2,1)S(1)} %bitcast.27), channel_id=1, source_target_pairs={{0,1},{1,0},{2,3},{3,2},{4,5},{5,4},{6,7},{7,6},{8,9},{9,8},{10,11... | collective-permute-start | bytes 786440 | tf_op jit(solution)/shard_map/ppermute | solution.py:273
  11.3 0.7 copy.11
  12.0 1.0 pad.7
  13.0 0.0 copy-done.1
  13.0 0.0 copy-done
  13.0 0.4 shard_map.84
  13.5 0.1 add_convert_fusion.ends
  13.5 0.0 collective-permute-done.across
  13.5 0.0 collective-permute-done.1.beside
  13.6 2.8 %shard_map.85 = (bf16[256,1024]{1,0:T(8,128)(2,1)S(1)}, f32[256,1024]{1,0:T(8,128)S(1)}, f32[100,512]{1,0:T(8,128)S(1)}, bf16[128,512]{1,0:T(8,128)(2,1)S(1)}) custom-call(s32[1]{0:T(128)} %bitcast.7.core, f32[2]{0:T(128)S(1)} %add_convert_fusion.ends, bf16[256,512]{1,0:T(8,128)(2,1)S(1)} %collective-permute-done.across, bf16[256,512]{1,0:T(8,128)(2,1)S(1)} %bitcast.28, ...), custom_call_target="tpu_custom_call" | custom-call | tf_op jit(solution)/shard_map/pallas_call | solution.py:303
  16.4 15.7 %all_to_all.35.refs_1_ = bf16[8,16,512]{2,1,0:T(8,128)(2,1)S(1)} all-to-all(bf16[8,16,512]{2,1,0:T(8,128)(2,1)S(1)} %bitcast.33), channel_id=1, replica_groups=mesh['x'=4,'yh'=2,'z'=8,'yl'=4,'c'=2] {'x','yh'}, dimensions={0} | all-to-all | bytes 262144 | tf_op jit(solution)/shard_map/all_to_all | solution.py:258
  32.1 1.1 shard_map.86
  33.2 11.8 %all_to_all.36 = bf16[8,16,512]{2,1,0:T(8,128)(2,1)S(1)} all-to-all(bf16[8,16,512]{2,1,0:T(8,128)(2,1)S(1)} %get-tuple-element.38), channel_id=1, replica_groups=mesh['x'=4,'yh'=2,'z'=8,'yl'=4,'c'=2] {'x','yh'}, dimensions={0} | all-to-all | bytes 262144 | tf_op jit(solution)/shard_map/all_to_all | solution.py:258
  45.0 3.3 %shard_map.87 = bf16[6656,128]{1,0:T(8,128)(2,1)S(1)} custom-call(s32[1]{0:T(128)} %bitcast.7.core, f32[1,1]{1,0:T(1,128)} %get-tuple-element.37.loss, bf16[128,512]{1,0:T(8,128)(2,1)S(1)} %bitcast.32, bf16[3,256,336]{2,1,0:T(8,128)(2,1)S(1)} %get-tuple-element.39.w_back, f32[256,1024]{1,0:T(8,128)S(1)} %get-tuple-element.40.slope, ...), custom_call_target="tpu_custom_call" | custom-call | tf_op jit(solution)/shard_map/pallas_call | solution.py:330
  48.4 6.9 %all_to_all.37.refs_1_ = bf16[2,3328,128]{2,1,0:T(8,128)(2,1)S(1)} all-to-all(bf16[2,3328,128]{2,1,0:T(8,128)(2,1)S(1)} %bitcast.24), channel_id=1, replica_groups=mesh['x'=4,'yh'=2,'z'=8,'yl'=4,'c'=2] {'c'}, dimensions={0} | all-to-all | bytes 3407872 | tf_op jit(solution)/shard_map/all_to_all | solution.py:258
  55.3 0.2 shard_map.88
  55.5 14.8 %all_to_all.38.refs_1_ = bf16[4,832,128]{2,1,0:T(8,128)(2,1)S(1)} all-to-all(bf16[4,832,128]{2,1,0:T(8,128)(2,1)S(1)} %bitcast.25), channel_id=1, replica_groups=mesh['x'=4,'yh'=2,'z'=8,'yl'=4,'c'=2] {'x'}, dimensions={0} | all-to-all | bytes 1703936 | tf_op jit(solution)/shard_map/all_to_all | solution.py:258
  70.3 0.1 shard_map.89
  70.4 15.5 %all_to_all.39.refs_1_ = bf16[8,104,128]{2,1,0:T(8,128)(2,1)S(1)} all-to-all(bf16[8,104,128]{2,1,0:T(8,128)(2,1)S(1)} %bitcast.31), channel_id=1, replica_groups=mesh['x'=4,'yh'=2,'z'=8,'yl'=4,'c'=2] {'yh','yl'}, dimensions={0} | all-to-all | bytes 425984 | tf_op jit(solution)/shard_map/all_to_all | solution.py:258
  86.0 18.7 %all_to_all.40.refs_1_ = bf16[8,104,128]{2,1,0:T(8,128)(2,1)S(1)} all-to-all(bf16[8,104,128]{2,1,0:T(8,128)(2,1)S(1)} %shard_map.90), channel_id=1, replica_groups=mesh['x'=4,'yh'=2,'z'=8,'yl'=4,'c'=2] {'z'}, dimensions={0} | all-to-all | bytes 425984 | tf_op jit(solution)/shard_map/all_to_all | solution.py:258
  104.7 11.5 %all_to_all.41 = bf16[8,104,128]{2,1,0:T(8,128)(2,1)S(1)} all-to-all(bf16[8,104,128]{2,1,0:T(8,128)(2,1)S(1)} %shard_map.91), channel_id=1, replica_groups=mesh['x'=4,'yh'=2,'z'=8,'yl'=4,'c'=2] {'yh','yl'}, dimensions={0} | all-to-all | bytes 425984 | tf_op jit(solution)/shard_map/all_to_all | solution.py:258
  116.2 11.9 %all_gather.3.own = bf16[3328,128]{1,0:T(8,128)(2,1)S(1)} all-gather(bf16[832,128]{1,0:T(8,128)(2,1)S(1)} %bitcast.37), channel_id=1, replica_groups=mesh['x'=4,'yh'=2,'z'=8,'yl'=4,'c'=2] {'x'}, dimensions={0}, use_global_device_ids=true | all-gather | bytes 1064960 | tf_op jit(solution)/shard_map/all_gather | solution.py:349
  128.1 9.5 %collective-permute-start.2 = (bf16[3328,128]{1,0:T(8,128)(2,1)S(1)}, bf16[3328,128]{1,0:T(8,128)(2,1)S(1)}, u32[]{:S(2)}, u32[]{:S(2)}) collective-permute-start(bf16[3328,128]{1,0:T(8,128)(2,1)S(1)} %all_gather.3.own), channel_id=1, source_target_pairs={{0,1},{1,0},{2,3},{3,2},{4,5},{5,4},{6,7},{7,6},{8,9},{9,8},{10,11... | collective-permute-start | bytes 2555912 | tf_op jit(solution)/shard_map/ppermute | solution.py:350
  137.7 0.8 reshape.86
  138.5 1.2 collective-permute-done.2.other
  139.7 1.5 %shard_map.92 = (bf16[256,2304]{1,0:T(8,128)(2,1)}, bf16[100,2304]{1,0:T(8,128)(2,1)}, f32[1,1]{1,0:T(1,128)}) custom-call(s32[1]{0:T(128)} %bitcast.7.core, bf16[3328,128]{1,0:T(8,128)(2,1)S(1)} %all_gather.3.own, bf16[3328,128]{1,0:T(8,128)(2,1)S(1)} %collective-permute-done.2.other), custom_call_target="tpu_custom_call" | custom-call | tf_op jit(solution)/shard_map/pallas_call | solution.py:352
  (4 shorter events, 0.1 us)
Async XLA Ops:
  0.6 12.4 %copy-start.1 = (bf16[100,2304]{1,0:T(8,128)(2,1)S(1)}, bf16[100,2304]{1,0:T(8,128)(2,1)}, u32[]{:S(2)}) copy-start(bf16[100,2304]{1,0:T(8,128)(2,1)} %w2.1) | copy-start | bytes 1382404
  0.6 12.4 %copy-start = (bf16[256,2304]{1,0:T(8,128)(2,1)S(1)}, bf16[256,2304]{1,0:T(8,128)(2,1)}, u32[]{:S(2)}) copy-start(bf16[256,2304]{1,0:T(8,128)(2,1)} %w1.1) | copy-start | bytes 3538948
  1.8 11.8 %collective-permute-start = (bf16[256,512]{1,0:T(8,128)(2,1)S(1)}, bf16[256,512]{1,0:T(8,128)(2,1)S(1)}, u32[]{:S(2)}, u32[]{:S(2)}) collective-permute-start(bf16[256,512]{1,0:T(8,128)(2,1)S(1)} %bitcast.26), channel_id=1, source_target_pairs={{1,2},{3,4},{5,6},{7,8},{9,10},{11,12},{13,14},{15,16},{17,18},{19... | collective-permute-start | bytes 786440 | tf_op jit(solution)/shard_map/ppermute | solution.py:272
  6.4 7.2 %collective-permute-start.1 = (bf16[256,512]{1,0:T(8,128)(2,1)S(1)}, bf16[256,512]{1,0:T(8,128)(2,1)S(1)}, u32[]{:S(2)}, u32[]{:S(2)}) collective-permute-start(bf16[256,512]{1,0:T(8,128)(2,1)S(1)} %bitcast.27), channel_id=1, source_target_pairs={{0,1},{1,0},{2,3},{3,2},{4,5},{5,4},{6,7},{7,6},{8,9},{9,8},{10,11... | collective-permute-start | bytes 786440 | tf_op jit(solution)/shard_map/ppermute | solution.py:273
  128.1 11.5 %collective-permute-start.2 = (bf16[3328,128]{1,0:T(8,128)(2,1)S(1)}, bf16[3328,128]{1,0:T(8,128)(2,1)S(1)}, u32[]{:S(2)}, u32[]{:S(2)}) collective-permute-start(bf16[3328,128]{1,0:T(8,128)(2,1)S(1)} %all_gather.3.own), channel_id=1, source_target_pairs={{0,1},{1,0},{2,3},{3,2},{4,5},{5,4},{6,7},{7,6},{8,9},{9,8},{10,11... | collective-permute-start | bytes 2555912 | tf_op jit(solution)/shard_map/ppermute | solution.py:350

commit v7 on v6

--- a/solution.py
+++ b/solution.py
@@ -25,7 +25,8 @@
 ROWS = 2
 CELLS = ROWS * LON
 MEMBERS = 8
-SHARE = 16
+FIRST = 48
+SHARE = 56
 VPAD = 112
 TAPS = 9
 LANES = 128
@@ -106,9 +107,7 @@
         if i == wide - 1:
             steep = steep * ends[1]
         slope[:, lanes] = steep
-    top = V // 16 * 16
-    sent[top:, :] = jnp.zeros((MEMBERS * SHARE - top, CELLS), BF16)
-    spare = jnp.zeros((VPAD - V, LON), F32)
+    spare = jnp.zeros((FIRST + SHARE - V, LON), F32)
     for i in range(ROWS):
         total = None
         for b in range(3):
@@ -121,15 +120,21 @@
             total = part if total is None else total + part
         lanes = slice(i * LON, (i + 1) * LON)
         outlook[:, lanes] = total
-        sent[:VPAD, lanes] = jnp.concatenate([total, spare], axis=0).astype(BF16)
+        padded = jnp.concatenate([total, spare], axis=0)
+        for part in range(2):
+            tile = padded[:, part * LANES : (part + 1) * LANES]
+            sent[2 * i + part] = tile[:SHARE].astype(BF16)
+            sent[4 + 2 * i + part] = tile[FIRST:].astype(BF16)
 
 
 def score_kernel(points, me, every, obs, land, errors, loss):
-    area = 1.0 + LAND_WEIGHT * land[...].astype(F32)
+    half = me[0] // 4
+    cells = pl.ds(pl.multiple_of(me[0] % 4 * LANES, LANES), LANES)
+    area = 1.0 + LAND_WEIGHT * land[:, cells].astype(F32)
     x = [every[p].astype(F32) for p in range(MEMBERS)]
-    truth = obs[me[0]]
+    truth = obs[pl.ds(pl.multiple_of(half * FIRST, FIRST), SHARE), cells]
     count = MEMBERS * (MEMBERS - 1)
-    skill = pairs = jnp.zeros((SHARE, CELLS), F32)
+    skill = pairs = jnp.zeros((SHARE, LANES), F32)
     slopes = []
     for p in range(MEMBERS):
         d = x[p] - truth
@@ -146,9 +151,9 @@
             s = d * inverse * (1.0 / count)
             slopes[p] = slopes[p] - s
             slopes[q] = slopes[q] + s
-    variable = me[0] * SHARE + lax.broadcasted_iota(jnp.int32, (SHARE, CELLS), 0)
+    variable = lax.broadcasted_iota(jnp.int32, (SHARE, LANES), 0)
     crps = area * (skill * (1.0 / MEMBERS) - pairs * (1.0 / count))
-    crps = jnp.where(variable < V, crps, 0.0)
+    crps = jnp.where(variable < jnp.where(half == 0, FIRST, V - FIRST), crps, 0.0)
     loss[...] = jnp.sum(crps, axis=(0, 1), keepdims=True) * (1.0 / points)
     factor = area * (LOSS_SCALE / points)
     for p in range(MEMBERS):
@@ -156,7 +161,7 @@
 
 
 def backward_kernel(
-    core, loss, err, w_back, slope, hidden, across, local, beside, out, e, pg, trunk
+    core, loss, err, w_back, slope, hidden, across, local, beside, theirs, e, pg, trunk
 ):
     trunk[:, 2 * LON : 4 * LON] = local[...]
 
@@ -166,7 +171,12 @@
 
     by_side(core, across, beside, fill)
     for i in range(ROWS):
-        row = err[:VPAD, i * LON : (i + 1) * LON].astype(F32)
+        spare = jnp.zeros((VPAD - FIRST - SHARE, LANES), F32)
+        tiles = []
+        for tile in (2 * i, 2 * i + 1):
+            lower, upper = err[tile].astype(F32)[:FIRST], err[4 + tile].astype(F32)
+            tiles.append(jnp.concatenate([lower, upper, spare], axis=0))
+        row = jnp.concatenate(tiles, axis=1)
         for b in range(3):
             e[b * VPAD : (b + 1) * VPAD, i * LON : (i + 1) * LON] = turn(row, b - 1).astype(BF16)
     wide = ROWS + 2
@@ -180,46 +190,72 @@
         grad = back * slope[:, lanes]
         for b in range(3):
             pg[b * C : (b + 1) * C, lanes] = turn(grad, b - 1).astype(BF16)
+    pl.when(core[0] == 0)(lambda: lower_half(loss, hidden, e, pg, trunk, theirs))
+    pl.when(core[0] == 1)(lambda: upper_half(pg, trunk, theirs))
+
+
+def own_half_kernel(core, loss, hidden, e, pg, trunk, mine):
+    pl.when(core[0] == 0)(lambda: upper_half(pg, trunk, mine))
+    pl.when(core[0] == 1)(lambda: lower_half(loss, hidden, e, pg, trunk, mine))
+
+
+def first_tiles(pg, trunk, tiles, out, start):
+    a = tiles[0] // 6
+    window = trunk[:, a * LON : (a + ROWS + 2) * LON]
+    head, tail = tiles[0] % 6 // 2, tiles[-1] % 6 // 2
+    both = lax.dot_general(
+        pg[head * C : (tail + 1) * C, :], window, NT, preferred_element_type=F32
+    )
+    for tile in tiles:
+        b, part = tile % 6 // 2 - head, tile % 2
+        value = both[b * C : (b + 1) * C, part * LANES : (part + 1) * LANES]
+        out[tile * C - start : (tile + 1) * C - start, :] = value.astype(BF16)
+
+
+def upper_half(pg, trunk, out):
+    for tiles in (range(6), range(6, 12), range(12, 13)):
+        first_tiles(pg, trunk, tiles, out, 0)
+
+
+def lower_half(loss, hidden, e, pg, trunk, out):
+    first_tiles(pg, trunk, range(13, 18), out, HALF)
     for a in range(3):
-        window = trunk[:, a * LON : (a + wide) * LON]
-        for b in range(3):
-            first = lax.dot_general(
-                pg[b * C : (b + 1) * C, :], window, NT, preferred_element_type=F32
-            ).astype(BF16)
-            second = lax.dot_general(
-                e[b * VPAD : (b + 1) * VPAD, :],
-                hidden[:, a * LON : a * LON + CELLS],
-                NT,
-                preferred_element_type=F32,
-            ).astype(BF16)
+        reach = hidden[:, a * LON : a * LON + CELLS]
+        seconds = lax.dot_general(e[...], reach, NT, preferred_element_type=F32)
+        for b in range(3):
+            second = seconds[b * VPAD : (b + 1) * VPAD].astype(BF16)
             for part in range(2):
-                tile = 2 * (3 * a + b) + part
-                lanes = slice(part * LANES, (part + 1) * LANES)
-                out[tile * C : (tile + 1) * C, :] = first[:, lanes]
-                at = SECOND + tile * VPAD
-                out[at : at + VPAD, :] = second[:, lanes]
+                at = SECOND + (2 * (3 * a + b) + part) * VPAD - HALF
+                out[at : at + VPAD, :] = second[:, part * LANES : (part + 1) * LANES]
     high, low = split(jnp.broadcast_to(loss[...], (1, LANES)))
-    out[LOSS:, :] = jnp.zeros((FLAT - LOSS, LANES), BF16)
-    row = lax.broadcasted_iota(jnp.int32, (16, LANES), 0)
-    both = jnp.where(row == 0, high.astype(F32), jnp.where(row == 1, low.astype(F32), 0.0))
-    out[LOSS : LOSS + 16, :] = both.astype(BF16)
-
-
-def sum_kernel(row, holder, parts, out):
-    total = parts[0].astype(F32)
-    for i in range(1, parts.shape[0]):
-        total = total + parts[i].astype(F32)
-    copies = out.shape[0]
-    value = total.astype(BF16)
+    index = lax.broadcasted_iota(jnp.int32, (16, LANES), 0)
+    both = jnp.where(index == 0, high.astype(F32), jnp.where(index == 1, low.astype(F32), 0.0))
+    at = LOSS - HALF
+    out[at : at + 16, :] = both.astype(BF16)
+    out[at + 16 :, :] = jnp.zeros((HALF - at - 16, LANES), BF16)
+
+
+def sum_kernel(row, holder, *refs):
+    out = refs[-1]
+
+    def total(at, n):
+        value = None
+        for parts in refs[:-1]:
+            for i in range(parts.shape[0]):
+                term = parts[i, at : at + n].astype(F32)
+                value = term if value is None else value + term
+        return value
+
+    copies, size = out.shape[:2]
+    value = total(0, size).astype(BF16)
     for i in range(copies):
         out[i] = value
-    base = row // 16 * 16 if row + 16 <= total.shape[0] and row % 16 == 0 else 0
-    span = 16 if row % 16 == 0 else total.shape[0]
+    base, span = (row, 16) if row % 16 == 0 else (0, size)
 
     @pl.when(holder[0] == 1)
     def _():
-        here = total[base : base + span]
-        high, low = split(total[row : row + 1] + total[row + 1 : row + 2])
+        here = total(base, span)
+        high, low = split(here[row - base : row - base + 1] + here[row - base + 1 : row - base + 2])
         index = lax.broadcasted_iota(jnp.int32, (span, LANES), 0) + base
         fixed = jnp.where(index == row, high.astype(F32), here)
         fixed = jnp.where(index == row + 1, low.astype(F32), fixed)
@@ -227,15 +263,15 @@
             out[i, base : base + span, :] = fixed.astype(BF16)
 
 
-def summed(parts, row, holder, copies=1):
+def summed(row, holder, copies, *arrays):
     body = lambda *refs: sum_kernel(row, *refs)
     return pl.pallas_call(
         body,
-        out_shape=jax.ShapeDtypeStruct((copies,) + parts.shape[1:], BF16),
-        in_specs=[SMEM, VMEM],
+        out_shape=jax.ShapeDtypeStruct((copies,) + arrays[0].shape[1:], BF16),
+        in_specs=[SMEM] + [VMEM] * len(arrays),
         out_specs=VMEM,
         compiler_params=PARAMS,
-    )(holder, parts)
+    )(holder, *arrays)
 
 
 def last_kernel(core, own, other, first, second, loss):
@@ -283,8 +319,7 @@
         compiler_params=PARAMS,
     )(w_first, later_kernel_matrix)
     ends = jnp.stack([(dom > 0).astype(F32), (dom < dom_size - 1).astype(F32)])
-    obs = jnp.pad(observed_state.reshape(V, CELLS), ((0, MEMBERS * SHARE - V), (0, 0)))
-    obs = obs.reshape(MEMBERS, SHARE, CELLS)
+    obs = jnp.pad(observed_state.reshape(V, CELLS), ((0, FIRST + SHARE - V), (0, 0)))
     area = land.reshape(1, CELLS)
     me = lax.axis_index(ENS).reshape(1)
     stages = (("c", 2), ("x", 4), (Y, 8))
@@ -306,7 +341,7 @@
             jax.ShapeDtypeStruct((C, 4 * LON), BF16),
             jax.ShapeDtypeStruct((C, 4 * LON), F32),
             jax.ShapeDtypeStruct((V, CELLS), F32),
-            jax.ShapeDtypeStruct((MEMBERS * SHARE, CELLS), BF16),
+            jax.ShapeDtypeStruct((MEMBERS, SHARE, LANES), BF16),
         ),
         in_specs=[SMEM] * 2 + [VMEM] * 5,
         out_specs=(VMEM,) * 4,
@@ -314,40 +349,52 @@
         compiler_params=PARAMS,
     )(core, ends, across, local, beside, w1, w2)
 
-    every = exchange(sent.reshape(MEMBERS, SHARE, CELLS), ENS)
+    every = exchange(sent, ENS)
     errors, loss = pl.pallas_call(
         lambda *refs: score_kernel(points, *refs),
         out_shape=(
-            jax.ShapeDtypeStruct((MEMBERS, SHARE, CELLS), BF16),
+            jax.ShapeDtypeStruct((MEMBERS, SHARE, LANES), BF16),
             jax.ShapeDtypeStruct((1, 1), F32),
         ),
         in_specs=[SMEM] + [VMEM] * 3,
         out_specs=(VMEM,) * 2,
         compiler_params=PARAMS,
     )(me, every, obs, area)
-    errors = exchange(errors, ENS).reshape(MEMBERS * SHARE, CELLS)
-
-    flat = pl.pallas_call(
+    errors = exchange(errors, ENS)
+
+    theirs, e, pg, trunk = pl.pallas_call(
         backward_kernel,
-        out_shape=jax.ShapeDtypeStruct((FLAT, LANES), BF16),
+        out_shape=(
+            jax.ShapeDtypeStruct((HALF, LANES), BF16),
+            jax.ShapeDtypeStruct((3 * VPAD, CELLS), BF16),
+            jax.ShapeDtypeStruct((3 * C, 4 * LON), BF16),
+            jax.ShapeDtypeStruct((C, 6 * LON), BF16),
+        ),
         in_specs=[SMEM] + [VMEM] * 8,
+        out_specs=(VMEM,) * 4,
+        compiler_params=PARAMS,
+    )(core, loss, errors, w_back, slope, hidden, across, local, beside)
+    mine = pl.pallas_call(
+        own_half_kernel,
+        out_shape=jax.ShapeDtypeStruct((HALF, LANES), BF16),
+        in_specs=[SMEM] + [VMEM] * 5,
         out_specs=VMEM,
-        scratch_shapes=[
-            pltpu.VMEM((3 * VPAD, CELLS), BF16),
-            pltpu.VMEM((3 * C, 4 * LON), BF16),
-            pltpu.VMEM((C, 6 * LON), BF16),
-        ],
-        compiler_params=PARAMS,
-    )(core, loss, errors, w_back, slope, hidden, across, local, beside)
-
-    part = flat
+        compiler_params=PARAMS,
+    )(core, loss, hidden, e, pg, trunk)
+
+    swap = [(0, 1), (1, 0)]
+    theirs = lax.ppermute(theirs, "c", swap)
+    part = None
     for (axes, n), flag, (row, size) in zip(stages, flags, places):
-        part = exchange(part.reshape(n, size, LANES), axes)
-        part = summed(part, row, flag, 8 if axes == Y else 1)
-    part = summed(exchange(part, "z"), row, flag, 8)
+        if part is None:
+            part = summed(row, flag, 1, mine[None], theirs[None])
+        else:
+            part = exchange(part.reshape(n, size, LANES), axes)
+            part = summed(row, flag, 8 if axes == Y else 1, part)
+    part = summed(row, flag, 8, exchange(part, "z"))
     part = exchange(part, Y).reshape(8 * size, LANES)
     part = lax.all_gather(part, "x", axis=0, tiled=True)
-    other = lax.ppermute(part, "c", [(0, 1), (1, 0)])
+    other = lax.ppermute(part, "c", swap)
     other, outlook = lax.optimization_barrier((other, outlook.reshape(1, V, ROWS, LON)))
     first, second, loss = pl.pallas_call(
         last_kernel,

time: 142 us -> 140 us (0.986)
  blocking collectives: 107 us -> 99.6 us
  starting transfers between devices: 19 us -> 23.1 us
    all_to_all x7 -> x6, blocking collectives: 95 us -> 87.7 us  [exchange(): return lax.all_to_all(array, axes, 0, 0, tiled=True)]
    ppermute x1 -> x2, starting transfers between devices: 9.52 us -> 13.7 us  [the longest x1 9.52 us: body(): other = lax.ppermute(part, 'c', swap)]
    pallas_call x5 -> x6, Pallas kernels: 3.72 us -> 4.74 us  [the longest x1 2.81 us: body(): pl.pallas_call(backward_kernel, out_shape=(jax.ShapeDtypeStruct((HALF, LA...]
  transfers between devices with their start and end apart: 3 -> 4, of which waited for: 1 -> 2; matrix products, arithmetic and copies ran while one was open for 2% -> 2% of each run, Pallas kernels for 0% -> 1%
where the time goes in v7:
time: 140 us; the launch traced here: 139 us
  blocking collectives  99.6 us (71%)
  starting transfers between devices  23.1 us (16%)
  Pallas kernels  10.5 us (8%)
  local copies, waits for them, and re-layouts  3.64 us (3%)
  waiting for transfers between devices  1.6 us (1%)
    all_to_all x6, blocking collectives, exchange(): return lax.all_to_all(array, axes, 0, 0, tiled=True)  87.7 us
    all_gather x1, blocking collectives, body(): part = lax.all_gather(part, 'x', axis=0, tiled=True)  11.9 us
    ppermute x1, starting transfers between devices, body(): other = lax.ppermute(part, 'c', swap)  9.52 us
    ppermute x1, starting transfers between devices, body(): beside = lax.ppermute(local, DOM, cores)  4.87 us
    ppermute x1, starting transfers between devices, body(): across = lax.ppermute(local, DOM, chips)  4.59 us
    ppermute x1, starting transfers between devices, body(): theirs = lax.ppermute(theirs, 'c', swap)  4.13 us
    pallas_call x1, Pallas kernels, body(): pl.pallas_call(forward_kernel, out_shape=(jax.ShapeDtypeStruct((C, 4 * LO...  2.85 us
    unnamed x8, local copies, waits for them, and re-layouts  2.82 us
  transfers between devices with their start and end apart: 4, of which 2 were waited for; matrix products, arithmetic and copies ran while one was open for 2% of the time, Pallas kernels for 1%

profile of v7, /device:TPU:1, one launch (start us, length us, event | category | flops | bytes accessed | tf_op | source)
XLA Modules:
  0.0 139.3 jit_solution(17638614124379013610)
XLA Ops:
  0.6 0.0 copy-start.1
  0.6 0.0 copy-start
  0.7 1.1 copy.9
  1.8 4.6 %collective-permute-start = (bf16[256,512]{1,0:T(8,128)(2,1)S(1)}, bf16[256,512]{1,0:T(8,128)(2,1)S(1)}, u32[]{:S(2)}, u32[]{:S(2)}) collective-permute-start(bf16[256,512]{1,0:T(8,128)(2,1)S(1)} %bitcast.24), channel_id=1, source_target_pairs={{1,2},{3,4},{5,6},{7,8},{9,10},{11,12},{13,14},{15,16},{17,18},{19... | collective-permute-start | bytes 786440 | tf_op jit(solution)/shard_map/ppermute | solution.py:308
  6.4 4.9 %collective-permute-start.1 = (bf16[256,512]{1,0:T(8,128)(2,1)S(1)}, bf16[256,512]{1,0:T(8,128)(2,1)S(1)}, u32[]{:S(2)}, u32[]{:S(2)}) collective-permute-start(bf16[256,512]{1,0:T(8,128)(2,1)S(1)} %bitcast.25), channel_id=1, source_target_pairs={{0,1},{1,0},{2,3},{3,2},{4,5},{5,4},{6,7},{7,6},{8,9},{9,8},{10,11... | collective-permute-start | bytes 786440 | tf_op jit(solution)/shard_map/ppermute | solution.py:309
  11.3 0.7 copy.11
  12.0 1.0 pad.7
  13.0 0.0 copy-done.1
  13.0 0.0 copy-done
  13.0 0.4 shard_map.84
  13.5 0.1 add_convert_fusion.ends
  13.5 0.0 collective-permute-done.across
  13.5 0.0 collective-permute-done.1.beside
  13.5 2.9 %shard_map.85 = (bf16[256,1024]{1,0:T(8,128)(2,1)S(1)}, f32[256,1024]{1,0:T(8,128)S(1)}, f32[100,512]{1,0:T(8,128)S(1)}, bf16[8,56,128]{2,1,0:T(8,128)(2,1)S(1)}) custom-call(s32[1]{0:T(128)} %bitcast.6.core, f32[2]{0:T(128)S(1)} %add_convert_fusion.ends, bf16[256,512]{1,0:T(8,128)(2,1)S(1)} %collective-permute-done.across, bf16[256,512]{1,0:T(8,128)(2,1)S(1)} %bitcast.26, ...), custom_call_target="tpu_custom_call" | custom-call | tf_op jit(solution)/shard_map/pallas_call | solution.py:338
  16.4 15.3 %all_to_all.30.refs_1_ = bf16[8,56,128]{2,1,0:T(8,128)(2,1)S(1)} all-to-all(bf16[8,56,128]{2,1,0:T(8,128)(2,1)S(1)} %get-tuple-element.38), channel_id=1, replica_groups=mesh['x'=4,'yh'=2,'z'=8,'yl'=4,'c'=2] {'x','yh'}, dimensions={0} | all-to-all | bytes 229376 | tf_op jit(solution)/shard_map/all_to_all | solution.py:294
  31.7 1.0 shard_map.86
  32.7 11.8 %all_to_all.31.err = bf16[8,56,128]{2,1,0:T(8,128)(2,1)S(1)} all-to-all(bf16[8,56,128]{2,1,0:T(8,128)(2,1)S(1)} %get-tuple-element.43), channel_id=1, replica_groups=mesh['x'=4,'yh'=2,'z'=8,'yl'=4,'c'=2] {'x','yh'}, dimensions={0} | all-to-all | bytes 229376 | tf_op jit(solution)/shard_map/all_to_all | solution.py:294
  44.5 2.8 %shard_map.87 = (bf16[3328,128]{1,0:T(8,128)(2,1)S(1)}, bf16[336,512]{1,0:T(8,128)(2,1)S(1)}, bf16[768,1024]{1,0:T(8,128)(2,1)S(1)}, bf16[256,1536]{1,0:T(8,128)(2,1)S(1)}) custom-call(s32[1]{0:T(128)} %bitcast.6.core, f32[1,1]{1,0:T(1,128)} %get-tuple-element.41.loss, bf16[8,56,128]{2,1,0:T(8,128)(2,1)S(1)} %all_to_all.31.err, ...), custom_call_target="tpu_custom_call" | custom-call | tf_op jit(solution)/shard_map/pallas_call | solution.py:365
  47.3 4.1 %collective-permute-start.2 = (bf16[3328,128]{1,0:T(8,128)(2,1)S(1)}, bf16[3328,128]{1,0:T(8,128)(2,1)S(1)}, u32[]{:S(2)}, u32[]{:S(2)}) collective-permute-start(bf16[3328,128]{1,0:T(8,128)(2,1)S(1)} %get-tuple-element.49), channel_id=1, source_target_pairs={{0,1},{1,0},{2,3},{3,2},{4,5},{5,4},{6,7},{7,6},{8,9},{9,8},{10,11... | collective-permute-start | bytes 2555912 | tf_op jit(solution)/shard_map/ppermute | solution.py:386
  51.4 1.6 %shard_map.88 = bf16[3328,128]{1,0:T(8,128)(2,1)S(1)} custom-call(s32[1]{0:T(128)} %bitcast.6.core, f32[1,1]{1,0:T(1,128)} %get-tuple-element.41.loss, bf16[256,1024]{1,0:T(8,128)(2,1)S(1)} %get-tuple-element.42.hidden, bf16[336,512]{1,0:T(8,128)(2,1)S(1)} %get-tuple-element.46.e, bf16[768,1024]{1,0:T(8,128)(2,1)S(1)} %get-tuple-element.47.pg, ...), custom_call_target="tpu_custom_call" | custom-call | tf_op jit(solution)/shard_map/pallas_call | solution.py:377
  53.0 0.4 collective-permute-done.2
  53.4 0.2 shard_map.89
  53.6 14.8 %all_to_all.32.refs_1_ = bf16[4,832,128]{2,1,0:T(8,128)(2,1)S(1)} all-to-all(bf16[4,832,128]{2,1,0:T(8,128)(2,1)S(1)} %bitcast.23), channel_id=1, replica_groups=mesh['x'=4,'yh'=2,'z'=8,'yl'=4,'c'=2] {'x'}, dimensions={0} | all-to-all | bytes 1703936 | tf_op jit(solution)/shard_map/all_to_all | solution.py:294
  68.5 0.1 shard_map.90
  68.6 15.3 %all_to_all.33.refs_1_ = bf16[8,104,128]{2,1,0:T(8,128)(2,1)S(1)} all-to-all(bf16[8,104,128]{2,1,0:T(8,128)(2,1)S(1)} %bitcast.29), channel_id=1, replica_groups=mesh['x'=4,'yh'=2,'z'=8,'yl'=4,'c'=2] {'yh','yl'}, dimensions={0} | all-to-all | bytes 425984 | tf_op jit(solution)/shard_map/all_to_all | solution.py:294
  83.9 19.0 %all_to_all.34.refs_1_ = bf16[8,104,128]{2,1,0:T(8,128)(2,1)S(1)} all-to-all(bf16[8,104,128]{2,1,0:T(8,128)(2,1)S(1)} %shard_map.91), channel_id=1, replica_groups=mesh['x'=4,'yh'=2,'z'=8,'yl'=4,'c'=2] {'z'}, dimensions={0} | all-to-all | bytes 425984 | tf_op jit(solution)/shard_map/all_to_all | solution.py:294
  102.9 11.5 %all_to_all.35 = bf16[8,104,128]{2,1,0:T(8,128)(2,1)S(1)} all-to-all(bf16[8,104,128]{2,1,0:T(8,128)(2,1)S(1)} %shard_map.92), channel_id=1, replica_groups=mesh['x'=4,'yh'=2,'z'=8,'yl'=4,'c'=2] {'yh','yl'}, dimensions={0} | all-to-all | bytes 425984 | tf_op jit(solution)/shard_map/all_to_all | solution.py:294
  114.4 11.9 %all_gather.3.own = bf16[3328,128]{1,0:T(8,128)(2,1)S(1)} all-gather(bf16[832,128]{1,0:T(8,128)(2,1)S(1)} %bitcast.33), channel_id=1, replica_groups=mesh['x'=4,'yh'=2,'z'=8,'yl'=4,'c'=2] {'x'}, dimensions={0}, use_global_device_ids=true | all-gather | bytes 1064960 | tf_op jit(solution)/shard_map/all_gather | solution.py:396
  126.3 9.5 %collective-permute-start.3 = (bf16[3328,128]{1,0:T(8,128)(2,1)S(1)}, bf16[3328,128]{1,0:T(8,128)(2,1)S(1)}, u32[]{:S(2)}, u32[]{:S(2)}) collective-permute-start(bf16[3328,128]{1,0:T(8,128)(2,1)S(1)} %all_gather.3.own), channel_id=1, source_target_pairs={{0,1},{1,0},{2,3},{3,2},{4,5},{5,4},{6,7},{7,6},{8,9},{9,8},{10,11... | collective-permute-start | bytes 2555912 | tf_op jit(solution)/shard_map/ppermute | solution.py:397
  135.9 0.8 reshape.70
  136.7 1.2 collective-permute-done.3.other
  137.9 1.5 %shard_map.93 = (bf16[256,2304]{1,0:T(8,128)(2,1)}, bf16[100,2304]{1,0:T(8,128)(2,1)}, f32[1,1]{1,0:T(1,128)}) custom-call(s32[1]{0:T(128)} %bitcast.6.core, bf16[3328,128]{1,0:T(8,128)(2,1)S(1)} %all_gather.3.own, bf16[3328,128]{1,0:T(8,128)(2,1)S(1)} %collective-permute-done.3.other), custom_call_target="tpu_custom_call" | custom-call | tf_op jit(solution)/shard_map/pallas_call | solution.py:399
  (4 shorter events, 0.1 us)
Async XLA Ops:
  0.6 12.4 %copy-start.1 = (bf16[100,2304]{1,0:T(8,128)(2,1)S(1)}, bf16[100,2304]{1,0:T(8,128)(2,1)}, u32[]{:S(2)}) copy-start(bf16[100,2304]{1,0:T(8,128)(2,1)} %w2.1) | copy-start | bytes 1382404
  0.6 12.4 %copy-start = (bf16[256,2304]{1,0:T(8,128)(2,1)S(1)}, bf16[256,2304]{1,0:T(8,128)(2,1)}, u32[]{:S(2)}) copy-start(bf16[256,2304]{1,0:T(8,128)(2,1)} %w1.1) | copy-start | bytes 3538948
  1.8 11.8 %collective-permute-start = (bf16[256,512]{1,0:T(8,128)(2,1)S(1)}, bf16[256,512]{1,0:T(8,128)(2,1)S(1)}, u32[]{:S(2)}, u32[]{:S(2)}) collective-permute-start(bf16[256,512]{1,0:T(8,128)(2,1)S(1)} %bitcast.24), channel_id=1, source_target_pairs={{1,2},{3,4},{5,6},{7,8},{9,10},{11,12},{13,14},{15,16},{17,18},{19... | collective-permute-start | bytes 786440 | tf_op jit(solution)/shard_map/ppermute | solution.py:308
  6.4 7.2 %collective-permute-start.1 = (bf16[256,512]{1,0:T(8,128)(2,1)S(1)}, bf16[256,512]{1,0:T(8,128)(2,1)S(1)}, u32[]{:S(2)}, u32[]{:S(2)}) collective-permute-start(bf16[256,512]{1,0:T(8,128)(2,1)S(1)} %bitcast.25), channel_id=1, source_target_pairs={{0,1},{1,0},{2,3},{3,2},{4,5},{5,4},{6,7},{7,6},{8,9},{9,8},{10,11... | collective-permute-start | bytes 786440 | tf_op jit(solution)/shard_map/ppermute | solution.py:309
  47.3 6.1 %collective-permute-start.2 = (bf16[3328,128]{1,0:T(8,128)(2,1)S(1)}, bf16[3328,128]{1,0:T(8,128)(2,1)S(1)}, u32[]{:S(2)}, u32[]{:S(2)}) collective-permute-start(bf16[3328,128]{1,0:T(8,128)(2,1)S(1)} %get-tuple-element.49), channel_id=1, source_target_pairs={{0,1},{1,0},{2,3},{3,2},{4,5},{5,4},{6,7},{7,6},{8,9},{9,8},{10,11... | collective-permute-start | bytes 2555912 | tf_op jit(solution)/shard_map/ppermute | solution.py:386
  126.3 11.5 %collective-permute-start.3 = (bf16[3328,128]{1,0:T(8,128)(2,1)S(1)}, bf16[3328,128]{1,0:T(8,128)(2,1)S(1)}, u32[]{:S(2)}, u32[]{:S(2)}) collective-permute-start(bf16[3328,128]{1,0:T(8,128)(2,1)S(1)} %all_gather.3.own), channel_id=1, source_target_pairs={{0,1},{1,0},{2,3},{3,2},{4,5},{5,4},{6,7},{7,6},{8,9},{9,8},{10,11... | collective-permute-start | bytes 2555912 | tf_op jit(solution)/shard_map/ppermute | solution.py:397

commit v8 on v7

--- a/solution.py
+++ b/solution.py
@@ -13,9 +13,10 @@
 GELU_B = 0.044715
 
 ENS = ("x", "yh")
-DOM = ("z", "yl", "c")
-Y = ("yh", "yl")
-PARTS = {"x": 4, "yh": 2, "z": 8, "yl": 4, "c": 2}
+DOM = ("zh", "zl", "yl", "c")
+Z = ("zl", "zh")
+Y = ("yl", "yh")
+PARTS = {"x": 4, "yh": 2, "zh": 2, "zl": 4, "yl": 4, "c": 2}
 F32 = jnp.float32
 BF16 = jnp.bfloat16
 
@@ -321,7 +322,7 @@
     ends = jnp.stack([(dom > 0).astype(F32), (dom < dom_size - 1).astype(F32)])
     obs = jnp.pad(observed_state.reshape(V, CELLS), ((0, FIRST + SHARE - V), (0, 0)))
     area = land.reshape(1, CELLS)
-    me = lax.axis_index(ENS).reshape(1)
+    me = lax.axis_index(("yh", "x")).reshape(1)
     stages = (("c", 2), ("x", 4), (Y, 8))
     holder = jnp.bool_(True)
     row, size = LOSS, FLAT
@@ -349,7 +350,7 @@
         compiler_params=PARAMS,
     )(core, ends, across, local, beside, w1, w2)
 
-    every = exchange(sent, ENS)
+    every = exchange(sent, ("yh", "x"))
     errors, loss = pl.pallas_call(
         lambda *refs: score_kernel(points, *refs),
         out_shape=(
@@ -360,7 +361,7 @@
         out_specs=(VMEM,) * 2,
         compiler_params=PARAMS,
     )(me, every, obs, area)
-    errors = exchange(errors, ENS)
+    errors = exchange(errors, ("yh", "x"))
 
     theirs, e, pg, trunk = pl.pallas_call(
         backward_kernel,
@@ -391,7 +392,7 @@
         else:
             part = exchange(part.reshape(n, size, LANES), axes)
             part = summed(row, flag, 8 if axes == Y else 1, part)
-    part = summed(row, flag, 8, exchange(part, "z"))
+    part = summed(row, flag, 8, exchange(part, Z))
     part = exchange(part, Y).reshape(8 * size, LANES)
     part = lax.all_gather(part, "x", axis=0, tiled=True)
     other = lax.ppermute(part, "c", swap)

time: 140 us -> 136 us (0.971)
  blocking collectives: 99.6 us -> 95.4 us
    all_to_all x6, blocking collectives: 87.7 us -> 83.6 us  [exchange(): return lax.all_to_all(array, axes, 0, 0, tiled=True)]
where the time goes in v8:
time: 136 us; the launch traced here: 135 us
  blocking collectives  95.4 us (70%)
  starting transfers between devices  23.1 us (17%)
  Pallas kernels  10.5 us (8%)
  local copies, waits for them, and re-layouts  3.64 us (3%)
  waiting for transfers between devices  1.6 us (1%)
    all_to_all x6, blocking collectives, exchange(): return lax.all_to_all(array, axes, 0, 0, tiled=True)  83.6 us
    all_gather x1, blocking collectives, body(): part = lax.all_gather(part, 'x', axis=0, tiled=True)  11.8 us
    ppermute x1, starting transfers between devices, body(): other = lax.ppermute(part, 'c', swap)  9.43 us
    ppermute x1, starting transfers between devices, body(): beside = lax.ppermute(local, DOM, cores)  4.87 us
    ppermute x1, starting transfers between devices, body(): across = lax.ppermute(local, DOM, chips)  4.59 us
    ppermute x1, starting transfers between devices, body(): theirs = lax.ppermute(theirs, 'c', swap)  4.16 us
    pallas_call x1, Pallas kernels, body(): pl.pallas_call(forward_kernel, out_shape=(jax.ShapeDtypeStruct((C, 4 * LO...  2.86 us
    unnamed x8, local copies, waits for them, and re-layouts  2.82 us
  transfers between devices with their start and end apart: 4, of which 2 were waited for; matrix products, arithmetic and copies ran while one was open for 2% of the time, Pallas kernels for 1%

profile of v8, /device:TPU:1, one launch (start us, length us, event | category | flops | bytes accessed | tf_op | source)
XLA Modules:
  0.0 135.1 jit_solution(10611967986837150073)
XLA Ops:
  0.6 0.0 copy-start.1
  0.6 0.0 copy-start
  0.7 1.1 copy.9
  1.8 4.6 %collective-permute-start = (bf16[256,512]{1,0:T(8,128)(2,1)S(1)}, bf16[256,512]{1,0:T(8,128)(2,1)S(1)}, u32[]{:S(2)}, u32[]{:S(2)}) collective-permute-start(bf16[256,512]{1,0:T(8,128)(2,1)S(1)} %bitcast.24), channel_id=1, source_target_pairs={{1,2},{3,4},{5,6},{7,8},{9,10},{11,12},{13,14},{15,16},{17,18},{19... | collective-permute-start | bytes 786440 | tf_op jit(solution)/shard_map/ppermute | solution.py:309
  6.4 4.9 %collective-permute-start.1 = (bf16[256,512]{1,0:T(8,128)(2,1)S(1)}, bf16[256,512]{1,0:T(8,128)(2,1)S(1)}, u32[]{:S(2)}, u32[]{:S(2)}) collective-permute-start(bf16[256,512]{1,0:T(8,128)(2,1)S(1)} %bitcast.25), channel_id=1, source_target_pairs={{0,1},{1,0},{2,3},{3,2},{4,5},{5,4},{6,7},{7,6},{8,9},{9,8},{10,11... | collective-permute-start | bytes 786440 | tf_op jit(solution)/shard_map/ppermute | solution.py:310
  11.3 0.7 copy.11
  12.0 1.0 pad.7
  13.0 0.0 copy-done.1
  13.0 0.0 copy-done
  13.0 0.4 shard_map.84
  13.5 0.1 add_convert_fusion.ends
  13.5 0.0 collective-permute-done.across
  13.5 0.0 collective-permute-done.1.beside
  13.6 2.9 %shard_map.85 = (bf16[256,1024]{1,0:T(8,128)(2,1)S(1)}, f32[256,1024]{1,0:T(8,128)S(1)}, f32[100,512]{1,0:T(8,128)S(1)}, bf16[8,56,128]{2,1,0:T(8,128)(2,1)S(1)}) custom-call(s32[1]{0:T(128)} %bitcast.6.core, f32[2]{0:T(128)S(1)} %add_convert_fusion.ends, bf16[256,512]{1,0:T(8,128)(2,1)S(1)} %collective-permute-done.across, bf16[256,512]{1,0:T(8,128)(2,1)S(1)} %bitcast.26, ...), custom_call_target="tpu_custom_call" | custom-call | tf_op jit(solution)/shard_map/pallas_call | solution.py:339
  16.4 15.2 %all_to_all.30.refs_1_ = bf16[8,56,128]{2,1,0:T(8,128)(2,1)S(1)} all-to-all(bf16[8,56,128]{2,1,0:T(8,128)(2,1)S(1)} %get-tuple-element.38), channel_id=1, replica_groups=mesh['x'=4,'yh'=2,'zh'=2,'zl'=4,'yl'=4,'c'=2] {'yh','x'}, dimensions={0} | all-to-all | bytes 229376 | tf_op jit(solution)/shard_map/all_to_all | solution.py:295
  31.6 1.0 shard_map.86
  32.6 11.7 %all_to_all.31.err = bf16[8,56,128]{2,1,0:T(8,128)(2,1)S(1)} all-to-all(bf16[8,56,128]{2,1,0:T(8,128)(2,1)S(1)} %get-tuple-element.43), channel_id=1, replica_groups=mesh['x'=4,'yh'=2,'zh'=2,'zl'=4,'yl'=4,'c'=2] {'yh','x'}, dimensions={0} | all-to-all | bytes 229376 | tf_op jit(solution)/shard_map/all_to_all | solution.py:295
  44.3 2.8 %shard_map.87 = (bf16[3328,128]{1,0:T(8,128)(2,1)S(1)}, bf16[336,512]{1,0:T(8,128)(2,1)S(1)}, bf16[768,1024]{1,0:T(8,128)(2,1)S(1)}, bf16[256,1536]{1,0:T(8,128)(2,1)S(1)}) custom-call(s32[1]{0:T(128)} %bitcast.6.core, f32[1,1]{1,0:T(1,128)} %get-tuple-element.41.loss, bf16[8,56,128]{2,1,0:T(8,128)(2,1)S(1)} %all_to_all.31.err, ...), custom_call_target="tpu_custom_call" | custom-call | tf_op jit(solution)/shard_map/pallas_call | solution.py:366
  47.1 4.2 %collective-permute-start.2 = (bf16[3328,128]{1,0:T(8,128)(2,1)S(1)}, bf16[3328,128]{1,0:T(8,128)(2,1)S(1)}, u32[]{:S(2)}, u32[]{:S(2)}) collective-permute-start(bf16[3328,128]{1,0:T(8,128)(2,1)S(1)} %get-tuple-element.49), channel_id=1, source_target_pairs={{0,1},{1,0},{2,3},{3,2},{4,5},{5,4},{6,7},{7,6},{8,9},{9,8},{10,11... | collective-permute-start | bytes 2555912 | tf_op jit(solution)/shard_map/ppermute | solution.py:387
  51.2 1.6 %shard_map.88 = bf16[3328,128]{1,0:T(8,128)(2,1)S(1)} custom-call(s32[1]{0:T(128)} %bitcast.6.core, f32[1,1]{1,0:T(1,128)} %get-tuple-element.41.loss, bf16[256,1024]{1,0:T(8,128)(2,1)S(1)} %get-tuple-element.42.hidden, bf16[336,512]{1,0:T(8,128)(2,1)S(1)} %get-tuple-element.46.e, bf16[768,1024]{1,0:T(8,128)(2,1)S(1)} %get-tuple-element.47.pg, ...), custom_call_target="tpu_custom_call" | custom-call | tf_op jit(solution)/shard_map/pallas_call | solution.py:378
  52.8 0.4 collective-permute-done.2
  53.2 0.2 shard_map.89
  53.4 14.8 %all_to_all.32.refs_1_ = bf16[4,832,128]{2,1,0:T(8,128)(2,1)S(1)} all-to-all(bf16[4,832,128]{2,1,0:T(8,128)(2,1)S(1)} %bitcast.23), channel_id=1, replica_groups=mesh['x'=4,'yh'=2,'zh'=2,'zl'=4,'yl'=4,'c'=2] {'x'}, dimensions={0} | all-to-all | bytes 1703936 | tf_op jit(solution)/shard_map/all_to_all | solution.py:295
  68.3 0.1 shard_map.90
  68.4 13.3 %all_to_all.33.refs_1_ = bf16[8,104,128]{2,1,0:T(8,128)(2,1)S(1)} all-to-all(bf16[8,104,128]{2,1,0:T(8,128)(2,1)S(1)} %bitcast.29), channel_id=1, replica_groups=mesh['x'=4,'yh'=2,'zh'=2,'zl'=4,'yl'=4,'c'=2] {'yl','yh'}, dimensions={0} | all-to-all | bytes 425984 | tf_op jit(solution)/shard_map/all_to_all | solution.py:295
  81.8 17.5 %all_to_all.34.refs_1_ = bf16[8,104,128]{2,1,0:T(8,128)(2,1)S(1)} all-to-all(bf16[8,104,128]{2,1,0:T(8,128)(2,1)S(1)} %shard_map.91), channel_id=1, replica_groups=mesh['x'=4,'yh'=2,'zh'=2,'zl'=4,'yl'=4,'c'=2] {'zl','zh'}, dimensions={0} | all-to-all | bytes 425984 | tf_op jit(solution)/shard_map/all_to_all | solution.py:295
  99.3 11.0 %all_to_all.35 = bf16[8,104,128]{2,1,0:T(8,128)(2,1)S(1)} all-to-all(bf16[8,104,128]{2,1,0:T(8,128)(2,1)S(1)} %shard_map.92), channel_id=1, replica_groups=mesh['x'=4,'yh'=2,'zh'=2,'zl'=4,'yl'=4,'c'=2] {'yl','yh'}, dimensions={0} | all-to-all | bytes 425984 | tf_op jit(solution)/shard_map/all_to_all | solution.py:295
  110.3 11.8 %all_gather.3.own = bf16[3328,128]{1,0:T(8,128)(2,1)S(1)} all-gather(bf16[832,128]{1,0:T(8,128)(2,1)S(1)} %bitcast.33), channel_id=1, replica_groups=mesh['x'=4,'yh'=2,'zh'=2,'zl'=4,'yl'=4,'c'=2] {'x'}, dimensions={0}, use_global_device_ids=true | all-gather | bytes 1064960 | tf_op jit(solution)/shard_map/all_gather | solution.py:397
  122.2 9.4 %collective-permute-start.3 = (bf16[3328,128]{1,0:T(8,128)(2,1)S(1)}, bf16[3328,128]{1,0:T(8,128)(2,1)S(1)}, u32[]{:S(2)}, u32[]{:S(2)}) collective-permute-start(bf16[3328,128]{1,0:T(8,128)(2,1)S(1)} %all_gather.3.own), channel_id=1, source_target_pairs={{0,1},{1,0},{2,3},{3,2},{4,5},{5,4},{6,7},{7,6},{8,9},{9,8},{10,11... | collective-permute-start | bytes 2555912 | tf_op jit(solution)/shard_map/ppermute | solution.py:398
  131.6 0.8 reshape.70
  132.4 1.2 collective-permute-done.3.other
  133.6 1.5 %shard_map.93 = (bf16[256,2304]{1,0:T(8,128)(2,1)}, bf16[100,2304]{1,0:T(8,128)(2,1)}, f32[1,1]{1,0:T(1,128)}) custom-call(s32[1]{0:T(128)} %bitcast.6.core, bf16[3328,128]{1,0:T(8,128)(2,1)S(1)} %all_gather.3.own, bf16[3328,128]{1,0:T(8,128)(2,1)S(1)} %collective-permute-done.3.other), custom_call_target="tpu_custom_call" | custom-call | tf_op jit(solution)/shard_map/pallas_call | solution.py:400
  (4 shorter events, 0.1 us)
Async XLA Ops:
  0.6 12.4 %copy-start.1 = (bf16[100,2304]{1,0:T(8,128)(2,1)S(1)}, bf16[100,2304]{1,0:T(8,128)(2,1)}, u32[]{:S(2)}) copy-start(bf16[100,2304]{1,0:T(8,128)(2,1)} %w2.1) | copy-start | bytes 1382404
  0.6 12.4 %copy-start = (bf16[256,2304]{1,0:T(8,128)(2,1)S(1)}, bf16[256,2304]{1,0:T(8,128)(2,1)}, u32[]{:S(2)}) copy-start(bf16[256,2304]{1,0:T(8,128)(2,1)} %w1.1) | copy-start | bytes 3538948
  1.8 11.8 %collective-permute-start = (bf16[256,512]{1,0:T(8,128)(2,1)S(1)}, bf16[256,512]{1,0:T(8,128)(2,1)S(1)}, u32[]{:S(2)}, u32[]{:S(2)}) collective-permute-start(bf16[256,512]{1,0:T(8,128)(2,1)S(1)} %bitcast.24), channel_id=1, source_target_pairs={{1,2},{3,4},{5,6},{7,8},{9,10},{11,12},{13,14},{15,16},{17,18},{19... | collective-permute-start | bytes 786440 | tf_op jit(solution)/shard_map/ppermute | solution.py:309
  6.4 7.2 %collective-permute-start.1 = (bf16[256,512]{1,0:T(8,128)(2,1)S(1)}, bf16[256,512]{1,0:T(8,128)(2,1)S(1)}, u32[]{:S(2)}, u32[]{:S(2)}) collective-permute-start(bf16[256,512]{1,0:T(8,128)(2,1)S(1)} %bitcast.25), channel_id=1, source_target_pairs={{0,1},{1,0},{2,3},{3,2},{4,5},{5,4},{6,7},{7,6},{8,9},{9,8},{10,11... | collective-permute-start | bytes 786440 | tf_op jit(solution)/shard_map/ppermute | solution.py:310
  47.1 6.1 %collective-permute-start.2 = (bf16[3328,128]{1,0:T(8,128)(2,1)S(1)}, bf16[3328,128]{1,0:T(8,128)(2,1)S(1)}, u32[]{:S(2)}, u32[]{:S(2)}) collective-permute-start(bf16[3328,128]{1,0:T(8,128)(2,1)S(1)} %get-tuple-element.49), channel_id=1, source_target_pairs={{0,1},{1,0},{2,3},{3,2},{4,5},{5,4},{6,7},{7,6},{8,9},{9,8},{10,11... | collective-permute-start | bytes 2555912 | tf_op jit(solution)/shard_map/ppermute | solution.py:387
  122.2 11.4 %collective-permute-start.3 = (bf16[3328,128]{1,0:T(8,128)(2,1)S(1)}, bf16[3328,128]{1,0:T(8,128)(2,1)S(1)}, u32[]{:S(2)}, u32[]{:S(2)}) collective-permute-start(bf16[3328,128]{1,0:T(8,128)(2,1)S(1)} %all_gather.3.own), channel_id=1, source_target_pairs={{0,1},{1,0},{2,3},{3,2},{4,5},{5,4},{6,7},{7,6},{8,9},{9,8},{10,11... | collective-permute-start | bytes 2555912 | tf_op jit(solution)/shard_map/ppermute | solution.py:398

commit v9 on v8

--- a/solution.py
+++ b/solution.py
@@ -72,27 +72,46 @@
         w_back[a] = jnp.concatenate(turned, axis=1).astype(BF16)
 
 
-def forward_kernel(core, ends, across, local, beside, w1, w2, hidden, slope, outlook, sent, stack):
+def taps_of(w1, b, a, n):
+    return jnp.concatenate(
+        [w1[:, (3 * k + b) * C : (3 * k + b + 1) * C] for k in range(a, a + n)], axis=1
+    )
+
+
+def own_kernel(local, w1, partial, stack):
+    upper, lower = local[:, :LON], local[:, LON:]
+    stack[:C, :] = upper
+    stack[C:, :] = lower
+    for i in range(ROWS + 2):
+        a = max(ROWS - i, 0)
+        rows = (upper, stack, stack, lower)[i]
+        total = None
+        for b in range(3):
+            part = turn(dot(taps_of(w1, b, a, (1, 2, 2, 1)[i]), rows[...]), 1 - b)
+            total = part if total is None else total + part
+        partial[:, i * LON : (i + 1) * LON] = total
+
+
+def forward_kernel(
+    core, ends, partial, across, beside, w1, w2, hidden, slope, outlook, sent, stack
+):
     wide = ROWS + 2
 
-    def fill(chosen, ref):
-        for a in range(3):
-            for i in range(wide):
-                if (i + a) // 2 == chosen:
-                    row = ref[:, (i + a) % 2 * LON : ((i + a) % 2 + 1) * LON]
-                    stack[a * C : (a + 1) * C, i * LON : (i + 1) * LON] = row
-
-    fill(1, local)
-    by_side(core, across, beside, lambda before, after: (fill(0, before), fill(2, after)))
+    def fill(before, after):
+        stack[:C, :LON] = before[:, :LON]
+        stack[C:, :LON] = before[:, LON:]
+        stack[:C, LON:] = after[:, :LON]
+        stack[C:, LON:] = after[:, LON:]
+
+    by_side(core, across, beside, fill)
     for i in range(wide):
         lanes = slice(i * LON, (i + 1) * LON)
-        pre = None
-        for b in range(3):
-            taps = jnp.concatenate(
-                [w1[:, (3 * a + b) * C : (3 * a + b + 1) * C] for a in range(3)], axis=1
-            )
-            part = turn(dot(taps, stack[:, lanes]), 1 - b)
-            pre = part if pre is None else pre + part
+        side = slice(0, LON) if i < 2 else slice(LON, 2 * LON)
+        at = (slice(0, 2 * C), slice(C, 2 * C), slice(0, C), slice(0, 2 * C))[i]
+        a, n = ((0, 2), (0, 1), (2, 1), (1, 2))[i]
+        pre = partial[:, lanes]
+        for b in range(3):
+            pre = pre + turn(dot(taps_of(w1, b, a, n), stack[at, side]), 1 - b)
         square = pre * pre
         t = jnp.tanh(GELU_A * pre * (1.0 + GELU_B * square))
         half = 0.5 * (1.0 + t)
@@ -319,6 +338,14 @@
         out_specs=(VMEM,) * 3,
         compiler_params=PARAMS,
     )(w_first, later_kernel_matrix)
+    partial = pl.pallas_call(
+        own_kernel,
+        out_shape=jax.ShapeDtypeStruct((C, 4 * LON), F32),
+        in_specs=[VMEM] * 2,
+        out_specs=VMEM,
+        scratch_shapes=[pltpu.VMEM((2 * C, LON), BF16)],
+        compiler_params=PARAMS,
+    )(local, w1)
     ends = jnp.stack([(dom > 0).astype(F32), (dom < dom_size - 1).astype(F32)])
     obs = jnp.pad(observed_state.reshape(V, CELLS), ((0, FIRST + SHARE - V), (0, 0)))
     area = land.reshape(1, CELLS)
@@ -333,8 +360,8 @@
         row %= size
         flags.append(holder.astype(jnp.int32).reshape(1))
         places.append((row, size))
-    across, obs, area, me, ends, flags = lax.optimization_barrier(
-        (across, obs, area, me, ends, flags)
+    across, obs, area, me, ends, flags, partial = lax.optimization_barrier(
+        (across, obs, area, me, ends, flags, partial)
     )
     hidden, slope, outlook, sent = pl.pallas_call(
         forward_kernel,
@@ -346,9 +373,9 @@
         ),
         in_specs=[SMEM] * 2 + [VMEM] * 5,
         out_specs=(VMEM,) * 4,
-        scratch_shapes=[pltpu.VMEM((3 * C, 4 * LON), BF16)],
-        compiler_params=PARAMS,
-    )(core, ends, across, local, beside, w1, w2)
+        scratch_shapes=[pltpu.VMEM((2 * C, 2 * LON), BF16)],
+        compiler_params=PARAMS,
+    )(core, ends, partial, across, beside, w1, w2)
 
     every = exchange(sent, ("yh", "x"))
     errors, loss = pl.pallas_call(

time: 136 us -> 135 us (level)
  blocking collectives: 95.4 us -> 93.9 us
    all_to_all x6, blocking collectives: 83.6 us -> 82.1 us  [exchange(): return lax.all_to_all(array, axes, 0, 0, tiled=True)]
  transfers between devices with their start and end apart: 4 -> 4, of which waited for: 2 -> 2; matrix products, arithmetic and copies ran while one was open for 2% -> 2% of each run, Pallas kernels for 1% -> 2%
where the time goes in v9:
time: 135 us
  blocking collectives  93.9 us (70%)
  starting transfers between devices  23.6 us (17%)
  Pallas kernels  10.9 us (8%)
  local copies, waits for them, and re-layouts  3.64 us (3%)
  waiting for transfers between devices  1.61 us (1%)
    all_to_all x6, blocking collectives, exchange(): return lax.all_to_all(array, axes, 0, 0, tiled=True)  82.1 us
    all_gather x1, blocking collectives, body(): part = lax.all_gather(part, 'x', axis=0, tiled=True)  11.8 us
    ppermute x1, starting transfers between devices, body(): other = lax.ppermute(part, 'c', swap)  9.43 us
    ppermute x1, starting transfers between devices, body(): beside = lax.ppermute(local, DOM, cores)  4.87 us
    ppermute x1, starting transfers between devices, body(): theirs = lax.ppermute(theirs, 'c', swap)  4.72 us
    ppermute x1, starting transfers between devices, body(): across = lax.ppermute(local, DOM, chips)  4.59 us
    unnamed x8, local copies, waits for them, and re-layouts  2.82 us
    pallas_call x1, Pallas kernels, body(): pl.pallas_call(backward_kernel, out_shape=(jax.ShapeDtypeStruct((HALF, LA...  2.8 us
  transfers between devices with their start and end apart: 4, of which 2 were waited for; matrix products, arithmetic and copies ran while one was open for 2% of the time, Pallas kernels for 2%

profile of v9, /device:TPU:1, one launch (start us, length us, event | category | flops | bytes accessed | tf_op | source)
XLA Modules:
  0.0 134.6 jit_solution(13232322233884448079)
XLA Ops:
  0.6 0.0 copy-start.1
  0.6 0.0 copy-start
  0.7 1.1 copy.9
  1.8 4.6 %collective-permute-start = (bf16[256,512]{1,0:T(8,128)(2,1)S(1)}, bf16[256,512]{1,0:T(8,128)(2,1)S(1)}, u32[]{:S(2)}, u32[]{:S(2)}) collective-permute-start(bf16[256,512]{1,0:T(8,128)(2,1)S(1)} %bitcast.24), channel_id=1, source_target_pairs={{1,2},{3,4},{5,6},{7,8},{9,10},{11,12},{13,14},{15,16},{17,18},{19... | collective-permute-start | bytes 786440 | tf_op jit(solution)/shard_map/ppermute | solution.py:328
  6.4 4.9 %collective-permute-start.1 = (bf16[256,512]{1,0:T(8,128)(2,1)S(1)}, bf16[256,512]{1,0:T(8,128)(2,1)S(1)}, u32[]{:S(2)}, u32[]{:S(2)}) collective-permute-start(bf16[256,512]{1,0:T(8,128)(2,1)S(1)} %bitcast.25), channel_id=1, source_target_pairs={{0,1},{1,0},{2,3},{3,2},{4,5},{5,4},{6,7},{7,6},{8,9},{9,8},{10,11... | collective-permute-start | bytes 786440 | tf_op jit(solution)/shard_map/ppermute | solution.py:329
  11.3 0.7 copy.11
  12.0 1.0 pad.7
  13.0 0.0 copy-done.1
  13.0 0.0 copy-done
  13.0 0.4 shard_map.84
  13.5 0.9 shard_map.85.partial
  14.4 0.1 add_convert_fusion.ends
  14.5 0.0 collective-permute-done.across
  14.5 0.0 collective-permute-done.1.beside
  14.5 2.4 %shard_map.86 = (bf16[256,1024]{1,0:T(8,128)(2,1)S(1)}, f32[256,1024]{1,0:T(8,128)S(1)}, f32[100,512]{1,0:T(8,128)S(1)}, bf16[8,56,128]{2,1,0:T(8,128)(2,1)S(1)}) custom-call(s32[1]{0:T(128)} %bitcast.6.core, f32[2]{0:T(128)S(1)} %add_convert_fusion.ends, f32[256,1024]{1,0:T(8,128)S(1)} %shard_map.85.partial, ...), custom_call_target="tpu_custom_call" | custom-call | tf_op jit(solution)/shard_map/pallas_call | solution.py:366
  16.9 14.6 %all_to_all.30.refs_1_ = bf16[8,56,128]{2,1,0:T(8,128)(2,1)S(1)} all-to-all(bf16[8,56,128]{2,1,0:T(8,128)(2,1)S(1)} %get-tuple-element.40), channel_id=1, replica_groups=mesh['x'=4,'yh'=2,'zh'=2,'zl'=4,'yl'=4,'c'=2] {'yh','x'}, dimensions={0} | all-to-all | bytes 229376 | tf_op jit(solution)/shard_map/all_to_all | solution.py:314
  31.5 1.0 shard_map.87
  32.5 11.7 %all_to_all.31.err = bf16[8,56,128]{2,1,0:T(8,128)(2,1)S(1)} all-to-all(bf16[8,56,128]{2,1,0:T(8,128)(2,1)S(1)} %get-tuple-element.45), channel_id=1, replica_groups=mesh['x'=4,'yh'=2,'zh'=2,'zl'=4,'yl'=4,'c'=2] {'yh','x'}, dimensions={0} | all-to-all | bytes 229376 | tf_op jit(solution)/shard_map/all_to_all | solution.py:314
  44.2 2.8 %shard_map.88 = (bf16[3328,128]{1,0:T(8,128)(2,1)S(1)}, bf16[336,512]{1,0:T(8,128)(2,1)S(1)}, bf16[768,1024]{1,0:T(8,128)(2,1)S(1)}, bf16[256,1536]{1,0:T(8,128)(2,1)S(1)}) custom-call(s32[1]{0:T(128)} %bitcast.6.core, f32[1,1]{1,0:T(1,128)} %get-tuple-element.43.loss, bf16[8,56,128]{2,1,0:T(8,128)(2,1)S(1)} %all_to_all.31.err, ...), custom_call_target="tpu_custom_call" | custom-call | tf_op jit(solution)/shard_map/pallas_call | solution.py:393
  47.0 4.7 %collective-permute-start.2 = (bf16[3328,128]{1,0:T(8,128)(2,1)S(1)}, bf16[3328,128]{1,0:T(8,128)(2,1)S(1)}, u32[]{:S(2)}, u32[]{:S(2)}) collective-permute-start(bf16[3328,128]{1,0:T(8,128)(2,1)S(1)} %get-tuple-element.51), channel_id=1, source_target_pairs={{0,1},{1,0},{2,3},{3,2},{4,5},{5,4},{6,7},{7,6},{8,9},{9,8},{10,11... | collective-permute-start | bytes 2555912 | tf_op jit(solution)/shard_map/ppermute | solution.py:414
  51.7 1.5 %shard_map.89 = bf16[3328,128]{1,0:T(8,128)(2,1)S(1)} custom-call(s32[1]{0:T(128)} %bitcast.6.core, f32[1,1]{1,0:T(1,128)} %get-tuple-element.43.loss, bf16[256,1024]{1,0:T(8,128)(2,1)S(1)} %get-tuple-element.44.hidden, bf16[336,512]{1,0:T(8,128)(2,1)S(1)} %get-tuple-element.48.e, bf16[768,1024]{1,0:T(8,128)(2,1)S(1)} %get-tuple-element.49.pg, ...), custom_call_target="tpu_custom_call" | custom-call | tf_op jit(solution)/shard_map/pallas_call | solution.py:405
  53.3 0.4 collective-permute-done.2
  53.7 0.2 shard_map.90
  53.9 14.8 %all_to_all.32.refs_1_ = bf16[4,832,128]{2,1,0:T(8,128)(2,1)S(1)} all-to-all(bf16[4,832,128]{2,1,0:T(8,128)(2,1)S(1)} %bitcast.23), channel_id=1, replica_groups=mesh['x'=4,'yh'=2,'zh'=2,'zl'=4,'yl'=4,'c'=2] {'x'}, dimensions={0} | all-to-all | bytes 1703936 | tf_op jit(solution)/shard_map/all_to_all | solution.py:314
  68.7 0.1 shard_map.91
  68.8 13.7 %all_to_all.33.refs_1_ = bf16[8,104,128]{2,1,0:T(8,128)(2,1)S(1)} all-to-all(bf16[8,104,128]{2,1,0:T(8,128)(2,1)S(1)} %bitcast.29), channel_id=1, replica_groups=mesh['x'=4,'yh'=2,'zh'=2,'zl'=4,'yl'=4,'c'=2] {'yl','yh'}, dimensions={0} | all-to-all | bytes 425984 | tf_op jit(solution)/shard_map/all_to_all | solution.py:314
  82.6 16.2 %all_to_all.34.refs_1_ = bf16[8,104,128]{2,1,0:T(8,128)(2,1)S(1)} all-to-all(bf16[8,104,128]{2,1,0:T(8,128)(2,1)S(1)} %shard_map.92), channel_id=1, replica_groups=mesh['x'=4,'yh'=2,'zh'=2,'zl'=4,'yl'=4,'c'=2] {'zl','zh'}, dimensions={0} | all-to-all | bytes 425984 | tf_op jit(solution)/shard_map/all_to_all | solution.py:314
  98.9 11.0 %all_to_all.35 = bf16[8,104,128]{2,1,0:T(8,128)(2,1)S(1)} all-to-all(bf16[8,104,128]{2,1,0:T(8,128)(2,1)S(1)} %shard_map.93), channel_id=1, replica_groups=mesh['x'=4,'yh'=2,'zh'=2,'zl'=4,'yl'=4,'c'=2] {'yl','yh'}, dimensions={0} | all-to-all | bytes 425984 | tf_op jit(solution)/shard_map/all_to_all | solution.py:314
  109.9 11.8 %all_gather.3.own = bf16[3328,128]{1,0:T(8,128)(2,1)S(1)} all-gather(bf16[832,128]{1,0:T(8,128)(2,1)S(1)} %bitcast.33), channel_id=1, replica_groups=mesh['x'=4,'yh'=2,'zh'=2,'zl'=4,'yl'=4,'c'=2] {'x'}, dimensions={0}, use_global_device_ids=true | all-gather | bytes 1064960 | tf_op jit(solution)/shard_map/all_gather | solution.py:424
  121.7 9.4 %collective-permute-start.3 = (bf16[3328,128]{1,0:T(8,128)(2,1)S(1)}, bf16[3328,128]{1,0:T(8,128)(2,1)S(1)}, u32[]{:S(2)}, u32[]{:S(2)}) collective-permute-start(bf16[3328,128]{1,0:T(8,128)(2,1)S(1)} %all_gather.3.own), channel_id=1, source_target_pairs={{0,1},{1,0},{2,3},{3,2},{4,5},{5,4},{6,7},{7,6},{8,9},{9,8},{10,11... | collective-permute-start | bytes 2555912 | tf_op jit(solution)/shard_map/ppermute | solution.py:425
  131.2 0.8 reshape.70
  132.0 1.2 collective-permute-done.3.other
  133.2 1.5 %shard_map.94 = (bf16[256,2304]{1,0:T(8,128)(2,1)}, bf16[100,2304]{1,0:T(8,128)(2,1)}, f32[1,1]{1,0:T(1,128)}) custom-call(s32[1]{0:T(128)} %bitcast.6.core, bf16[3328,128]{1,0:T(8,128)(2,1)S(1)} %all_gather.3.own, bf16[3328,128]{1,0:T(8,128)(2,1)S(1)} %collective-permute-done.3.other), custom_call_target="tpu_custom_call" | custom-call | tf_op jit(solution)/shard_map/pallas_call | solution.py:427
  (4 shorter events, 0.1 us)
Async XLA Ops:
  0.6 12.4 %copy-start.1 = (bf16[100,2304]{1,0:T(8,128)(2,1)S(1)}, bf16[100,2304]{1,0:T(8,128)(2,1)}, u32[]{:S(2)}) copy-start(bf16[100,2304]{1,0:T(8,128)(2,1)} %w2.1) | copy-start | bytes 1382404
  0.6 12.4 %copy-start = (bf16[256,2304]{1,0:T(8,128)(2,1)S(1)}, bf16[256,2304]{1,0:T(8,128)(2,1)}, u32[]{:S(2)}) copy-start(bf16[256,2304]{1,0:T(8,128)(2,1)} %w1.1) | copy-start | bytes 3538948
  1.8 12.7 %collective-permute-start = (bf16[256,512]{1,0:T(8,128)(2,1)S(1)}, bf16[256,512]{1,0:T(8,128)(2,1)S(1)}, u32[]{:S(2)}, u32[]{:S(2)}) collective-permute-start(bf16[256,512]{1,0:T(8,128)(2,1)S(1)} %bitcast.24), channel_id=1, source_target_pairs={{1,2},{3,4},{5,6},{7,8},{9,10},{11,12},{13,14},{15,16},{17,18},{19... | collective-permute-start | bytes 786440 | tf_op jit(solution)/shard_map/ppermute | solution.py:328
  6.4 8.1 %collective-permute-start.1 = (bf16[256,512]{1,0:T(8,128)(2,1)S(1)}, bf16[256,512]{1,0:T(8,128)(2,1)S(1)}, u32[]{:S(2)}, u32[]{:S(2)}) collective-permute-start(bf16[256,512]{1,0:T(8,128)(2,1)S(1)} %bitcast.25), channel_id=1, source_target_pairs={{0,1},{1,0},{2,3},{3,2},{4,5},{5,4},{6,7},{7,6},{8,9},{9,8},{10,11... | collective-permute-start | bytes 786440 | tf_op jit(solution)/shard_map/ppermute | solution.py:329
  47.0 6.7 %collective-permute-start.2 = (bf16[3328,128]{1,0:T(8,128)(2,1)S(1)}, bf16[3328,128]{1,0:T(8,128)(2,1)S(1)}, u32[]{:S(2)}, u32[]{:S(2)}) collective-permute-start(bf16[3328,128]{1,0:T(8,128)(2,1)S(1)} %get-tuple-element.51), channel_id=1, source_target_pairs={{0,1},{1,0},{2,3},{3,2},{4,5},{5,4},{6,7},{7,6},{8,9},{9,8},{10,11... | collective-permute-start | bytes 2555912 | tf_op jit(solution)/shard_map/ppermute | solution.py:414
  121.7 11.4 %collective-permute-start.3 = (bf16[3328,128]{1,0:T(8,128)(2,1)S(1)}, bf16[3328,128]{1,0:T(8,128)(2,1)S(1)}, u32[]{:S(2)}, u32[]{:S(2)}) collective-permute-start(bf16[3328,128]{1,0:T(8,128)(2,1)S(1)} %all_gather.3.own), channel_id=1, source_target_pairs={{0,1},{1,0},{2,3},{3,2},{4,5},{5,4},{6,7},{7,6},{8,9},{9,8},{10,11... | collective-permute-start | bytes 2555912 | tf_op jit(solution)/shard_map/ppermute | solution.py:425
